TPU v7x, 128 devices: a whole 4x4x4 slice. The times are simulated.
128 devices in a mesh: sect: 8 (over x, core), cell: 16 (over y, z).
Axes of the slice: x: 4, y: 4, z: 4, core: 2. Of those that a mesh axis runs over, the one named last changes fastest.
Arguments:
- atm_fields: bfloat16 [24, 524288], P(None, ('sect', 'cell')), may hold values from -6 to 6
- ocn_state: float32 [8, 1048576], P(None, ('sect', 'cell')), may hold values from -6 to 6
- ice_state: float32 [8, 1048576], P(None, ('sect', 'cell')), may hold values from -6 to 6
- ice_level: int32 [1048576], P(('sect', 'cell')), may hold values from 0 to 8
- lnd_state: float32 [8, 262144], P(None, ('sect', 'cell')), may hold values from -6 to 6
- lnd_level: int32 [262144], P(('sect', 'cell')), may hold values from 1 to 8
- ocn_map: int32 [8192, 2], P(('sect', 'cell')), may hold values from 0 to 4095, as said below
- ocn_local: int32 [8192, 2], P(('sect', 'cell')), may hold values from 0 to 31
- ocn_tiles: bfloat16 [8192, 4, 128, 128], P(('sect', 'cell')), may hold values from -0.25 to 0.25
- lnd_map: int32 [2048, 2], P(('sect', 'cell')), may hold values from 0 to 4095, as said below
- lnd_local: int32 [2048, 2], P(('sect', 'cell')), may hold values from 0 to 31
- lnd_tiles: bfloat16 [2048, 4, 128, 128], P(('sect', 'cell')), may hold values from -0.25 to 0.25
Outputs:
- atm_flux: float32 [8, 524288], P(None, ('sect', 'cell'))
- ocn_flux: float32 [8, 1048576], P(None, ('sect', 'cell'))
- lnd_flux: float32 [8, 262144], P(None, ('sect', 'cell'))
Inputs may be any that keep to these rules, and one draw needn't show every extreme that they name: Global atmosphere block indices; the device of block b is b // 32, and devices are numbered sect-major. For the ocn_map rows of one device q's 64 ocean blocks taken together with the lnd_map rows of its 16 land blocks, every named device is (q + t) modulo the device count for some t from -8 to 7; at most 15 of these entries name any one device, and exactly 15 name some device. `lnd_map`: global atmosphere block indices, counted together with ocn_map as stated there.
All inputs are finite; a program needn't handle non-finite values.
Results may differ from a plain program's by a relative error of at most 0.0022.
Values may be sent and summed in bfloat16 or wider, within the bound.
No kernel may reach another device: no remote copies, remote signals or barrier semaphores. Data moves between devices by JAX's collectives and lax.ppermute only.
A program may use at most 64 MiB of HBM per device.

v0:
```python
import jax
import jax.numpy as jnp
from jax import lax
from jax.sharding import PartitionSpec as P

ocean_coef = (1.2, 0.9, 1.5, 0.7, 1.1, 1.3, 0.8, 1.0)
ice_coef = (0.5, 1.4, 0.6, 1.2, 0.9, 0.4, 1.6, 0.7)
land_coef = (0.8, 1.1, 0.6, 1.5, 0.7, 1.2, 1.0, 0.5)


def padded(x, sides, width):
    for axis, dim in sides:
        size, length = (lax.axis_size(axis), x.shape[dim])
        up = [(i, (i + 1) % size) for i in range(size)]
        down = [(j, i) for i, j in up]
        last = lax.slice_in_dim(x, length - width, length, axis=dim)
        initial = lax.slice_in_dim(x, 0, width, axis=dim)
        before = lax.ppermute(last, axis, up)
        after = lax.ppermute(initial, axis, down)
        x = jnp.concatenate([before, x, after], axis=dim)
    return x


def bulk_flux(remapped, surface, factors):
    wind_speed = jnp.sqrt(
        1.0 + remapped[:, 0::3] * remapped[:, 0::3] + remapped[:, 1::3] * remapped[:, 1::3]
    )
    weights = jnp.asarray(factors, jnp.float32)[None, :, None]
    return weights * wind_speed * (remapped[:, 2::3] - surface)


def pair_ranks(owner_dev):
    position = jnp.arange(owner_dev.shape[-1])
    earlier = position[None, :] < position[:, None]
    same_owner = (owner_dev[..., :, None] == owner_dev[..., None, :]) & earlier
    return jnp.sum(same_owner.astype(jnp.int32), axis=-1)


def as_blocks(array, count, block_len):
    return array.reshape(array.shape[0], count, block_len).transpose(1, 0, 2)


def per_device(
    atm_fields,
    ocn_state,
    ice_state,
    ice_level,
    lnd_state,
    lnd_level,
    ocn_map,
    ocn_local,
    ocn_tiles,
    lnd_map,
    lnd_local,
    lnd_tiles,
):
    field_count, width_all = atm_fields.shape
    block_len = ocn_tiles.shape[2]
    flux_count = ocn_state.shape[0]
    blocks_here = width_all // block_len
    ocean_blocks = ocn_map.shape[0]
    land_blocks = lnd_map.shape[0]
    remote_count = ocn_map.shape[1]
    cell_count = lax.axis_size("cell")
    my_index = lax.axis_index(("sect", "cell"))
    my_cell = my_index % cell_count
    source = jnp.concatenate([ocn_map.reshape(-1), lnd_map.reshape(-1)])
    pair_count = source.shape[0]
    base_share = (pair_count + cell_count - 1) // cell_count
    capacity = base_share + (base_share + 1) // 2
    owner_dev = source // blocks_here
    pair_rank = pair_ranks(owner_dev)
    row_maps = lax.all_gather(source, "cell", axis=0, tiled=True).reshape(1, cell_count, pair_count)
    near_maps = padded(row_maps, (("sect", 0),), 1)
    near_owner = near_maps // blocks_here
    near_rank = pair_ranks(near_owner)
    match_mask = (near_owner == my_index)[..., None] & (
        near_rank[..., None] == jnp.arange(capacity)[None, None, None, :]
    )
    wanted = jnp.sum(jnp.where(match_mask, (near_maps % blocks_here)[..., None] + 1, 0), axis=2) - 1
    atm_rows = atm_fields.reshape(field_count, blocks_here, block_len).transpose(1, 0, 2)
    flat_rows = atm_rows.reshape(blocks_here, field_count * block_len)
    row_width = field_count * block_len
    term_width = flux_count * block_len
    three_picker = wanted.reshape(-1)[:, None] == jnp.arange(blocks_here)[None, :]
    outgoing = jnp.dot(
        three_picker.astype(jnp.bfloat16), flat_rows, preferred_element_type=jnp.float32
    ).astype(jnp.bfloat16)
    rimmed = padded(outgoing.reshape(3, cell_count * capacity, row_width), (("sect", 0),), 1)
    relayed = rimmed[0] + rimmed[2] + rimmed[4]
    incoming = lax.all_to_all(relayed, "cell", split_axis=0, concat_axis=0, tiled=True)
    wanted_rows = jnp.max(wanted, axis=0).reshape(-1)
    picker = wanted_rows[:, None] == jnp.arange(blocks_here)[None, :]
    slot_of = owner_dev % cell_count * capacity + pair_rank
    slot_count = cell_count * capacity
    pair_data = jnp.take(incoming, slot_of, axis=0)
    ocean_pairs = ocean_blocks * remote_count
    ocean_remote = pair_data[:ocean_pairs].reshape(
        ocean_blocks, remote_count, field_count, block_len
    )
    land_remote = pair_data[ocean_pairs:].reshape(land_blocks, remote_count, field_count, block_len)
    ocean_sources = jnp.concatenate([ocean_remote, jnp.take(atm_rows, ocn_local, axis=0)], axis=1)
    land_sources = jnp.concatenate([land_remote, jnp.take(atm_rows, lnd_local, axis=0)], axis=1)
    ocean_mixed = jnp.einsum(
        "bkfs,bksd->bfd", ocean_sources, ocn_tiles, preferred_element_type=jnp.float32
    )
    land_mixed = jnp.einsum(
        "bkfs,bksd->bfd", land_sources, lnd_tiles, preferred_element_type=jnp.float32
    )
    ice_frac = (ice_level.astype(jnp.float32) / 8.0).reshape(ocean_blocks, 1, block_len)
    ocean_flux = (1.0 - ice_frac) * bulk_flux(
        ocean_mixed, as_blocks(ocn_state, ocean_blocks, block_len), ocean_coef
    )
    ocean_flux = ocean_flux + ice_frac * bulk_flux(
        ocean_mixed, as_blocks(ice_state, ocean_blocks, block_len), ice_coef
    )
    land_frac = (lnd_level.astype(jnp.float32) / 8.0).reshape(land_blocks, 1, block_len)
    land_flux = land_frac * bulk_flux(
        land_mixed, as_blocks(lnd_state, land_blocks, block_len), land_coef
    )
    ocean_terms = jnp.einsum(
        "bfd,bksd->bkfs",
        ocean_flux.astype(jnp.bfloat16),
        ocn_tiles,
        preferred_element_type=jnp.float32,
    )
    land_terms = jnp.einsum(
        "bfd,bksd->bkfs",
        land_flux.astype(jnp.bfloat16),
        lnd_tiles,
        preferred_element_type=jnp.float32,
    )
    remote_terms = jnp.concatenate(
        [
            ocean_terms[:, :remote_count].reshape(-1, term_width),
            land_terms[:, :remote_count].reshape(-1, term_width),
        ],
        axis=0,
    )
    local_terms = jnp.concatenate(
        [
            ocean_terms[:, remote_count:].reshape(-1, term_width),
            land_terms[:, remote_count:].reshape(-1, term_width),
        ],
        axis=0,
    )
    local_targets = jnp.concatenate([ocn_local.reshape(-1), lnd_local.reshape(-1)])
    back_out = jnp.zeros((slot_count, term_width), jnp.float32).at[slot_of].set(remote_terms)
    crossed = lax.all_to_all(back_out, "cell", split_axis=0, concat_axis=0, tiled=True).reshape(
        cell_count, capacity, term_width
    )
    sect_step = (
        jnp.arange(cell_count, dtype=jnp.int32) - my_cell + cell_count // 2 - 1
    ) // cell_count
    stacked = jnp.stack(
        [jnp.where((sect_step == step - 1)[:, None, None], crossed, 0.0) for step in range(3)]
    ).reshape(3, cell_count * capacity, term_width)
    rimmed_back = padded(stacked, (("sect", 0),), 1)
    back_in = rimmed_back[0] + rimmed_back[2] + rimmed_back[4]
    local_picker = (local_targets[None, :] == jnp.arange(blocks_here)[:, None]).astype(jnp.float32)
    summed = jnp.dot(local_picker, local_terms, precision=lax.Precision.HIGHEST)
    summed = summed + jnp.dot(
        picker.astype(jnp.float32).T, back_in, precision=lax.Precision.HIGHEST
    )
    atm_flux = (
        summed.reshape(blocks_here, flux_count, block_len)
        .transpose(1, 0, 2)
        .reshape(flux_count, width_all)
    )
    ocn_flux = ocean_flux.transpose(1, 0, 2).reshape(flux_count, ocean_blocks * block_len)
    lnd_flux = land_flux.transpose(1, 0, 2).reshape(flux_count, land_blocks * block_len)
    return (atm_flux, ocn_flux, lnd_flux)


def solution(mesh):
    in_specs = (
        P(None, ("sect", "cell")),
        P(None, ("sect", "cell")),
        P(None, ("sect", "cell")),
        P(("sect", "cell")),
        P(None, ("sect", "cell")),
        P(("sect", "cell")),
        P(("sect", "cell"), None),
        P(("sect", "cell"), None),
        P(("sect", "cell"), None, None, None),
        P(("sect", "cell"), None),
        P(("sect", "cell"), None),
        P(("sect", "cell"), None, None, None),
    )
    out_specs = (P(None, ("sect", "cell")), P(None, ("sect", "cell")), P(None, ("sect", "cell")))
    return jax.shard_map(
        per_device, mesh=mesh, in_specs=in_specs, out_specs=out_specs, check_vma=False
    )
```

profile of v0, /device:TPU:5, one launch (start us, length us, event | category | flops | bytes accessed | tf_op | source)
XLA Modules:
  0.0 233.7 jit_solution(8977313917243157317)
XLA Ops:
  0.7 0.9 copy.63
  1.6 0.1 concatenate.126
  1.7 0.8 copy.64
  2.6 1.2 dynamic-slice
  4.5 0.3 dynamic-update-slice
  4.8 61.8 %all-reduce = s32[2560]{0:T(1024)S(1)} all-reduce(s32[2560]{0:T(1024)S(1)} %dynamic-update-slice), channel_id=1, replica_groups=mesh['sect'=8,'cell'=16] {'cell'}, use_global_device_ids=true, to_apply=%add | all-reduce | flops 2560 | bytes 20480
  66.6 15.6 %collective-permute-start = (s32[1,16,160]{2,1,0:T(8,128)S(1)}, s32[1,16,160]{2,1,0:T(8,128)S(1)}, u32[]{:S(2)}, u32[]{:S(2)}) collective-permute-start(s32[1,16,160]{2,1,0:T(8,128)S(1)} %reshape.781), channel_id=1, source_target_pairs={{0,16},{16,32},{32,48},{48,64},{64,80},{80,96},{96,112},{112,0},{1... | collective-permute-start | bytes 30728 | tf_op jit(solution)/shard_map/ppermute | solution.py:18
  82.2 1.0 copy_bitcast_fusion.2
  83.2 0.7 compare_select_fusion.4
  84.0 1.4 collective-permute-done.1
  85.5 3.5 %convert_reduce_fusion = s32[3,16,160]{2,1,0:T(8,128)S(1)} fusion(s32[3,16,160]{2,1,0:T(8,128)S(1)} %get-tuple-element.4, pred[160,160]{1,0:T(8,128)(4,1)S(1)} %iota_compare_fusion.3), kind=kLoop, calls=%fused_computation.4 | loop fusion | flops 4907520 | bytes 87040 | tf_op jit(solution)/shard_map/reduce_sum | solution.py:36
  89.0 0.9 select_reduce_fusion
  90.1 1.4 convolution_convert_fusion
  91.4 2.1 fusion.51
  93.6 0.3 collective-permute-start.2
  93.9 0.2 collective-permute-start.3
  94.1 0.1 concatenate.130
  94.4 0.1 reshape.807
  94.7 0.1 copy.69
  94.9 0.8 gather_fusion.1
  95.6 0.6 gather_fusion.2
  96.4 0.2 convert_reduce_fusion.1
  96.6 2.5 %squeeze.19 = bf16[16,15,3072]{2,1,0:T(8,128)(2,1)} reshape(bf16[240,3072]{1,0:T(8,128)(2,1)} %get-tuple-element.5) | data formatting | bytes 2949120 | tf_op jit(solution)/shard_map/squeeze | solution.py:90
  99.1 11.4 %collective-permute-done.2 = bf16[1,240,3072]{2,1,0:T(8,128)(2,1)} collective-permute-done((bf16[1,240,3072]{2,1,0:T(8,128)(2,1)}, bf16[1,240,3072]{2,1,0:T(8,128)(2,1)}, u32[]{:S(2)}, u32[]{:S(2)}) %collective-permute-start.2) | collective-permute-done | bytes 1474592 | tf_op jit(solution)/shard_map/ppermute | solution.py:18
  110.5 2.5 %squeeze.18 = bf16[16,15,3072]{2,1,0:T(8,128)(2,1)} reshape(bf16[1,240,3072]{2,1,0:T(8,128)(2,1)} %collective-permute-done.2) | data formatting | bytes 2949120 | tf_op jit(solution)/shard_map/squeeze | solution.py:90
  113.0 2.5 %squeeze.20 = bf16[16,15,3072]{2,1,0:T(8,128)(2,1)} reshape(bf16[1,240,3072]{2,1,0:T(8,128)(2,1)} %collective-permute-done.3) | data formatting | bytes 2949120 | tf_op jit(solution)/shard_map/squeeze | solution.py:90
  115.5 3.7 %add_add_fusion = bf16[16,15,3072]{2,1,0:T(8,128)(2,1)} fusion(bf16[16,15,3072]{2,1,0:T(8,128)(2,1)} %squeeze.20, bf16[16,15,3072]{2,1,0:T(8,128)(2,1)} %squeeze.18, bf16[16,15,3072]{2,1,0:T(8,128)(2,1)} %squeeze.19), kind=kLoop, calls=%fused_computation.10 | loop fusion | flops 1474560 | bytes 5898240 | tf_op jit(solution)/shard_map/add | solution.py:90
  119.3 4.7 %all-to-all-start = ((bf16[16,15,3072]{2,1,0:T(8,128)(2,1)}), bf16[16,15,3072]{2,1,0:T(8,128)(2,1)}, u32[]{:S(2)}, u32[]{:S(2)}) async-start(bf16[16,15,3072]{2,1,0:T(8,128)(2,1)} %add_add_fusion), calls=%async_computation | async-start | bytes 3145728 | tf_op jit(solution)/shard_map/all_to_all | solution.py:91
  124.0 0.5 compare_and_fusion.2
  124.5 0.6 multiply_bitcast_fusion.1
  125.3 1.1 broadcast_select_fusion.1
  126.4 18.1 %all-to-all-done = bf16[16,15,3072]{2,1,0:T(8,128)(2,1)} async-done(((bf16[16,15,3072]{2,1,0:T(8,128)(2,1)}), bf16[16,15,3072]{2,1,0:T(8,128)(2,1)}, u32[]{:S(2)}, u32[]{:S(2)}) %all-to-all-start) | async-done | bytes 1474592 | tf_op jit(solution)/shard_map/all_to_all | solution.py:91
  144.5 2.5 %all_to_all.13 = bf16[240,3072]{1,0:T(8,128)(2,1)} reshape(bf16[16,15,3072]{2,1,0:T(8,128)(2,1)} %all-to-all-done) | data formatting | bytes 2949120 | tf_op jit(solution)/shard_map/all_to_all | solution.py:91
  146.9 4.7 %gather_fusion = bf16[160,3072]{1,0:T(8,128)(2,1)} fusion(bf16[240,3072]{1,0:T(8,128)(2,1)} %all_to_all.13, s32[1024]{0:T(1024)S(1)} %pad_clamp_fusion.2), kind=kCustom, calls=%fused_computation | custom fusion | bytes 1966720 | tf_op jit(solution)/shard_map/jit(_take)/gather | solution.py:96
  151.7 1.4 broadcast_select_fusion
  153.1 0.2 copy.81
  153.3 0.9 copy-done.2
  154.2 5.6 %fusion.4 = f32[64,24,128]{2,1,0:T(8,128)} fusion(bf16[64,4,128,128]{3,2,1,0:T(8,128)(2,1)} %param.23, bf16[64,2,24,128]{3,2,1,0:T(8,128)(2,1)S(1)} %copy-done.2, bf16[64,2,24,128]{3,2,1,0:T(8,128)(2,1)S(1)} %bitcast.130), kind=kOutput, calls=%fused_computation.14 | convolution fusion | flops 202113024 | bytes 10747904 | tf_op jit(solution)/shard_map/bkfs,bksd->bfd/dot_general | solution.py:104
  159.8 2.6 %slice.77 = f32[64,8,128]{2,1,0:T(8,128)} slice(f32[64,24,128]{2,1,0:T(8,128)} %fusion.4), slice={[0:64:1], [0:24:3], [0:128:1]} | slice | bytes 524288 | tf_op jit(solution)/shard_map/slice | solution.py:26
  162.3 2.6 %slice.78 = f32[64,8,128]{2,1,0:T(8,128)} slice(f32[64,24,128]{2,1,0:T(8,128)} %fusion.4), slice={[0:64:1], [1:24:3], [0:128:1]} | slice | bytes 524288 | tf_op jit(solution)/shard_map/slice | solution.py:26
  164.9 2.6 %slice.79 = f32[64,8,128]{2,1,0:T(8,128)} slice(f32[64,24,128]{2,1,0:T(8,128)} %fusion.4), slice={[0:64:1], [2:24:3], [0:128:1]} | slice | bytes 524288 | tf_op jit(solution)/shard_map/slice | solution.py:29
  167.6 0.4 convolution_bitcast_fusion.2
  168.2 0.3 copy-done.4
  168.6 1.2 fusion.23
  169.9 5.7 %convolution_bitcast_fusion = f32[64,4,8,128]{3,2,1,0:T(8,128)S(1)} fusion(bf16[64,4,128,128]{3,2,1,0:T(8,128)(2,1)} %param.23, f32[64,8,128]{2,1,0:T(8,128)S(1)} %fusion.23), kind=kOutput, calls=%fused_computation.13 | convolution fusion | flops 67174400 | bytes 9699328 | tf_op jit(solution)/shard_map/bfd,bksd->bkfs/dot_general | solution.py:121
  175.6 0.9 fusion.52
  176.5 0.9 copy.99
  177.5 0.6 convolution_bitcast_fusion.1
  178.2 1.9 scatter_custom_fusion
  180.2 1.1 all_to_all.14
  181.3 4.2 %all-to-all-start.1 = ((f32[16,15,1024]{2,1,0:T(8,128)}), f32[16,15,1024]{2,1,0:T(8,128)S(1)}, u32[]{:S(2)}, u32[]{:S(2)}) async-start(f32[16,15,1024]{2,1,0:T(8,128)} %all_to_all.14), calls=%async_computation.1 | async-start | bytes 2097152 | tf_op jit(solution)/shard_map/all_to_all | solution.py:149
  185.6 11.7 %all-to-all-done.1 = f32[16,15,1024]{2,1,0:T(8,128)S(1)} async-done(((f32[16,15,1024]{2,1,0:T(8,128)}), f32[16,15,1024]{2,1,0:T(8,128)S(1)}, u32[]{:S(2)}, u32[]{:S(2)}) %all-to-all-start.1) | async-done | bytes 983072 | tf_op jit(solution)/shard_map/all_to_all | solution.py:149
  197.2 1.8 broadcast_select_fusion.4
  199.0 2.3 slice.88
  201.4 13.0 %collective-permute-start.4 = (f32[1,240,1024]{2,1,0:T(8,128)}, f32[1,240,1024]{2,1,0:T(8,128)}, u32[]{:S(2)}, u32[]{:S(2)}) collective-permute-start(f32[1,240,1024]{2,1,0:T(8,128)} %slice.88), channel_id=1, source_target_pairs={{0,16},{16,32},{32,48},{48,64},{64,80},{80,96},{96,112},{112,0},{1... | collective-permute-start | bytes 2949128 | tf_op jit(solution)/shard_map/ppermute | solution.py:18
  214.4 2.4 %slice.89 = f32[1,240,1024]{2,1,0:T(8,128)} reshape(f32[16,15,1024]{2,1,0:T(8,128)} %get-tuple-element.9) | data formatting | bytes 1966080 | tf_op jit(solution)/shard_map/slice | solution.py:17
  217.0 0.1 reshape.778
  217.4 1.1 copy.100
  218.6 0.3 fusion.9
  218.9 1.1 squeeze.22
  220.0 5.7 %collective-permute-done.4 = f32[1,240,1024]{2,1,0:T(8,128)} collective-permute-done((f32[1,240,1024]{2,1,0:T(8,128)}, f32[1,240,1024]{2,1,0:T(8,128)}, u32[]{:S(2)}, u32[]{:S(2)}) %collective-permute-start.4) | collective-permute-done | bytes 983072 | tf_op jit(solution)/shard_map/ppermute | solution.py:18
  225.8 4.9 %collective-permute-done.5 = f32[1,240,1024]{2,1,0:T(8,128)} collective-permute-done((f32[1,240,1024]{2,1,0:T(8,128)}, f32[1,240,1024]{2,1,0:T(8,128)}, u32[]{:S(2)}, u32[]{:S(2)}) %collective-permute-start.5) | collective-permute-done | bytes 983072 | tf_op jit(solution)/shard_map/ppermute | solution.py:19
  230.6 2.4 %fusion.7 = f32[4,8,8,128]{3,1,2,0:T(8,128)S(1)} fusion(f32[32,1024]{1,0:T(8,128)S(1)} %fusion.9, f32[1,240,1024]{2,1,0:T(8,128)} %collective-permute-done.5, f32[240,1024]{1,0:T(8,128)} %squeeze.22, f32[1,240,1024]{2,1,0:T(8,128)} %collective-permute-done.4, s32[240]{0:T(256)S(1)} %eq.134), kind=kOutput, calls=%fused_computation.18 | convolution fusion | flops 94903808 | bytes 3212224 | tf_op jit(solution)/shard_map/dot_general | solution.py:162
  233.0 0.7 copy.87
  (94 shorter events, 2.3 us)
Async XLA Ops:
  0.6 167.0 %copy-start = (bf16[16,4,128,128]{3,2,1,0:T(8,128)(2,1)S(1)}, bf16[16,4,128,128]{3,2,1,0:T(8,128)(2,1)}, u32[]{:S(2)}) copy-start(bf16[16,4,128,128]{3,2,1,0:T(8,128)(2,1)} %param.26) | copy-start | bytes 6291460
  66.6 17.3 %collective-permute-start = (s32[1,16,160]{2,1,0:T(8,128)S(1)}, s32[1,16,160]{2,1,0:T(8,128)S(1)}, u32[]{:S(2)}, u32[]{:S(2)}) collective-permute-start(s32[1,16,160]{2,1,0:T(8,128)S(1)} %reshape.781), channel_id=1, source_target_pairs={{0,16},{16,32},{32,48},{48,64},{64,80},{80,96},{96,112},{112,0},{1... | collective-permute-start | bytes 30728 | tf_op jit(solution)/shard_map/ppermute | solution.py:18
  82.2 3.2 %collective-permute-start.1 = (s32[1,16,160]{2,1,0:T(8,128)S(1)}, s32[1,16,160]{2,1,0:T(8,128)S(1)}, u32[]{:S(2)}, u32[]{:S(2)}) collective-permute-start(s32[1,16,160]{2,1,0:T(8,128)S(1)} %reshape.781), channel_id=1, source_target_pairs={{16,0},{32,16},{48,32},{64,48},{80,64},{96,80},{112,96},{0,112},{1... | collective-permute-start | bytes 30728 | tf_op jit(solution)/shard_map/ppermute | solution.py:19
  91.4 2.7 %copy-start.15 = (s32[16,2]{0,1:T(2,128)S(1)}, s32[16,2]{0,1:T(2,128)}, u32[]{:S(2)}) copy-start(s32[16,2]{0,1:T(2,128)} %param.25) | copy-start | bytes 388
  91.4 3.3 %copy-start.13 = (s32[64,2]{0,1:T(2,128)S(1)}, s32[64,2]{0,1:T(2,128)}, u32[]{:S(2)}) copy-start(s32[64,2]{0,1:T(2,128)} %param.22) | copy-start | bytes 1540
  93.6 17.0 %collective-permute-start.2 = (bf16[1,240,3072]{2,1,0:T(8,128)(2,1)}, bf16[1,240,3072]{2,1,0:T(8,128)(2,1)}, u32[]{:S(2)}, u32[]{:S(2)}) collective-permute-start(bf16[1,240,3072]{2,1,0:T(8,128)(2,1)} %get-tuple-element.7), channel_id=1, source_target_pairs={{0,16},{16,32},{32,48},{48,64},{64,80},{80,96},{96,112},{112,0},{1... | collective-permute-start | bytes 4423688 | tf_op jit(solution)/shard_map/ppermute | solution.py:18
  93.9 19.1 %collective-permute-start.3 = (bf16[1,240,3072]{2,1,0:T(8,128)(2,1)}, bf16[1,240,3072]{2,1,0:T(8,128)(2,1)}, u32[]{:S(2)}, u32[]{:S(2)}) collective-permute-start(bf16[1,240,3072]{2,1,0:T(8,128)(2,1)} %get-tuple-element.6), channel_id=1, source_target_pairs={{16,0},{32,16},{48,32},{64,48},{80,64},{96,80},{112,96},{0,112},{1... | collective-permute-start | bytes 4423688 | tf_op jit(solution)/shard_map/ppermute | solution.py:19
  96.6 16.4 %copy-start.12 = (s32[160,1]{0,1:T(1,128)}, s32[160,1]{0,1:T(1,128)S(1)}, u32[]{:S(2)}) copy-start(s32[160,1]{0,1:T(1,128)S(1)} %compare_select_fusion) | copy-start | bytes 1924
  119.3 5.3 %copy-start.11 = (s32[2048]{0:T(1024)S(1)}, s32[2048]{0:T(1024)}, u32[]{:S(2)}) copy-start(s32[2048]{0:T(1024)} %param.20) | copy-start | bytes 24580
  119.3 5.9 %copy-start.8 = (s32[8192]{0:T(1024)S(1)}, s32[8192]{0:T(1024)}, u32[]{:S(2)}) copy-start(s32[8192]{0:T(1024)} %param.18) | copy-start | bytes 98308
  119.3 25.2 %all-to-all-start = ((bf16[16,15,3072]{2,1,0:T(8,128)(2,1)}), bf16[16,15,3072]{2,1,0:T(8,128)(2,1)}, u32[]{:S(2)}, u32[]{:S(2)}) async-start(bf16[16,15,3072]{2,1,0:T(8,128)(2,1)} %add_add_fusion), calls=%async_computation | async-start | bytes 3145728 | tf_op jit(solution)/shard_map/all_to_all | solution.py:91
  146.9 4.7 %copy-start.17 = (pred[160]{0:T(512)(128)(4,1)S(1)}, pred[160]{0:T(512)(128)(4,1)}, u32[]{:S(2)}) copy-start(pred[160]{0:T(512)(128)(4,1)} %compare_and_fusion.2) | copy-start | bytes 484
  153.0 1.1 copy-start.2
  167.5 0.7 copy-start.19
  167.5 0.7 copy-start.20
  167.5 1.0 copy-start.4
  167.5 1.0 copy-start.5
  167.5 1.1 copy-start.6
  169.9 5.7 %copy-start.3 = (f32[64,8,128]{2,1,0:T(8,128)}, f32[64,8,128]{2,1,0:T(8,128)S(1)}, u32[]{:S(2)}) copy-start(f32[64,8,128]{2,1,0:T(8,128)S(1)} %fusion.23) | copy-start | bytes 786436
  175.6 1.8 copy-start.9
  175.6 1.8 copy-start.10
  175.6 1.8 copy-start.18
  177.5 2.6 %copy-start.7 = (f32[16,8,128]{2,1,0:T(8,128)}, f32[16,8,128]{2,1,0:T(8,128)S(1)}, u32[]{:S(2)}) copy-start(f32[16,8,128]{2,1,0:T(8,128)S(1)} %fusion.32) | copy-start | bytes 196612
  181.3 15.9 %all-to-all-start.1 = ((f32[16,15,1024]{2,1,0:T(8,128)}), f32[16,15,1024]{2,1,0:T(8,128)S(1)}, u32[]{:S(2)}, u32[]{:S(2)}) async-start(f32[16,15,1024]{2,1,0:T(8,128)} %all_to_all.14), calls=%async_computation.1 | async-start | bytes 2097152 | tf_op jit(solution)/shard_map/all_to_all | solution.py:149
  199.0 17.8 %copy-start.14 = (s32[64,2]{0,1:T(2,128)S(1)}, s32[64,2]{0,1:T(2,128)}, u32[]{:S(2)}) copy-start(s32[64,2]{0,1:T(2,128)} %param.22) | copy-start | bytes 1540
  199.0 17.9 %copy-start.16 = (s32[16,2]{0,1:T(2,128)S(1)}, s32[16,2]{0,1:T(2,128)}, u32[]{:S(2)}) copy-start(s32[16,2]{0,1:T(2,128)} %param.25) | copy-start | bytes 388
  201.4 24.4 %collective-permute-start.4 = (f32[1,240,1024]{2,1,0:T(8,128)}, f32[1,240,1024]{2,1,0:T(8,128)}, u32[]{:S(2)}, u32[]{:S(2)}) collective-permute-start(f32[1,240,1024]{2,1,0:T(8,128)} %slice.88), channel_id=1, source_target_pairs={{0,16},{16,32},{32,48},{48,64},{64,80},{80,96},{96,112},{112,0},{1... | collective-permute-start | bytes 2949128 | tf_op jit(solution)/shard_map/ppermute | solution.py:18
  214.4 4.5 %copy-start.1 = (f32[16,15,1024]{2,1,0:T(8,128)S(1)}, f32[16,15,1024]{2,1,0:T(8,128)}, u32[]{:S(2)}) copy-start(f32[16,15,1024]{2,1,0:T(8,128)} %get-tuple-element.10) | copy-start | bytes 2949124
  216.8 13.8 %collective-permute-start.5 = (f32[1,240,1024]{2,1,0:T(8,128)}, f32[1,240,1024]{2,1,0:T(8,128)}, u32[]{:S(2)}, u32[]{:S(2)}) collective-permute-start(f32[1,240,1024]{2,1,0:T(8,128)} %slice.89), channel_id=1, source_target_pairs={{16,0},{32,16},{48,32},{64,48},{80,64},{96,80},{112,96},{0,112},{1... | collective-permute-start | bytes 2949128 | tf_op jit(solution)/shard_map/ppermute | solution.py:19
where the time goes:
time: 235 us; the launch traced here: 234 us
  blocking collectives  61.8 us (26%)
  waiting for transfers between devices  53.2 us (23%)
  local copies, waits for them, and re-layouts  44.5 us (19%)
  starting transfers between devices  38.1 us (16%)
  other arithmetic  17.9 us (8%)
  matrix products  16.5 us (7%)
    unnamed x1, blocking collectives  61.8 us
    ppermute x3, starting transfers between devices, padded(): before = lax.ppermute(last, axis, up)  29 us
    all_to_all x1, waiting for transfers between devices, per_device(): lax.all_to_all(relayed, 'cell', split_axis=0, concat_axis=0, tiled=True)  18.1 us
    ppermute x3, waiting for transfers between devices, padded(): before = lax.ppermute(last, axis, up)  17.1 us
    all_to_all x1, waiting for transfers between devices, per_device(): lax.all_to_all(back_out, 'cell', split_axis=0, concat_axis=0, tiled=True)  11.7 us
    unnamed x63, local copies, waits for them, and re-layouts  8.03 us
    squeeze x3, local copies, waits for them, and re-layouts, per_device(): relayed = rimmed[0] + rimmed[2] + rimmed[4]  7.52 us
    ppermute x3, waiting for transfers between devices, padded(): after = lax.ppermute(initial, axis, down)  6.31 us
  transfers between devices with their start and end apart: 8, of which 6 were waited for; matrix products, arithmetic and copies ran while one was open for 7% of the time, Pallas kernels for 0%

commit v1 on v0

v1 whole, which is shorter than its diff:
```python
import functools

import jax
import jax.numpy as jnp
from jax import lax
from jax.experimental import pallas as pl
from jax.experimental.pallas import tpu as pltpu
from jax.sharding import PartitionSpec as P

ocean_coef = (1.2, 0.9, 1.5, 0.7, 1.1, 1.3, 0.8, 1.0)
ice_coef = (0.5, 1.4, 0.6, 1.2, 0.9, 0.4, 1.6, 0.7)
land_coef = (0.8, 1.1, 0.6, 1.5, 0.7, 1.2, 1.0, 0.5)

BL = 128
AB = 32
CAP = 15
VMEM = pltpu.VMEM
SMEM = pltpu.SMEM
NN = (((1,), (0,)), ((), ()))
NT = (((1,), (1,)), ((), ()))


def dot(a, b, dims):
    return lax.dot_general(a, b, dims, preferred_element_type=jnp.float32)


def lanes(i):
    return pl.ds(pl.multiple_of(i * BL, BL), BL)


def whole(space=VMEM):
    return pl.BlockSpec(memory_space=space)


def column(values):
    row = lax.broadcasted_iota(jnp.int32, (8, BL), 0)
    out = jnp.full((8, BL), values[7], jnp.float32)
    for j in range(7):
        out = jnp.where(row == j, values[j], out)
    return out


def request_kernel(cells, om_ref, lm_ref, req_ref, slot_ref):
    sect = lax.axis_index("sect")
    before = jnp.zeros((cells, 1), jnp.float32)
    req = jnp.zeros((cells, BL), jnp.float32)
    slot_ref[...] = jnp.zeros(slot_ref.shape, jnp.int32)
    row = 0
    for ref in (om_ref, lm_ref):
        n = ref.shape[1]
        earlier = lax.broadcasted_iota(jnp.int32, (n, n), 0) < lax.broadcasted_iota(
            jnp.int32, (n, n), 1
        )
        earlier = jnp.where(earlier, 1.0, 0.0).astype(jnp.bfloat16)
        for k in range(ref.shape[0]):
            src = ref[k : k + 1, :]
            owner = src // AB
            col = owner % cells
            value = src % AB + jnp.where(owner // cells == sect, 0, AB)
            chosen = lax.broadcasted_iota(jnp.int32, (cells, n), 0) == col
            onehot = jnp.where(chosen, 1.0, 0.0)
            ranks = before + dot(onehot.astype(jnp.bfloat16), earlier, NN)
            rank = jnp.sum(jnp.where(chosen, ranks, 0.0), axis=0, keepdims=True)
            before = before + jnp.sum(onehot, axis=1, keepdims=True)
            place = lax.broadcasted_iota(jnp.int32, (BL, n), 0) == rank.astype(jnp.int32)
            place = jnp.where(place, 1.0, 0.0).astype(jnp.bfloat16)
            asked = jnp.where(chosen, (value + 1).astype(jnp.float32), 0.0)
            req = req + dot(asked.astype(jnp.bfloat16), place, NT)
            slot_ref[row : row + 1, :n] = col * CAP + rank.astype(jnp.int32)
            row += 1
    req_ref[...] = req.astype(jnp.int32) - 1


def requests(om, lm, cells):
    return pl.pallas_call(
        functools.partial(request_kernel, cells),
        out_shape=(
            jax.ShapeDtypeStruct((cells, BL), jnp.int32),
            jax.ShapeDtypeStruct((8, BL), jnp.int32),
        ),
        in_specs=[whole()] * 2,
        out_specs=[whole()] * 2,
        name="requests",
    )(om, lm)


def serve_kernel(cells, asked_ref, own_ref, near_ref, out_ref, both):
    width = own_ref.shape[1]
    both[:, :width] = own_ref[...]
    both[:, width:] = near_ref[...]

    def body(c, _):
        for r in range(CAP):
            i = jnp.maximum(asked_ref[c, r], 0)
            out_ref[c * CAP + r] = both[:, lanes(i)]
        return 0

    lax.fori_loop(0, cells, body, 0)


def serve(asked, own, near, cells):
    fields, width = own.shape
    return pl.pallas_call(
        functools.partial(serve_kernel, cells),
        out_shape=jax.ShapeDtypeStruct((cells * CAP, fields, BL), own.dtype),
        in_specs=[whole(SMEM), whole(), whole()],
        out_specs=whole(),
        scratch_shapes=[VMEM((fields, 2 * width), own.dtype)],
        compiler_params=pltpu.CompilerParams(vmem_limit_bytes=24 << 20),
        name="serve",
    )(asked, own, near)


STEPS = 8


def tile_specs(ob, lb, half):
    return [
        pl.BlockSpec((ob // STEPS, 2, BL, BL), lambda i: (i, half, 0, 0)),
        pl.BlockSpec((lb // STEPS, 2, BL, BL), lambda i: (i, half, 0, 0)),
    ]


def near_mix_kernel(ol_ref, ll_ref, f_ref, ot_ref, lt_ref, om_ref, lm_ref):
    step = pl.program_id(0)
    for ids, tiles, out in ((ol_ref, ot_ref, om_ref), (ll_ref, lt_ref, lm_ref)):
        n = tiles.shape[0]
        for b in range(n):
            src = [f_ref[:, lanes(ids[k, step * n + b])] for k in range(2)]
            out[b] = dot(
                jnp.concatenate(src, axis=1), tiles[b].reshape(2 * BL, BL), NN
            )


def near_mix(ol, ll, fields, ot, lt):
    ob, lb = ot.shape[0], lt.shape[0]
    nf = fields.shape[0]
    return pl.pallas_call(
        near_mix_kernel,
        grid=(STEPS,),
        out_shape=(
            jax.ShapeDtypeStruct((ob, nf, BL), jnp.float32),
            jax.ShapeDtypeStruct((lb, nf, BL), jnp.float32),
        ),
        in_specs=[
            whole(SMEM),
            whole(SMEM),
            pl.BlockSpec(fields.shape, lambda i: (0, 0)),
            *tile_specs(ob, lb, 1),
        ],
        out_specs=[
            pl.BlockSpec((ob // STEPS, nf, BL), lambda i: (i, 0, 0)),
            pl.BlockSpec((lb // STEPS, nf, BL), lambda i: (i, 0, 0)),
        ],
        compiler_params=pltpu.CompilerParams(vmem_limit_bytes=24 << 20),
        cost_estimate=pl.CostEstimate(
            flops=2 * (ob + lb) * 2 * BL * BL * 128,
            bytes_accessed=(ob + lb) * 2 * BL * BL * 2,
            transcendentals=0,
        ),
        name="near_mix",
    )(ol, ll, fields, ot, lt)


def far_kernel(
    slot_ref, got_ref, ot_ref, lt_ref, om_ref, lm_ref, os_ref, is_ref, il_ref, ls_ref, ll_ref,
    of_ref, lf_ref, send_ref, mixed,
):
    step = pl.program_id(0)

    @pl.when(step == 0)
    def _():
        send_ref[...] = jnp.zeros(send_ref.shape, send_ref.dtype)

    ocean, ice, land = column(ocean_coef), column(ice_coef), column(land_coef)
    no, nl = ot_ref.shape[0], lt_ref.shape[0]
    for b in range(no + nl):
        is_ocean = b < no
        tiles, near = (ot_ref, om_ref) if is_ocean else (lt_ref, lm_ref)
        c = b if is_ocean else b - no
        base = 0 if is_ocean else 2
        at = step * (no if is_ocean else nl) + c
        slots = [slot_ref[base + k, at] for k in range(2)]
        weights = tiles[c].reshape(2 * BL, BL)
        src = jnp.concatenate([got_ref[s] for s in slots], axis=1)
        mixed[b] = near[c] + dot(src, weights, NN)
        u = mixed[b, pl.ds(0, 8, stride=3), :]
        v = mixed[b, pl.ds(1, 8, stride=3), :]
        t = mixed[b, pl.ds(2, 8, stride=3), :]
        wind = jnp.sqrt(1.0 + u * u + v * v)
        here = slice(c * BL, (c + 1) * BL)
        if is_ocean:
            frac = il_ref[c : c + 1, :].astype(jnp.float32) / 8.0
            flux = (1.0 - frac) * (ocean * wind * (t - os_ref[:, here]))
            flux = flux + frac * (ice * wind * (t - is_ref[:, here]))
            of_ref[:, here] = flux
        else:
            frac = ll_ref[pl.ds(at, 1), :].astype(jnp.float32) / 8.0
            flux = frac * (land * wind * (t - ls_ref[:, here]))
            lf_ref[:, here] = flux
        terms = dot(flux.astype(jnp.bfloat16), weights, NT).astype(send_ref.dtype)
        for k in range(2):
            send_ref[slots[k]] = terms[:, k * BL : (k + 1) * BL]


def far(slots, got, ot, lt, om, lm, os, ice, il, ls, ll):
    ob, lb = ot.shape[0], lt.shape[0]
    nf, ns = om.shape[1], os.shape[0]
    no, nl = ob // STEPS, lb // STEPS
    return pl.pallas_call(
        far_kernel,
        grid=(STEPS,),
        out_shape=(
            jax.ShapeDtypeStruct(os.shape, jnp.float32),
            jax.ShapeDtypeStruct(ls.shape, jnp.float32),
            jax.ShapeDtypeStruct((got.shape[0], ns, BL), jnp.bfloat16),
        ),
        in_specs=[
            whole(SMEM),
            pl.BlockSpec(got.shape, lambda i: (0, 0, 0)),
            *tile_specs(ob, lb, 0),
            pl.BlockSpec((no, nf, BL), lambda i: (i, 0, 0)),
            pl.BlockSpec((nl, nf, BL), lambda i: (i, 0, 0)),
            pl.BlockSpec((ns, no * BL), lambda i: (0, i)),
            pl.BlockSpec((ns, no * BL), lambda i: (0, i)),
            pl.BlockSpec((no, BL), lambda i: (i, 0)),
            pl.BlockSpec((ns, nl * BL), lambda i: (0, i)),
            pl.BlockSpec((lb, BL), lambda i: (0, 0)),
        ],
        out_specs=[
            pl.BlockSpec((ns, no * BL), lambda i: (0, i)),
            pl.BlockSpec((ns, nl * BL), lambda i: (0, i)),
            pl.BlockSpec((got.shape[0], ns, BL), lambda i: (0, 0, 0)),
        ],
        scratch_shapes=[VMEM((no + nl, nf, BL), jnp.float32)],
        compiler_params=pltpu.CompilerParams(vmem_limit_bytes=32 << 20),
        name="far",
    )(slots, got, ot, lt, om, lm, os, ice, il, ls, ll)


def near_back_kernel(ol_ref, ll_ref, of_ref, lf_ref, ot_ref, lt_ref, out_ref):
    step = pl.program_id(0)

    @pl.when(step == 0)
    def _():
        out_ref[...] = jnp.zeros(out_ref.shape, out_ref.dtype)

    for ids, flux, tiles in ((ol_ref, of_ref, ot_ref), (ll_ref, lf_ref, lt_ref)):
        n = tiles.shape[0]
        for b in range(n):
            g = flux[:, b * BL : (b + 1) * BL].astype(jnp.bfloat16)
            terms = dot(g, tiles[b].reshape(2 * BL, BL), NT)
            for k in range(2):
                at = lanes(ids[k, step * n + b])
                out_ref[:, at] = out_ref[:, at] + terms[:, k * BL : (k + 1) * BL]


def near_back(ol, ll, of, lf, ot, lt):
    ob, lb = ot.shape[0], lt.shape[0]
    ns = of.shape[0]
    return pl.pallas_call(
        near_back_kernel,
        grid=(STEPS,),
        out_shape=jax.ShapeDtypeStruct((ns, AB * BL), jnp.float32),
        in_specs=[
            whole(SMEM),
            whole(SMEM),
            pl.BlockSpec((ns, ob // STEPS * BL), lambda i: (0, i)),
            pl.BlockSpec((ns, lb // STEPS * BL), lambda i: (0, i)),
            *tile_specs(ob, lb, 1),
        ],
        out_specs=pl.BlockSpec((ns, AB * BL), lambda i: (0, 0)),
        compiler_params=pltpu.CompilerParams(vmem_limit_bytes=24 << 20),
        cost_estimate=pl.CostEstimate(
            flops=2 * (ob + lb) * 2 * BL * BL * 128,
            bytes_accessed=(ob + lb) * 2 * BL * BL * 2,
            transcendentals=0,
        ),
        name="near_back",
    )(ol, ll, of, lf, ot, lt)


def collect_kernel(cells, neighbours, asked_ref, back_ref, *refs):
    acc_refs, out_ref, total = refs[:-2], refs[-2], refs[-1]
    cell = lax.axis_index("cell")
    half = cells // 2
    width = out_ref.shape[1]
    if acc_refs:
        total[:, :width] = acc_refs[0][...]
    else:
        total[:, :width] = jnp.zeros((total.shape[0], width), jnp.float32)

    def body(c, _):
        far_one = jnp.logical_or(c <= cell - half, c > cell + half)

        @pl.when(far_one == neighbours)
        def _():
            for r in range(CAP):
                i = asked_ref[c, r]
                at = lanes(jnp.where(i < 0, AB, lax.rem(i, AB)))
                total[:, at] = total[:, at] + back_ref[c * CAP + r].astype(jnp.float32)

        return 0

    lax.fori_loop(0, cells, body, 0)
    out_ref[...] = total[:, :width]


def collect(asked, back, acc, neighbours, cells):
    ns = back.shape[1]
    accs = () if acc is None else (acc,)
    return pl.pallas_call(
        functools.partial(collect_kernel, cells, neighbours),
        out_shape=jax.ShapeDtypeStruct((ns, AB * BL), jnp.float32),
        in_specs=[whole(SMEM), whole(), *[whole()] * len(accs)],
        out_specs=whole(),
        scratch_shapes=[VMEM((ns, (AB + 1) * BL), jnp.float32)],
        cost_estimate=pl.CostEstimate(
            flops=1 << 20, bytes_accessed=4 << 20, transcendentals=0
        ),
        name="collect_far" if neighbours else "collect_own",
    )(asked, back, *accs)


def per_device(
    sects, cells, atm_fields, ocn_state, ice_state, ice_level, lnd_state, lnd_level,
    ocn_map, ocn_local, ocn_tiles, lnd_map, lnd_local, lnd_tiles,
):
    axes = ("sect", "cell")
    count = sects * cells
    half = cells // 2
    to_server = []
    for q in range(count):
        s, c = divmod(q, cells)
        to_server.append((q, (s + (1 if c >= half else -1)) % sects * cells + c))
    to_owner = [(b, a) for a, b in to_server]
    exchange = functools.partial(
        lax.all_to_all, axis_name="cell", split_axis=0, concat_axis=0, tiled=True
    )

    near_fields = lax.ppermute(atm_fields, axes, to_server)
    asking, slots = requests(ocn_map.T, lnd_map.T, cells)
    asked = exchange(asking)
    got = exchange(serve(asked, atm_fields, near_fields, cells))
    ol, ll = ocn_local.T, lnd_local.T
    om, lm = near_mix(ol, ll, atm_fields, ocn_tiles, lnd_tiles)
    of, lf, send = far(
        slots, got, ocn_tiles, lnd_tiles, om, lm, ocn_state, ice_state,
        ice_level.reshape(-1, BL), lnd_state, lnd_level.reshape(-1, BL),
    )
    back = exchange(send)
    acc = near_back(ol, ll, of, lf, ocn_tiles, lnd_tiles)
    away = lax.ppermute(collect(asked, back, None, True, cells), axes, to_owner)
    own = collect(asked, back, acc, False, cells)
    return own + away, of, lf


def solution(mesh):
    a = ("sect", "cell")
    in_specs = (
        P(None, a), P(None, a), P(None, a), P(a), P(None, a), P(a),
        P(a, None), P(a, None), P(a, None, None, None),
        P(a, None), P(a, None), P(a, None, None, None),
    )
    return jax.shard_map(
        functools.partial(per_device, mesh.shape["sect"], mesh.shape["cell"]),
        mesh=mesh,
        in_specs=in_specs,
        out_specs=(P(None, a), P(None, a), P(None, a)),
        check_vma=False,
    )
```

time: 235 us -> 98 us (0.42)
  the two profiles are of different devices: /device:TPU:5 before, /device:TPU:1 now
where the time goes in v1:
time: 98 us; the launch traced here: 97.3 us
  blocking collectives  29.2 us (30%)
  Pallas kernels  23.9 us (24%)
  local copies, waits for them, and re-layouts  17.9 us (18%)
  waiting for transfers between devices  12.9 us (13%)
  starting transfers between devices  11.2 us (11%)
  other arithmetic  1.58 us (2%)
    unnamed x40, local copies, waits for them, and re-layouts  17.9 us
    all_to_all x1, blocking collectives, per_device(): asked = exchange(asking)  15.3 us
    all_to_all x1, blocking collectives, per_device(): back = exchange(send)  14 us
    all_to_all x1, waiting for transfers between devices, per_device(): got = exchange(serve(asked, atm_fields, near_fields, cells))  12.9 us
    pallas_call x1, Pallas kernels, far(): pl.pallas_call(far_kernel, grid=(STEPS,), out_shape=(jax.ShapeDtypeStruct...  9.8 us
    ppermute x1, starting transfers between devices, per_device(): away = lax.ppermute(collect(asked, back, None, True, cells), axes, to_owner)  5.28 us
    pallas_call x2, Pallas kernels, collect(): pl.pallas_call(functools.partial(collect_kernel, cells, neighbours), out_...  4.82 us
    all_to_all x1, starting transfers between devices, per_device(): got = exchange(serve(asked, atm_fields, near_fields, cells))  4.4 us
  transfers between devices with their start and end apart: 3, of which 1 were waited for; matrix products, arithmetic and copies ran while one was open for 0% of the time, Pallas kernels for 11%

profile of v1, /device:TPU:1, one launch (start us, length us, event | category | flops | bytes accessed | tf_op | source)
XLA Modules:
  0.0 97.3 jit_solution(17388667959775422927)
XLA Ops:
  0.6 1.5 %collective-permute-start = (bf16[24,4096]{1,0:T(8,128)(2,1)}, bf16[24,4096]{1,0:T(8,128)(2,1)S(1)}, u32[]{:S(2)}, u32[]{:S(2)}) collective-permute-start(bf16[24,4096]{1,0:T(8,128)(2,1)} %f_ref.1), channel_id=1, source_target_pairs={{0,112},{1,113},{2,114},{3,115},{4,116},{5,117},{6,118},{7,119},{8... | collective-permute-start | bytes 589832 | tf_op jit(solution)/shard_map/ppermute | solution.py:341
  2.1 1.8 %requests.1 = (s32[16,128]{1,0:T(8,128)}, s32[8,128]{1,0:T(8,128)}) custom-call(s32[2,64]{1,0:T(2,128)} %bitcast.20, s32[2,16]{1,0:T(2,128)} %bitcast.21), custom_call_target="tpu_custom_call" | custom-call | tf_op jit(solution)/shard_map/requests/pallas_call | solution.py:75
  3.9 15.3 %all_to_all.21 = s32[16,1,128]{2,1,0:T(1,128)S(1)} all-to-all(s32[16,1,128]{2,1,0:T(1,128)} %bitcast.19), channel_id=1, replica_groups=mesh['sect'=8,'cell'=16] {'cell'}, dimensions={0} | all-to-all | bytes 16384 | tf_op jit(solution)/shard_map/all_to_all | solution.py:343
  19.2 0.0 copy-start.11
  19.2 0.0 collective-permute-done.near_ref
  19.2 0.0 copy-start.5
  19.2 0.9 copy-done.5
  20.1 0.0 copy-start.3
  20.1 0.0 copy-start.6
  20.1 0.0 copy-start.17
  20.1 1.3 %serve.1 = bf16[240,24,128]{2,1,0:T(8,128)(2,1)S(1)} custom-call(s32[16,128]{1,0:T(8,128)S(1)} %bitcast.10, bf16[24,4096]{1,0:T(8,128)(2,1)S(1)} %copy-done.5, bf16[24,4096]{1,0:T(8,128)(2,1)S(1)} %collective-permute-done.near_ref), custom_call_target="tpu_custom_call" | custom-call | tf_op jit(solution)/shard_map/serve/pallas_call | solution.py:103
  21.4 0.0 copy-start.4
  21.4 1.1 %copy-done.4 = bf16[240,24,128]{2,1,0:T(8,128)(2,1)} copy-done((bf16[240,24,128]{2,1,0:T(8,128)(2,1)}, bf16[240,24,128]{2,1,0:T(8,128)(2,1)S(1)}, u32[]{:S(2)}) %copy-start.4) | copy-done | bytes 1474584
  22.6 0.0 copy-done.11
  22.6 4.4 %all-to-all-start.1 = ((bf16[240,24,128]{2,1,0:T(8,128)(2,1)}), bf16[240,24,128]{2,1,0:T(8,128)(2,1)}, u32[]{:S(2)}, u32[]{:S(2)}) async-start(bf16[240,24,128]{2,1,0:T(8,128)(2,1)} %copy-done.4), calls=%async_computation.1 | async-start | bytes 2949120 | tf_op jit(solution)/shard_map/all_to_all | solution.py:344
  27.0 0.0 copy-done.3
  27.0 0.0 copy-done.6
  27.0 0.0 copy-done.17
  27.0 0.0 copy-start
  27.0 3.4 %copy-done = bf16[64,4,128,128]{3,2,1,0:T(8,128)(2,1)S(1)} copy-done((bf16[64,4,128,128]{3,2,1,0:T(8,128)(2,1)S(1)}, bf16[64,4,128,128]{3,2,1,0:T(8,128)(2,1)}, u32[]{:S(2)}) %copy-start) | copy-done | bytes 8388632
  30.4 0.0 copy-start.18
  30.4 0.7 copy-done.18
  31.1 0.0 copy-start.8
  31.1 0.0 copy-start.15
  31.1 0.0 copy-start.16
  31.1 2.8 %near_mix.1 = (f32[64,24,128]{2,1,0:T(8,128)S(1)}, f32[16,24,128]{2,1,0:T(8,128)S(1)}) custom-call(s32[2,64]{1,0:T(2,128)S(1)} %bitcast.15, s32[2,16]{1,0:T(2,128)S(1)} %bitcast.17, bf16[24,4096]{1,0:T(8,128)(2,1)S(1)} %copy-done.6, bf16[64,4,128,128]{3,2,1,0:T(8,128)(2,1)S(1)} %copy-done, bf16[16,4,128,128]{3,2,1,0:T(8,128)(2,1)S(1)} %copy-done.3), custom_call_target="tpu_custom_call" | custom-call | flops 671088640 | bytes 5242880 | tf_op jit(solution)/shard_map/near_mix/pallas_call | solution.py:138
  33.9 12.9 %all-to-all-done.1.got_ref = bf16[240,24,128]{2,1,0:T(8,128)(2,1)} async-done(((bf16[240,24,128]{2,1,0:T(8,128)(2,1)}), bf16[240,24,128]{2,1,0:T(8,128)(2,1)}, u32[]{:S(2)}, u32[]{:S(2)}) %all-to-all-start.1) | async-done | bytes 1474592 | tf_op jit(solution)/shard_map/all_to_all | solution.py:344
  46.8 0.0 copy-done.8
  46.8 0.0 copy-done.15
  46.8 0.0 copy-done.16
  46.8 0.0 copy-start.1
  46.8 3.4 %copy-done.1 = bf16[64,4,128,128]{3,2,1,0:T(8,128)(2,1)S(1)} copy-done((bf16[64,4,128,128]{3,2,1,0:T(8,128)(2,1)S(1)}, bf16[64,4,128,128]{3,2,1,0:T(8,128)(2,1)}, u32[]{:S(2)}) %copy-start.1) | copy-done | bytes 8388632
  50.2 0.0 copy-start.9
  50.2 0.9 copy-done.9
  51.1 0.0 copy-start.12
  51.1 0.8 copy-done.12
  51.9 0.0 copy-start.14
  51.9 0.8 copy-done.14
  52.7 0.0 copy-start.19
  52.7 9.8 %far.1 = (f32[8,8192]{1,0:T(8,128)}, f32[8,2048]{1,0:T(8,128)}, bf16[240,8,128]{2,1,0:T(8,128)(2,1)S(1)}) custom-call(s32[8,128]{1,0:T(8,128)S(1)} %copy-done.16, bf16[240,24,128]{2,1,0:T(8,128)(2,1)} %all-to-all-done.1.got_ref, bf16[64,4,128,128]{3,2,1,0:T(8,128)(2,1)S(1)} %copy-done.1, bf16[16,4,128,128]{3,2,1,0:T(8,128)(2,1)S(1)} %copy-done.3, ...), custom_call_target="tpu_custom_call" | custom-call | tf_op jit(solution)/shard_map/far/pallas_call | solution.py:210
  62.5 14.0 %all_to_all.22.back_ref = bf16[240,8,128]{2,1,0:T(8,128)(2,1)} all-to-all(bf16[240,8,128]{2,1,0:T(8,128)(2,1)S(1)} %get-tuple-element.14), channel_id=1, replica_groups=mesh['sect'=8,'cell'=16] {'cell'}, dimensions={0} | all-to-all | bytes 983040 | tf_op jit(solution)/shard_map/all_to_all | solution.py:351
  76.5 2.3 %collect_far.1 = f32[8,4096]{1,0:T(8,128)} custom-call(s32[16,128]{1,0:T(8,128)} %bitcast.11, bf16[240,8,128]{2,1,0:T(8,128)(2,1)} %all_to_all.22.back_ref), custom_call_target="tpu_custom_call" | custom-call | flops 1048576 | bytes 4194304 | tf_op jit(solution)/shard_map/collect_far/pallas_call | solution.py:312
  78.8 5.3 %collective-permute-start.1 = (f32[8,4096]{1,0:T(8,128)}, f32[8,4096]{1,0:T(8,128)S(1)}, u32[]{:S(2)}, u32[]{:S(2)}) collective-permute-start(f32[8,4096]{1,0:T(8,128)} %collect_far.1), channel_id=1, source_target_pairs={{112,0},{113,1},{114,2},{115,3},{116,4},{117,5},{118,6},{119,7},{2... | collective-permute-start | bytes 393224 | tf_op jit(solution)/shard_map/ppermute | solution.py:353
  84.1 0.0 copy-done.19
  84.1 0.0 copy-start.2
  84.1 3.4 %copy-done.2 = bf16[64,4,128,128]{3,2,1,0:T(8,128)(2,1)S(1)} copy-done((bf16[64,4,128,128]{3,2,1,0:T(8,128)(2,1)S(1)}, bf16[64,4,128,128]{3,2,1,0:T(8,128)(2,1)}, u32[]{:S(2)}) %copy-start.2) | copy-done | bytes 8388632
  87.5 0.0 copy-start.10
  87.5 0.9 copy-done.10
  88.4 0.0 copy-start.13
  88.4 0.8 copy-done.13
  89.3 3.3 %near_back.1.refs_0_ = f32[8,4096]{1,0:T(8,128)S(1)} custom-call(s32[2,64]{1,0:T(2,128)S(1)} %bitcast.16, s32[2,16]{1,0:T(2,128)S(1)} %bitcast.18, f32[8,8192]{1,0:T(8,128)S(1)} %copy-done.10, f32[8,2048]{1,0:T(8,128)S(1)} %copy-done.13, bf16[64,4,128,128]{3,2,1,0:T(8,128)(2,1)S(1)} %copy-done.2, bf16[16,4,128,128]{3,2,1,0:T(8,128)(2,1)S(1)} %copy-done.3), custom_call_target="tpu_custom_call" | custom-call | flops 671088640 | bytes 5242880 | tf_op jit(solution)/shard_map/near_back/pallas_call | solution.py:261
  92.6 0.0 copy-start.7
  92.6 0.6 copy-done.7
  93.3 2.5 %collect_own.1 = f32[8,4096]{1,0:T(8,128)} custom-call(s32[16,128]{1,0:T(8,128)} %bitcast.12, bf16[240,8,128]{2,1,0:T(8,128)(2,1)} %all_to_all.22.back_ref, f32[8,4096]{1,0:T(8,128)} %copy-done.7), custom_call_target="tpu_custom_call" | custom-call | flops 1048576 | bytes 4194304 | tf_op jit(solution)/shard_map/collect_own/pallas_call | solution.py:312
  95.7 0.0 collective-permute-done.1
  95.7 1.6 %add.3 = f32[8,4096]{1,0:T(8,128)} add(f32[8,4096]{1,0:T(8,128)} %collect_own.1, f32[8,4096]{1,0:T(8,128)S(1)} %collective-permute-done.1) | non-fusion elementwise | flops 32768 | bytes 393216 | tf_op jit(solution)/shard_map/add | solution.py:355
Async XLA Ops:
  0.6 18.6 %collective-permute-start = (bf16[24,4096]{1,0:T(8,128)(2,1)}, bf16[24,4096]{1,0:T(8,128)(2,1)S(1)}, u32[]{:S(2)}, u32[]{:S(2)}) collective-permute-start(bf16[24,4096]{1,0:T(8,128)(2,1)} %f_ref.1), channel_id=1, source_target_pairs={{0,112},{1,113},{2,114},{3,115},{4,116},{5,117},{6,118},{7,119},{8... | collective-permute-start | bytes 589832 | tf_op jit(solution)/shard_map/ppermute | solution.py:341
  19.2 3.4 %copy-start.11 = (s32[16,1,128]{2,1,0:T(1,128)}, s32[16,1,128]{2,1,0:T(1,128)S(1)}, u32[]{:S(2)}) copy-start(s32[16,1,128]{2,1,0:T(1,128)S(1)} %all_to_all.21) | copy-start | bytes 24580
  19.2 0.9 copy-start.5
  20.1 6.8 %copy-start.3 = (bf16[16,4,128,128]{3,2,1,0:T(8,128)(2,1)S(1)}, bf16[16,4,128,128]{3,2,1,0:T(8,128)(2,1)}, u32[]{:S(2)}) copy-start(bf16[16,4,128,128]{3,2,1,0:T(8,128)(2,1)} %lt_ref.5) | copy-start | bytes 6291460
  20.1 6.8 %copy-start.6 = (bf16[24,4096]{1,0:T(8,128)(2,1)S(1)}, bf16[24,4096]{1,0:T(8,128)(2,1)}, u32[]{:S(2)}) copy-start(bf16[24,4096]{1,0:T(8,128)(2,1)} %f_ref.1) | copy-start | bytes 589828
  20.1 6.8 %copy-start.17 = (s32[64,2]{0,1:T(2,128)S(1)}, s32[64,2]{0,1:T(2,128)}, u32[]{:S(2)}) copy-start(s32[64,2]{0,1:T(2,128)} %param.19) | copy-start | bytes 1540
  21.4 1.1 %copy-start.4 = (bf16[240,24,128]{2,1,0:T(8,128)(2,1)}, bf16[240,24,128]{2,1,0:T(8,128)(2,1)S(1)}, u32[]{:S(2)}) copy-start(bf16[240,24,128]{2,1,0:T(8,128)(2,1)S(1)} %serve.1) | copy-start | bytes 4423684
  22.6 24.2 %all-to-all-start.1 = ((bf16[240,24,128]{2,1,0:T(8,128)(2,1)}), bf16[240,24,128]{2,1,0:T(8,128)(2,1)}, u32[]{:S(2)}, u32[]{:S(2)}) async-start(bf16[240,24,128]{2,1,0:T(8,128)(2,1)} %copy-done.4), calls=%async_computation.1 | async-start | bytes 2949120 | tf_op jit(solution)/shard_map/all_to_all | solution.py:344
  27.0 3.4 %copy-start = (bf16[64,4,128,128]{3,2,1,0:T(8,128)(2,1)S(1)}, bf16[64,4,128,128]{3,2,1,0:T(8,128)(2,1)}, u32[]{:S(2)}) copy-start(bf16[64,4,128,128]{3,2,1,0:T(8,128)(2,1)} %ot_ref.5) | copy-start | bytes 25165828
  30.4 0.7 copy-start.18
  31.1 15.7 %copy-start.8 = (f32[8,8192]{1,0:T(8,128)S(1)}, f32[8,8192]{1,0:T(8,128)}, u32[]{:S(2)}) copy-start(f32[8,8192]{1,0:T(8,128)} %os_ref.1) | copy-start | bytes 786436
  31.1 15.7 %copy-start.15 = (s32[2048]{0:T(1024)S(1)}, s32[2048]{0:T(1024)}, u32[]{:S(2)}) copy-start(s32[2048]{0:T(1024)} %param.17) | copy-start | bytes 24580
  31.1 15.7 %copy-start.16 = (s32[8,128]{1,0:T(8,128)S(1)}, s32[8,128]{1,0:T(8,128)}, u32[]{:S(2)}) copy-start(s32[8,128]{1,0:T(8,128)} %get-tuple-element.11.slot_ref) | copy-start | bytes 12292
  46.8 3.4 %copy-start.1 = (bf16[64,4,128,128]{3,2,1,0:T(8,128)(2,1)S(1)}, bf16[64,4,128,128]{3,2,1,0:T(8,128)(2,1)}, u32[]{:S(2)}) copy-start(bf16[64,4,128,128]{3,2,1,0:T(8,128)(2,1)} %ot_ref.5) | copy-start | bytes 25165828
  50.2 0.9 copy-start.9
  51.1 0.8 copy-start.12
  51.9 0.8 copy-start.14
  52.7 31.4 %copy-start.19 = (s32[16,2]{0,1:T(2,128)S(1)}, s32[16,2]{0,1:T(2,128)}, u32[]{:S(2)}) copy-start(s32[16,2]{0,1:T(2,128)} %param.22) | copy-start | bytes 388
  78.8 16.9 %collective-permute-start.1 = (f32[8,4096]{1,0:T(8,128)}, f32[8,4096]{1,0:T(8,128)S(1)}, u32[]{:S(2)}, u32[]{:S(2)}) collective-permute-start(f32[8,4096]{1,0:T(8,128)} %collect_far.1), channel_id=1, source_target_pairs={{112,0},{113,1},{114,2},{115,3},{116,4},{117,5},{118,6},{119,7},{2... | collective-permute-start | bytes 393224 | tf_op jit(solution)/shard_map/ppermute | solution.py:353
  84.1 3.4 %copy-start.2 = (bf16[64,4,128,128]{3,2,1,0:T(8,128)(2,1)S(1)}, bf16[64,4,128,128]{3,2,1,0:T(8,128)(2,1)}, u32[]{:S(2)}) copy-start(bf16[64,4,128,128]{3,2,1,0:T(8,128)(2,1)} %ot_ref.5) | copy-start | bytes 25165828
  87.5 0.9 copy-start.10
  88.4 0.8 copy-start.13
  92.6 0.7 copy-start.7

commit v2 on v1

--- a/solution.py
+++ b/solution.py
@@ -14,6 +14,8 @@
 BL = 128
 AB = 32
 CAP = 15
+GRANT = 60 << 20
+CHAINS = 5
 VMEM = pltpu.VMEM
 SMEM = pltpu.SMEM
 NN = (((1,), (0,)), ((), ()))
@@ -80,6 +82,7 @@
         ),
         in_specs=[whole()] * 2,
         out_specs=[whole()] * 2,
+        compiler_params=pltpu.CompilerParams(vmem_limit_bytes=GRANT),
         name="requests",
     )(om, lm)
 
@@ -106,12 +109,12 @@
         in_specs=[whole(SMEM), whole(), whole()],
         out_specs=whole(),
         scratch_shapes=[VMEM((fields, 2 * width), own.dtype)],
-        compiler_params=pltpu.CompilerParams(vmem_limit_bytes=24 << 20),
+        compiler_params=pltpu.CompilerParams(vmem_limit_bytes=GRANT),
         name="serve",
     )(asked, own, near)
 
 
-STEPS = 8
+STEPS = 4
 
 
 def tile_specs(ob, lb, half):
@@ -152,7 +155,7 @@
             pl.BlockSpec((ob // STEPS, nf, BL), lambda i: (i, 0, 0)),
             pl.BlockSpec((lb // STEPS, nf, BL), lambda i: (i, 0, 0)),
         ],
-        compiler_params=pltpu.CompilerParams(vmem_limit_bytes=24 << 20),
+        compiler_params=pltpu.CompilerParams(vmem_limit_bytes=GRANT),
         cost_estimate=pl.CostEstimate(
             flops=2 * (ob + lb) * 2 * BL * BL * 128,
             bytes_accessed=(ob + lb) * 2 * BL * BL * 2,
@@ -174,16 +177,18 @@
 
     ocean, ice, land = column(ocean_coef), column(ice_coef), column(land_coef)
     no, nl = ot_ref.shape[0], lt_ref.shape[0]
+    blocks = []
     for b in range(no + nl):
         is_ocean = b < no
+        c = b if is_ocean else b - no
+        at = step * (no if is_ocean else nl) + c
+        slots = [slot_ref[(0 if is_ocean else 2) + k, at] for k in range(2)]
+        blocks.append((is_ocean, c, at, slots))
+    for b, (is_ocean, c, at, slots) in enumerate(blocks):
         tiles, near = (ot_ref, om_ref) if is_ocean else (lt_ref, lm_ref)
-        c = b if is_ocean else b - no
-        base = 0 if is_ocean else 2
-        at = step * (no if is_ocean else nl) + c
-        slots = [slot_ref[base + k, at] for k in range(2)]
-        weights = tiles[c].reshape(2 * BL, BL)
         src = jnp.concatenate([got_ref[s] for s in slots], axis=1)
-        mixed[b] = near[c] + dot(src, weights, NN)
+        mixed[b] = near[c] + dot(src, tiles[c].reshape(2 * BL, BL), NN)
+    for b, (is_ocean, c, at, slots) in enumerate(blocks):
         u = mixed[b, pl.ds(0, 8, stride=3), :]
         v = mixed[b, pl.ds(1, 8, stride=3), :]
         t = mixed[b, pl.ds(2, 8, stride=3), :]
@@ -198,7 +203,11 @@
             frac = ll_ref[pl.ds(at, 1), :].astype(jnp.float32) / 8.0
             flux = frac * (land * wind * (t - ls_ref[:, here]))
             lf_ref[:, here] = flux
-        terms = dot(flux.astype(jnp.bfloat16), weights, NT).astype(send_ref.dtype)
+    for b, (is_ocean, c, at, slots) in enumerate(blocks):
+        tiles, flux = (ot_ref, of_ref) if is_ocean else (lt_ref, lf_ref)
+        here = slice(c * BL, (c + 1) * BL)
+        terms = dot(flux[:, here].astype(jnp.bfloat16), tiles[c].reshape(2 * BL, BL), NT)
+        terms = terms.astype(send_ref.dtype)
         for k in range(2):
             send_ref[slots[k]] = terms[:, k * BL : (k + 1) * BL]
 
@@ -233,7 +242,7 @@
             pl.BlockSpec((got.shape[0], ns, BL), lambda i: (0, 0, 0)),
         ],
         scratch_shapes=[VMEM((no + nl, nf, BL), jnp.float32)],
-        compiler_params=pltpu.CompilerParams(vmem_limit_bytes=32 << 20),
+        compiler_params=pltpu.CompilerParams(vmem_limit_bytes=GRANT),
         name="far",
     )(slots, got, ot, lt, om, lm, os, ice, il, ls, ll)
 
@@ -270,7 +279,7 @@
             *tile_specs(ob, lb, 1),
         ],
         out_specs=pl.BlockSpec((ns, AB * BL), lambda i: (0, 0)),
-        compiler_params=pltpu.CompilerParams(vmem_limit_bytes=24 << 20),
+        compiler_params=pltpu.CompilerParams(vmem_limit_bytes=GRANT),
         cost_estimate=pl.CostEstimate(
             flops=2 * (ob + lb) * 2 * BL * BL * 128,
             bytes_accessed=(ob + lb) * 2 * BL * BL * 2,
@@ -281,14 +290,11 @@
 
 
 def collect_kernel(cells, neighbours, asked_ref, back_ref, *refs):
-    acc_refs, out_ref, total = refs[:-2], refs[-2], refs[-1]
+    acc_refs, out_ref, totals = refs[: -1 - CHAINS], refs[-1 - CHAINS], refs[-CHAINS:]
     cell = lax.axis_index("cell")
     half = cells // 2
-    width = out_ref.shape[1]
-    if acc_refs:
-        total[:, :width] = acc_refs[0][...]
-    else:
-        total[:, :width] = jnp.zeros((total.shape[0], width), jnp.float32)
+    for total in totals:
+        total[...] = jnp.zeros(total.shape, jnp.float32)
 
     def body(c, _):
         far_one = jnp.logical_or(c <= cell - half, c > cell + half)
@@ -296,14 +302,18 @@
         @pl.when(far_one == neighbours)
         def _():
             for r in range(CAP):
+                total = totals[r % CHAINS]
                 i = asked_ref[c, r]
-                at = lanes(jnp.where(i < 0, AB, lax.rem(i, AB)))
+                at = lanes(jnp.where(i < 0, AB, i & (AB - 1)))
                 total[:, at] = total[:, at] + back_ref[c * CAP + r].astype(jnp.float32)
 
         return 0
 
     lax.fori_loop(0, cells, body, 0)
-    out_ref[...] = total[:, :width]
+    for b in range(AB):
+        here = slice(b * BL, (b + 1) * BL)
+        parts = [ref[:, here] for ref in (*acc_refs, *totals)]
+        out_ref[:, here] = functools.reduce(jnp.add, parts)
 
 
 def collect(asked, back, acc, neighbours, cells):
@@ -314,7 +324,8 @@
         out_shape=jax.ShapeDtypeStruct((ns, AB * BL), jnp.float32),
         in_specs=[whole(SMEM), whole(), *[whole()] * len(accs)],
         out_specs=whole(),
-        scratch_shapes=[VMEM((ns, (AB + 1) * BL), jnp.float32)],
+        scratch_shapes=[VMEM((ns, (AB + 1) * BL), jnp.float32)] * CHAINS,
+        compiler_params=pltpu.CompilerParams(vmem_limit_bytes=GRANT),
         cost_estimate=pl.CostEstimate(
             flops=1 << 20, bytes_accessed=4 << 20, transcendentals=0
         ),
@@ -350,6 +361,7 @@
     )
     back = exchange(send)
     acc = near_back(ol, ll, of, lf, ocn_tiles, lnd_tiles)
+    back, acc = lax.optimization_barrier((back, acc))
     away = lax.ppermute(collect(asked, back, None, True, cells), axes, to_owner)
     own = collect(asked, back, acc, False, cells)
     return own + away, of, lf

time: 98 us -> 80.6 us (0.82)
  local copies, waits for them, and re-layouts: 17.9 us -> 2.59 us
  blocking collectives: 29.2 us -> 15.2 us
  waiting for transfers between devices: 12.9 us -> 19 us
  starting transfers between devices: 11.2 us -> 15.1 us
  Pallas kernels: 23.9 us -> 25.1 us
    unnamed x40 -> x6, local copies, waits for them, and re-layouts: 17.9 us -> 2.59 us
    all_to_all x1 -> x0, blocking collectives: 14 us -> none  [per_device(): back = exchange(send)]
    all_to_all x0 -> x1, starting transfers between devices: none -> 4.7 us  [per_device(): back = exchange(send)]
    all_to_all x0 -> x1, waiting for transfers between devices: none -> 3.92 us  [per_device(): back = exchange(send)]
    pallas_call x1, Pallas kernels: 9.8 us -> 6.42 us  [far(): pl.pallas_call(far_kernel, grid=(STEPS,), out_shape=(jax.ShapeDtypeStruct...]
    all_to_all x1, waiting for transfers between devices: 12.9 us -> 15 us  [per_device(): got = exchange(serve(asked, atm_fields, near_fields, cells))]
    pallas_call x1, Pallas kernels: 2.81 us -> 4.71 us  [near_mix(): pl.pallas_call(near_mix_kernel, grid=(STEPS,), out_shape=(jax.ShapeDtypeS...]
    pallas_call x1, Pallas kernels: 3.34 us -> 4.85 us  [near_back(): pl.pallas_call(near_back_kernel, grid=(STEPS,), out_shape=jax.ShapeDtypeS...]
  transfers between devices with their start and end apart: 3 -> 4, of which waited for: 1 -> 2; matrix products, arithmetic and copies ran while one was open for 0% -> 0% of each run, Pallas kernels for 11% -> 17%
where the time goes in v2:
time: 80.6 us; the launch traced here: 79.2 us
  Pallas kernels  25.1 us (31%)
  waiting for transfers between devices  19 us (24%)
  blocking collectives  15.2 us (19%)
  starting transfers between devices  15.1 us (19%)
  local copies, waits for them, and re-layouts  2.59 us (3%)
  other arithmetic  1.57 us (2%)
    all_to_all x1, blocking collectives, per_device(): asked = exchange(asking)  15.2 us
    all_to_all x1, waiting for transfers between devices, per_device(): got = exchange(serve(asked, atm_fields, near_fields, cells))  15 us
    pallas_call x1, Pallas kernels, far(): pl.pallas_call(far_kernel, grid=(STEPS,), out_shape=(jax.ShapeDtypeStruct...  6.42 us
    ppermute x1, starting transfers between devices, per_device(): away = lax.ppermute(collect(asked, back, None, True, cells), axes, to_owner)  5.23 us
    pallas_call x1, Pallas kernels, near_back(): pl.pallas_call(near_back_kernel, grid=(STEPS,), out_shape=jax.ShapeDtypeS...  4.85 us
    pallas_call x1, Pallas kernels, near_mix(): pl.pallas_call(near_mix_kernel, grid=(STEPS,), out_shape=(jax.ShapeDtypeS...  4.71 us
    all_to_all x1, starting transfers between devices, per_device(): back = exchange(send)  4.7 us
    pallas_call x2, Pallas kernels, collect(): pl.pallas_call(functools.partial(collect_kernel, cells, neighbours), out_...  4.52 us
  transfers between devices with their start and end apart: 4, of which 2 were waited for; matrix products, arithmetic and copies ran while one was open for 0% of the time, Pallas kernels for 17%

profile of v2, /device:TPU:1, one launch (start us, length us, event | category | flops | bytes accessed | tf_op | source)
XLA Modules:
  0.0 79.2 jit_solution(13842323474555573873)
XLA Ops:
  0.6 1.5 %collective-permute-start = (bf16[24,4096]{1,0:T(8,128)(2,1)}, bf16[24,4096]{1,0:T(8,128)(2,1)S(1)}, u32[]{:S(2)}, u32[]{:S(2)}) collective-permute-start(bf16[24,4096]{1,0:T(8,128)(2,1)} %f_ref.1), channel_id=1, source_target_pairs={{0,112},{1,113},{2,114},{3,115},{4,116},{5,117},{6,118},{7,119},{8... | collective-permute-start | bytes 589832 | tf_op jit(solution)/shard_map/ppermute | solution.py:352
  2.1 1.8 %requests.1 = (s32[16,128]{1,0:T(8,128)}, s32[8,128]{1,0:T(8,128)}) custom-call(s32[2,64]{1,0:T(2,128)} %bitcast.20, s32[2,16]{1,0:T(2,128)} %bitcast.21), custom_call_target="tpu_custom_call" | custom-call | tf_op jit(solution)/shard_map/requests/pallas_call | solution.py:77
  3.9 15.2 %all_to_all.21 = s32[16,1,128]{2,1,0:T(1,128)} all-to-all(s32[16,1,128]{2,1,0:T(1,128)} %bitcast.14), channel_id=1, replica_groups=mesh['sect'=8,'cell'=16] {'cell'}, dimensions={0} | all-to-all | bytes 16384 | tf_op jit(solution)/shard_map/all_to_all | solution.py:354
  19.2 0.0 collective-permute-done.near_ref
  19.2 0.0 copy-start.2
  19.2 0.7 copy-done.2
  19.8 2.8 %serve.1 = bf16[240,24,128]{2,1,0:T(8,128)(2,1)} custom-call(s32[16,128]{1,0:T(8,128)} %bitcast.10, bf16[24,4096]{1,0:T(8,128)(2,1)} %f_ref.1, bf16[24,4096]{1,0:T(8,128)(2,1)} %copy-done.2), custom_call_target="tpu_custom_call" | custom-call | tf_op jit(solution)/shard_map/serve/pallas_call | solution.py:106
  22.6 3.7 %all-to-all-start.1 = ((bf16[240,24,128]{2,1,0:T(8,128)(2,1)}), bf16[240,24,128]{2,1,0:T(8,128)(2,1)S(1)}, u32[]{:S(2)}, u32[]{:S(2)}) async-start(bf16[240,24,128]{2,1,0:T(8,128)(2,1)} %serve.1), calls=%async_computation.1 | async-start | bytes 2949120 | tf_op jit(solution)/shard_map/all_to_all | solution.py:355
  26.3 4.7 %near_mix.1 = (f32[64,24,128]{2,1,0:T(8,128)}, f32[16,24,128]{2,1,0:T(8,128)}) custom-call(s32[2,64]{1,0:T(2,128)} %bitcast.16, s32[2,16]{1,0:T(2,128)} %bitcast.18, bf16[24,4096]{1,0:T(8,128)(2,1)} %f_ref.1, bf16[64,4,128,128]{3,2,1,0:T(8,128)(2,1)} %ot_ref.5, bf16[16,4,128,128]{3,2,1,0:T(8,128)(2,1)} %lt_ref.5), custom_call_target="tpu_custom_call" | custom-call | flops 671088640 | bytes 5242880 | tf_op jit(solution)/shard_map/near_mix/pallas_call | solution.py:141
  31.0 15.0 %all-to-all-done.1.got_ref = bf16[240,24,128]{2,1,0:T(8,128)(2,1)S(1)} async-done(((bf16[240,24,128]{2,1,0:T(8,128)(2,1)}), bf16[240,24,128]{2,1,0:T(8,128)(2,1)S(1)}, u32[]{:S(2)}, u32[]{:S(2)}) %all-to-all-start.1) | async-done | bytes 1474592 | tf_op jit(solution)/shard_map/all_to_all | solution.py:355
  46.1 0.0 copy-start
  46.1 1.1 %copy-done = bf16[240,24,128]{2,1,0:T(8,128)(2,1)} copy-done((bf16[240,24,128]{2,1,0:T(8,128)(2,1)}, bf16[240,24,128]{2,1,0:T(8,128)(2,1)S(1)}, u32[]{:S(2)}) %copy-start) | copy-done | bytes 1474584
  47.2 6.4 %far.1 = (f32[8,8192]{1,0:T(8,128)}, f32[8,2048]{1,0:T(8,128)}, bf16[240,8,128]{2,1,0:T(8,128)(2,1)}) custom-call(s32[8,128]{1,0:T(8,128)} %get-tuple-element.13.slot_ref, bf16[240,24,128]{2,1,0:T(8,128)(2,1)} %copy-done, bf16[64,4,128,128]{3,2,1,0:T(8,128)(2,1)} %ot_ref.5, bf16[16,4,128,128]{3,2,1,0:T(8,128)(2,1)} %lt_ref.5, ...), custom_call_target="tpu_custom_call" | custom-call | tf_op jit(solution)/shard_map/far/pallas_call | solution.py:219
  53.6 4.7 %all-to-all-start.2 = ((bf16[240,8,128]{2,1,0:T(8,128)(2,1)}), bf16[240,8,128]{2,1,0:T(8,128)(2,1)S(1)}, u32[]{:S(2)}, u32[]{:S(2)}) async-start(bf16[240,8,128]{2,1,0:T(8,128)(2,1)} %get-tuple-element.16), calls=%async_computation.2 | async-start | bytes 983040 | tf_op jit(solution)/shard_map/all_to_all | solution.py:362
  58.3 4.9 %near_back.1.refs_0_ = f32[8,4096]{1,0:T(8,128)} custom-call(s32[2,64]{1,0:T(2,128)} %bitcast.17, s32[2,16]{1,0:T(2,128)} %bitcast.19, f32[8,8192]{1,0:T(8,128)} %get-tuple-element.10.of_ref, f32[8,2048]{1,0:T(8,128)} %get-tuple-element.11.lf_ref, bf16[64,4,128,128]{3,2,1,0:T(8,128)(2,1)} %ot_ref.5, bf16[16,4,128,128]{3,2,1,0:T(8,128)(2,1)} %lt_ref.5), custom_call_target="tpu_custom_call" | custom-call | flops 671088640 | bytes 5242880 | tf_op jit(solution)/shard_map/near_back/pallas_call | solution.py:270
  63.2 3.9 %all-to-all-done.2.back_ref = bf16[240,8,128]{2,1,0:T(8,128)(2,1)S(1)} async-done(((bf16[240,8,128]{2,1,0:T(8,128)(2,1)}), bf16[240,8,128]{2,1,0:T(8,128)(2,1)S(1)}, u32[]{:S(2)}, u32[]{:S(2)}) %all-to-all-start.2) | async-done | bytes 491552 | tf_op jit(solution)/shard_map/all_to_all | solution.py:362
  67.1 0.0 copy-start.1
  67.1 0.8 copy-done.1
  67.9 2.2 %collect_far.1 = f32[8,4096]{1,0:T(8,128)} custom-call(s32[16,128]{1,0:T(8,128)} %bitcast.11, bf16[240,8,128]{2,1,0:T(8,128)(2,1)} %copy-done.1), custom_call_target="tpu_custom_call" | custom-call | flops 1048576 | bytes 4194304 | tf_op jit(solution)/shard_map/collect_far/pallas_call | solution.py:322
  70.1 5.2 %collective-permute-start.1 = (f32[8,4096]{1,0:T(8,128)}, f32[8,4096]{1,0:T(8,128)S(1)}, u32[]{:S(2)}, u32[]{:S(2)}) collective-permute-start(f32[8,4096]{1,0:T(8,128)} %collect_far.1), channel_id=1, source_target_pairs={{112,0},{113,1},{114,2},{115,3},{116,4},{117,5},{118,6},{119,7},{2... | collective-permute-start | bytes 393224 | tf_op jit(solution)/shard_map/ppermute | solution.py:365
  75.3 2.3 %collect_own.1 = f32[8,4096]{1,0:T(8,128)} custom-call(s32[16,128]{1,0:T(8,128)} %bitcast.12, bf16[240,8,128]{2,1,0:T(8,128)(2,1)} %copy-done.1, f32[8,4096]{1,0:T(8,128)} %near_back.1.refs_0_), custom_call_target="tpu_custom_call" | custom-call | flops 1048576 | bytes 4194304 | tf_op jit(solution)/shard_map/collect_own/pallas_call | solution.py:322
  77.7 0.0 collective-permute-done.1
  77.7 1.6 %add.3 = f32[8,4096]{1,0:T(8,128)} add(f32[8,4096]{1,0:T(8,128)} %collect_own.1, f32[8,4096]{1,0:T(8,128)S(1)} %collective-permute-done.1) | non-fusion elementwise | flops 32768 | bytes 393216 | tf_op jit(solution)/shard_map/add | solution.py:367
Async XLA Ops:
  0.6 18.5 %collective-permute-start = (bf16[24,4096]{1,0:T(8,128)(2,1)}, bf16[24,4096]{1,0:T(8,128)(2,1)S(1)}, u32[]{:S(2)}, u32[]{:S(2)}) collective-permute-start(bf16[24,4096]{1,0:T(8,128)(2,1)} %f_ref.1), channel_id=1, source_target_pairs={{0,112},{1,113},{2,114},{3,115},{4,116},{5,117},{6,118},{7,119},{8... | collective-permute-start | bytes 589832 | tf_op jit(solution)/shard_map/ppermute | solution.py:352
  19.2 0.7 copy-start.2
  22.6 23.5 %all-to-all-start.1 = ((bf16[240,24,128]{2,1,0:T(8,128)(2,1)}), bf16[240,24,128]{2,1,0:T(8,128)(2,1)S(1)}, u32[]{:S(2)}, u32[]{:S(2)}) async-start(bf16[240,24,128]{2,1,0:T(8,128)(2,1)} %serve.1), calls=%async_computation.1 | async-start | bytes 2949120 | tf_op jit(solution)/shard_map/all_to_all | solution.py:355
  46.1 1.1 %copy-start = (bf16[240,24,128]{2,1,0:T(8,128)(2,1)}, bf16[240,24,128]{2,1,0:T(8,128)(2,1)S(1)}, u32[]{:S(2)}) copy-start(bf16[240,24,128]{2,1,0:T(8,128)(2,1)S(1)} %all-to-all-done.1.got_ref) | copy-start | bytes 4423684
  53.6 13.5 %all-to-all-start.2 = ((bf16[240,8,128]{2,1,0:T(8,128)(2,1)}), bf16[240,8,128]{2,1,0:T(8,128)(2,1)S(1)}, u32[]{:S(2)}, u32[]{:S(2)}) async-start(bf16[240,8,128]{2,1,0:T(8,128)(2,1)} %get-tuple-element.16), calls=%async_computation.2 | async-start | bytes 983040 | tf_op jit(solution)/shard_map/all_to_all | solution.py:362
  67.1 0.8 copy-start.1
  70.1 7.5 %collective-permute-start.1 = (f32[8,4096]{1,0:T(8,128)}, f32[8,4096]{1,0:T(8,128)S(1)}, u32[]{:S(2)}, u32[]{:S(2)}) collective-permute-start(f32[8,4096]{1,0:T(8,128)} %collect_far.1), channel_id=1, source_target_pairs={{112,0},{113,1},{114,2},{115,3},{116,4},{117,5},{118,6},{119,7},{2... | collective-permute-start | bytes 393224 | tf_op jit(solution)/shard_map/ppermute | solution.py:365

commit v3 on v2

--- a/solution.py
+++ b/solution.py
@@ -14,7 +14,7 @@
 BL = 128
 AB = 32
 CAP = 15
-GRANT = 60 << 20
+GRANT, LARGE, SMALL = 60 << 20, 50 << 20, 8 << 20
 CHAINS = 5
 VMEM = pltpu.VMEM
 SMEM = pltpu.SMEM
@@ -87,31 +87,59 @@
     )(om, lm)
 
 
-def serve_kernel(cells, asked_ref, own_ref, near_ref, out_ref, both):
+def hold_kernel(own_ref, near_ref, out_ref, sems):
     width = own_ref.shape[1]
-    both[:, :width] = own_ref[...]
-    both[:, width:] = near_ref[...]
+    copies = [
+        pltpu.make_async_copy(ref, out_ref.at[:, pl.ds(k * width, width)], sems.at[k])
+        for k, ref in enumerate((own_ref, near_ref))
+    ]
+    for copy in copies:
+        copy.start()
+    for copy in copies:
+        copy.wait()
+
+
+def hold(own, near):
+    return pl.pallas_call(
+        hold_kernel,
+        out_shape=jax.ShapeDtypeStruct((own.shape[0], 2 * own.shape[1]), own.dtype),
+        in_specs=[whole(pl.ANY)] * 2,
+        out_specs=whole(),
+        scratch_shapes=[pltpu.SemaphoreType.DMA((2,))],
+        compiler_params=pltpu.CompilerParams(vmem_limit_bytes=SMALL),
+        cost_estimate=pl.CostEstimate(flops=1 << 20, bytes_accessed=4 << 20, transcendentals=0),
+        name="hold",
+    )(own, near)
+
+
+def serve_kernel(cells, asked_ref, both, out_ref, made, out_sems):
+    def out(c):
+        part = pl.ds(c * CAP, CAP)
+        return pltpu.make_async_copy(made.at[part], out_ref.at[part], out_sems.at[c])
 
     def body(c, _):
         for r in range(CAP):
             i = jnp.maximum(asked_ref[c, r], 0)
-            out_ref[c * CAP + r] = both[:, lanes(i)]
+            made[c * CAP + r] = both[:, lanes(i)]
+        out(c).start()
         return 0
 
     lax.fori_loop(0, cells, body, 0)
-
-
-def serve(asked, own, near, cells):
-    fields, width = own.shape
+    for c in range(cells):
+        out(c).wait()
+
+
+def serve(asked, both, cells):
+    shape = (cells * CAP, both.shape[0], BL)
     return pl.pallas_call(
         functools.partial(serve_kernel, cells),
-        out_shape=jax.ShapeDtypeStruct((cells * CAP, fields, BL), own.dtype),
-        in_specs=[whole(SMEM), whole(), whole()],
-        out_specs=whole(),
-        scratch_shapes=[VMEM((fields, 2 * width), own.dtype)],
-        compiler_params=pltpu.CompilerParams(vmem_limit_bytes=GRANT),
+        out_shape=jax.ShapeDtypeStruct(shape, both.dtype),
+        in_specs=[whole(SMEM), whole()],
+        out_specs=whole(pltpu.HBM),
+        scratch_shapes=[VMEM(shape, both.dtype), pltpu.SemaphoreType.DMA((cells,))],
+        compiler_params=pltpu.CompilerParams(vmem_limit_bytes=SMALL),
         name="serve",
-    )(asked, own, near)
+    )(asked, both)
 
 
 STEPS = 4
@@ -124,15 +152,17 @@
     ]
 
 
-def near_mix_kernel(ol_ref, ll_ref, f_ref, ot_ref, lt_ref, om_ref, lm_ref):
+def near_mix_kernel(ol_ref, ll_ref, f_ref, ot_ref, lt_ref, out_ref):
     step = pl.program_id(0)
-    for ids, tiles, out in ((ol_ref, ot_ref, om_ref), (ll_ref, lt_ref, lm_ref)):
+    at = 0
+    for ids, tiles in ((ol_ref, ot_ref), (ll_ref, lt_ref)):
         n = tiles.shape[0]
         for b in range(n):
             src = [f_ref[:, lanes(ids[k, step * n + b])] for k in range(2)]
-            out[b] = dot(
+            out_ref[at] = dot(
                 jnp.concatenate(src, axis=1), tiles[b].reshape(2 * BL, BL), NN
             )
+            at += 1
 
 
 def near_mix(ol, ll, fields, ot, lt):
@@ -141,20 +171,14 @@
     return pl.pallas_call(
         near_mix_kernel,
         grid=(STEPS,),
-        out_shape=(
-            jax.ShapeDtypeStruct((ob, nf, BL), jnp.float32),
-            jax.ShapeDtypeStruct((lb, nf, BL), jnp.float32),
-        ),
+        out_shape=jax.ShapeDtypeStruct((ob + lb, nf, BL), jnp.float32),
         in_specs=[
             whole(SMEM),
             whole(SMEM),
             pl.BlockSpec(fields.shape, lambda i: (0, 0)),
             *tile_specs(ob, lb, 1),
         ],
-        out_specs=[
-            pl.BlockSpec((ob // STEPS, nf, BL), lambda i: (i, 0, 0)),
-            pl.BlockSpec((lb // STEPS, nf, BL), lambda i: (i, 0, 0)),
-        ],
+        out_specs=pl.BlockSpec(((ob + lb) // STEPS, nf, BL), lambda i: (i, 0, 0)),
         compiler_params=pltpu.CompilerParams(vmem_limit_bytes=GRANT),
         cost_estimate=pl.CostEstimate(
             flops=2 * (ob + lb) * 2 * BL * BL * 128,
@@ -166,85 +190,121 @@
 
 
 def far_kernel(
-    slot_ref, got_ref, ot_ref, lt_ref, om_ref, lm_ref, os_ref, is_ref, il_ref, ls_ref, ll_ref,
-    of_ref, lf_ref, send_ref, mixed,
+    slot_ref, got_hbm, ot_hbm, lt_hbm, near_hbm, os_hbm, is_hbm, il_hbm, ls_hbm, ll_hbm,
+    of_hbm, lf_hbm, send_hbm,
+    got_ref, ot, lt, near, osv, isv, il, ls, ll, of, lf, send, mixed, in_sems, out_sems,
 ):
-    step = pl.program_id(0)
-
-    @pl.when(step == 0)
-    def _():
-        send_ref[...] = jnp.zeros(send_ref.shape, send_ref.dtype)
-
+    no, nl = ot.shape[0] // STEPS, lt.shape[0] // STEPS
+
+    def ins(i):
+        o, l, n = pl.ds(i * no, no), pl.ds(i * nl, nl), pl.ds(i * (no + nl), no + nl)
+        ow = pl.ds(pl.multiple_of(i * no * BL, no * BL), no * BL)
+        lw = pl.ds(pl.multiple_of(i * nl * BL, nl * BL), nl * BL)
+        pairs = (
+            (ot_hbm.at[o, pl.ds(0, 2)], ot.at[o]),
+            (lt_hbm.at[l, pl.ds(0, 2)], lt.at[l]),
+            (near_hbm.at[n], near.at[n]),
+            (os_hbm.at[:, ow], osv.at[:, ow]),
+            (is_hbm.at[:, ow], isv.at[:, ow]),
+            (ls_hbm.at[:, lw], ls.at[:, lw]),
+        )
+        return [
+            pltpu.make_async_copy(a, b, in_sems.at[k, i]) for k, (a, b) in enumerate(pairs)
+        ]
+
+    levels = [
+        pltpu.make_async_copy(a, b, in_sems.at[6, k])
+        for k, (a, b) in enumerate(((got_hbm, got_ref), (il_hbm, il), (ll_hbm, ll)))
+    ]
+    for copy in levels:
+        copy.start()
+    for i in range(STEPS):
+        for copy in ins(i):
+            copy.start()
+    send[...] = jnp.zeros(send.shape, send.dtype)
+    for copy in levels:
+        copy.wait()
     ocean, ice, land = column(ocean_coef), column(ice_coef), column(land_coef)
-    no, nl = ot_ref.shape[0], lt_ref.shape[0]
-    blocks = []
-    for b in range(no + nl):
-        is_ocean = b < no
-        c = b if is_ocean else b - no
-        at = step * (no if is_ocean else nl) + c
-        slots = [slot_ref[(0 if is_ocean else 2) + k, at] for k in range(2)]
-        blocks.append((is_ocean, c, at, slots))
-    for b, (is_ocean, c, at, slots) in enumerate(blocks):
-        tiles, near = (ot_ref, om_ref) if is_ocean else (lt_ref, lm_ref)
-        src = jnp.concatenate([got_ref[s] for s in slots], axis=1)
-        mixed[b] = near[c] + dot(src, tiles[c].reshape(2 * BL, BL), NN)
-    for b, (is_ocean, c, at, slots) in enumerate(blocks):
-        u = mixed[b, pl.ds(0, 8, stride=3), :]
-        v = mixed[b, pl.ds(1, 8, stride=3), :]
-        t = mixed[b, pl.ds(2, 8, stride=3), :]
-        wind = jnp.sqrt(1.0 + u * u + v * v)
-        here = slice(c * BL, (c + 1) * BL)
-        if is_ocean:
-            frac = il_ref[c : c + 1, :].astype(jnp.float32) / 8.0
-            flux = (1.0 - frac) * (ocean * wind * (t - os_ref[:, here]))
-            flux = flux + frac * (ice * wind * (t - is_ref[:, here]))
-            of_ref[:, here] = flux
-        else:
-            frac = ll_ref[pl.ds(at, 1), :].astype(jnp.float32) / 8.0
-            flux = frac * (land * wind * (t - ls_ref[:, here]))
-            lf_ref[:, here] = flux
-    for b, (is_ocean, c, at, slots) in enumerate(blocks):
-        tiles, flux = (ot_ref, of_ref) if is_ocean else (lt_ref, lf_ref)
-        here = slice(c * BL, (c + 1) * BL)
-        terms = dot(flux[:, here].astype(jnp.bfloat16), tiles[c].reshape(2 * BL, BL), NT)
-        terms = terms.astype(send_ref.dtype)
-        for k in range(2):
-            send_ref[slots[k]] = terms[:, k * BL : (k + 1) * BL]
-
-
-def far(slots, got, ot, lt, om, lm, os, ice, il, ls, ll):
+
+    def body(step, _):
+        for copy in ins(step):
+            copy.wait()
+        blocks = []
+        for b in range(no + nl):
+            is_ocean = b < no
+            at = step * no + b if is_ocean else step * nl + b - no
+            slots = [slot_ref[(0 if is_ocean else 2) + k, at] for k in range(2)]
+            blocks.append((is_ocean, at, slots))
+        for b, (is_ocean, at, slots) in enumerate(blocks):
+            tiles = ot if is_ocean else lt
+            src = jnp.concatenate([got_ref[s] for s in slots], axis=1)
+            mixed[b] = near[step * (no + nl) + b] + dot(src, tiles[at].reshape(2 * BL, BL), NN)
+        for b, (is_ocean, at, slots) in enumerate(blocks):
+            u = mixed[b, pl.ds(0, 8, stride=3), :]
+            v = mixed[b, pl.ds(1, 8, stride=3), :]
+            t = mixed[b, pl.ds(2, 8, stride=3), :]
+            wind = jnp.sqrt(1.0 + u * u + v * v)
+            here = lanes(at)
+            if is_ocean:
+                frac = il[pl.ds(at, 1), :].astype(jnp.float32) / 8.0
+                flux = (1.0 - frac) * (ocean * wind * (t - osv[:, here]))
+                of[:, here] = flux + frac * (ice * wind * (t - isv[:, here]))
+            else:
+                frac = ll[pl.ds(at, 1), :].astype(jnp.float32) / 8.0
+                lf[:, here] = frac * (land * wind * (t - ls[:, here]))
+        for b, (is_ocean, at, slots) in enumerate(blocks):
+            tiles, flux = (ot, of) if is_ocean else (lt, lf)
+            g = flux[:, lanes(at)].astype(jnp.bfloat16)
+            terms = dot(g, tiles[at].reshape(2 * BL, BL), NT).astype(send.dtype)
+            for k in range(2):
+                send[slots[k]] = terms[:, k * BL : (k + 1) * BL]
+        return 0
+
+    lax.fori_loop(0, STEPS, body, 0)
+    outs = [
+        pltpu.make_async_copy(a, b, out_sems.at[k])
+        for k, (a, b) in enumerate(((send, send_hbm), (of, of_hbm), (lf, lf_hbm)))
+    ]
+    for copy in outs:
+        copy.start()
+    for copy in outs:
+        copy.wait()
+
+
+def far(slots, got, ot, lt, near, os, ice, il, ls, ll):
     ob, lb = ot.shape[0], lt.shape[0]
-    nf, ns = om.shape[1], os.shape[0]
-    no, nl = ob // STEPS, lb // STEPS
+    nf, ns = near.shape[1], os.shape[0]
+    f32 = jnp.float32
+    back = (got.shape[0], ns, BL)
     return pl.pallas_call(
         far_kernel,
-        grid=(STEPS,),
         out_shape=(
-            jax.ShapeDtypeStruct(os.shape, jnp.float32),
-            jax.ShapeDtypeStruct(ls.shape, jnp.float32),
-            jax.ShapeDtypeStruct((got.shape[0], ns, BL), jnp.bfloat16),
+            jax.ShapeDtypeStruct(os.shape, f32),
+            jax.ShapeDtypeStruct(ls.shape, f32),
+            jax.ShapeDtypeStruct(back, jnp.bfloat16),
         ),
-        in_specs=[
-            whole(SMEM),
-            pl.BlockSpec(got.shape, lambda i: (0, 0, 0)),
-            *tile_specs(ob, lb, 0),
-            pl.BlockSpec((no, nf, BL), lambda i: (i, 0, 0)),
-            pl.BlockSpec((nl, nf, BL), lambda i: (i, 0, 0)),
-            pl.BlockSpec((ns, no * BL), lambda i: (0, i)),
-            pl.BlockSpec((ns, no * BL), lambda i: (0, i)),
-            pl.BlockSpec((no, BL), lambda i: (i, 0)),
-            pl.BlockSpec((ns, nl * BL), lambda i: (0, i)),
-            pl.BlockSpec((lb, BL), lambda i: (0, 0)),
+        in_specs=[whole(SMEM), *[whole(pl.ANY)] * 9],
+        out_specs=[whole(pltpu.HBM)] * 3,
+        scratch_shapes=[
+            VMEM(got.shape, got.dtype),
+            VMEM((ob, 2, BL, BL), ot.dtype),
+            VMEM((lb, 2, BL, BL), lt.dtype),
+            VMEM(near.shape, f32),
+            VMEM(os.shape, f32),
+            VMEM(ice.shape, f32),
+            VMEM(il.shape, il.dtype),
+            VMEM(ls.shape, f32),
+            VMEM(ll.shape, ll.dtype),
+            VMEM(os.shape, f32),
+            VMEM(ls.shape, f32),
+            VMEM(back, jnp.bfloat16),
+            VMEM(((ob + lb) // STEPS, nf, BL), f32),
+            pltpu.SemaphoreType.DMA((7, STEPS)),
+            pltpu.SemaphoreType.DMA((3,)),
         ],
-        out_specs=[
-            pl.BlockSpec((ns, no * BL), lambda i: (0, i)),
-            pl.BlockSpec((ns, nl * BL), lambda i: (0, i)),
-            pl.BlockSpec((got.shape[0], ns, BL), lambda i: (0, 0, 0)),
-        ],
-        scratch_shapes=[VMEM((no + nl, nf, BL), jnp.float32)],
-        compiler_params=pltpu.CompilerParams(vmem_limit_bytes=GRANT),
+        compiler_params=pltpu.CompilerParams(vmem_limit_bytes=LARGE),
         name="far",
-    )(slots, got, ot, lt, om, lm, os, ice, il, ls, ll)
+    )(slots, got, ot, lt, near, os, ice, il, ls, ll)
 
 
 def near_back_kernel(ol_ref, ll_ref, of_ref, lf_ref, ot_ref, lt_ref, out_ref):
@@ -290,10 +350,16 @@
 
 
 def collect_kernel(cells, neighbours, asked_ref, back_ref, *refs):
-    acc_refs, out_ref, totals = refs[: -1 - CHAINS], refs[-1 - CHAINS], refs[-CHAINS:]
+    if neighbours:
+        out_ref, *totals = refs
+    else:
+        acc_ref, out_ref, acc, sem, *totals = refs
+        load = pltpu.make_async_copy(acc_ref, acc, sem)
+        load.start()
+        totals = [acc, *totals]
     cell = lax.axis_index("cell")
     half = cells // 2
-    for total in totals:
+    for total in totals[-CHAINS:]:
         total[...] = jnp.zeros(total.shape, jnp.float32)
 
     def body(c, _):
@@ -302,7 +368,7 @@
         @pl.when(far_one == neighbours)
         def _():
             for r in range(CAP):
-                total = totals[r % CHAINS]
+                total = totals[r % CHAINS - CHAINS]
                 i = asked_ref[c, r]
                 at = lanes(jnp.where(i < 0, AB, i & (AB - 1)))
                 total[:, at] = total[:, at] + back_ref[c * CAP + r].astype(jnp.float32)
@@ -310,22 +376,26 @@
         return 0
 
     lax.fori_loop(0, cells, body, 0)
+    if not neighbours:
+        load.wait()
     for b in range(AB):
         here = slice(b * BL, (b + 1) * BL)
-        parts = [ref[:, here] for ref in (*acc_refs, *totals)]
-        out_ref[:, here] = functools.reduce(jnp.add, parts)
+        out_ref[:, here] = functools.reduce(jnp.add, [ref[:, here] for ref in totals])
 
 
 def collect(asked, back, acc, neighbours, cells):
     ns = back.shape[1]
-    accs = () if acc is None else (acc,)
+    shape = (ns, AB * BL)
+    accs, more = (), []
+    if acc is not None:
+        accs, more = (acc,), [VMEM(shape, jnp.float32), pltpu.SemaphoreType.DMA(())]
     return pl.pallas_call(
         functools.partial(collect_kernel, cells, neighbours),
-        out_shape=jax.ShapeDtypeStruct((ns, AB * BL), jnp.float32),
-        in_specs=[whole(SMEM), whole(), *[whole()] * len(accs)],
+        out_shape=jax.ShapeDtypeStruct(shape, jnp.float32),
+        in_specs=[whole(SMEM), whole(), *[whole(pltpu.HBM)] * len(accs)],
         out_specs=whole(),
-        scratch_shapes=[VMEM((ns, (AB + 1) * BL), jnp.float32)] * CHAINS,
-        compiler_params=pltpu.CompilerParams(vmem_limit_bytes=GRANT),
+        scratch_shapes=[*more, *[VMEM((ns, (AB + 1) * BL), jnp.float32)] * CHAINS],
+        compiler_params=pltpu.CompilerParams(vmem_limit_bytes=SMALL),
         cost_estimate=pl.CostEstimate(
             flops=1 << 20, bytes_accessed=4 << 20, transcendentals=0
         ),
@@ -352,11 +422,11 @@
     near_fields = lax.ppermute(atm_fields, axes, to_server)
     asking, slots = requests(ocn_map.T, lnd_map.T, cells)
     asked = exchange(asking)
-    got = exchange(serve(asked, atm_fields, near_fields, cells))
+    got = exchange(serve(asked, hold(atm_fields, near_fields), cells))
     ol, ll = ocn_local.T, lnd_local.T
-    om, lm = near_mix(ol, ll, atm_fields, ocn_tiles, lnd_tiles)
+    near = near_mix(ol, ll, atm_fields, ocn_tiles, lnd_tiles)
     of, lf, send = far(
-        slots, got, ocn_tiles, lnd_tiles, om, lm, ocn_state, ice_state,
+        slots, got, ocn_tiles, lnd_tiles, near, ocn_state, ice_state,
         ice_level.reshape(-1, BL), lnd_state, lnd_level.reshape(-1, BL),
     )
     back = exchange(send)

time: 80.6 us -> 77.6 us (0.963); the launches traced: 79.2 us -> 77.1 us
  blocking collectives: 15.2 us -> 0 us
  starting transfers between devices: 15.1 us -> 24.7 us
  waiting for transfers between devices: 19 us -> 24.2 us
  Pallas kernels: 25.1 us -> 23.6 us
  other arithmetic: 1.57 us -> 0.67 us
    all_to_all x1 -> x0, blocking collectives: 15.2 us -> none  [per_device(): asked = exchange(asking)]
    all_to_all x1 -> x2, starting transfers between devices: 3.7 us -> 12.7 us  [the longest x1 8.95 us: per_device(): asked = exchange(asking)]
    all_to_all x1 -> x2, waiting for transfers between devices: 15 us -> 20.1 us  [the longest x1 14.9 us: per_device(): got = exchange(serve(asked, hold(atm_fields, near_fields), cells))]
    pallas_call x2, Pallas kernels: 4.52 us -> 2.62 us  [collect(): pl.pallas_call(functools.partial(collect_kernel, cells, neighbours), out_...]
    pallas_call x2 -> x3, Pallas kernels: 11.1 us -> 12.3 us  [the longest x1 7.28 us: far(): pl.pallas_call(far_kernel, out_shape=(jax.ShapeDtypeStruct(os.shape, f32)...]
    add x1, other arithmetic: 1.57 us -> 0.67 us  [per_device(): return (own + away, of, lf)]
    unnamed x6 -> x18, local copies, waits for them, and re-layouts: 2.59 us -> 3.06 us
  transfers between devices with their start and end apart: 4 -> 5, of which waited for: 2 -> 3; matrix products, arithmetic and copies ran while one was open for 0% -> 0% of each run, Pallas kernels for 17% -> 17%
where the time goes in v3:
time: 77.6 us; the launch traced here: 77.1 us
  starting transfers between devices  24.7 us (32%)
  waiting for transfers between devices  24.2 us (31%)
  Pallas kernels  23.6 us (30%)
  local copies, waits for them, and re-layouts  3.06 us (4%)
  between operations  0.81 us (1%)
    all_to_all x1, waiting for transfers between devices, per_device(): got = exchange(serve(asked, hold(atm_fields, near_fields), cells))  14.9 us
    all_to_all x1, starting transfers between devices, per_device(): asked = exchange(asking)  8.95 us
    pallas_call x1, Pallas kernels, far(): pl.pallas_call(far_kernel, out_shape=(jax.ShapeDtypeStruct(os.shape, f32)...  7.28 us
    ppermute x1, starting transfers between devices, per_device(): away = lax.ppermute(collect(asked, back, None, True, cells), axes, to_owner)  5.48 us
    all_to_all x1, waiting for transfers between devices, per_device(): asked = exchange(asking)  5.21 us
    all_to_all x1, starting transfers between devices, per_device(): back = exchange(send)  5.08 us
    pallas_call x1, Pallas kernels, near_back(): pl.pallas_call(near_back_kernel, grid=(STEPS,), out_shape=jax.ShapeDtypeS...  4.86 us
    pallas_call x1, Pallas kernels, near_mix(): pl.pallas_call(near_mix_kernel, grid=(STEPS,), out_shape=jax.ShapeDtypeSt...  4.82 us
  transfers between devices with their start and end apart: 5, of which 3 were waited for; matrix products, arithmetic and copies ran while one was open for 0% of the time, Pallas kernels for 17%

profile of v3, /device:TPU:1, one launch (start us, length us, event | category | flops | bytes accessed | tf_op | source)
XLA Modules:
  0.0 77.1 jit_solution(15306209074583498763)
XLA Ops:
  0.6 1.5 %collective-permute-start = (bf16[24,4096]{1,0:T(8,128)(2,1)}, bf16[24,4096]{1,0:T(8,128)(2,1)S(1)}, u32[]{:S(2)}, u32[]{:S(2)}) collective-permute-start(bf16[24,4096]{1,0:T(8,128)(2,1)} %f_ref.1), channel_id=1, source_target_pairs={{0,112},{1,113},{2,114},{3,115},{4,116},{5,117},{6,118},{7,119},{8... | collective-permute-start | bytes 589832 | tf_op jit(solution)/shard_map/ppermute | solution.py:422
  2.1 1.8 %requests.1 = (s32[16,128]{1,0:T(8,128)}, s32[8,128]{1,0:T(8,128)}) custom-call(s32[2,64]{1,0:T(2,128)} %bitcast.20, s32[2,16]{1,0:T(2,128)} %bitcast.21), custom_call_target="tpu_custom_call" | custom-call | tf_op jit(solution)/shard_map/requests/pallas_call | solution.py:77
  3.9 8.9 %all-to-all-start = ((s32[16,1,128]{2,1,0:T(1,128)}), s32[16,1,128]{2,1,0:T(1,128)S(1)}, u32[]{:S(2)}, u32[]{:S(2)}) async-start(s32[16,1,128]{2,1,0:T(1,128)} %bitcast.15), calls=%async_computation | async-start | bytes 16384 | tf_op jit(solution)/shard_map/all_to_all | solution.py:424
  12.9 0.0 collective-permute-done.near_ref
  12.9 0.0 copy-start.1
  12.9 0.9 %copy-done.1 = bf16[24,4096]{1,0:T(8,128)(2,1)S(1)} copy-done((bf16[24,4096]{1,0:T(8,128)(2,1)S(1)}, bf16[24,4096]{1,0:T(8,128)(2,1)}, u32[]{:S(2)}) %copy-start.1) | copy-done | bytes 196632
  13.8 0.2 hold.1.both
  14.0 5.2 %all-to-all-done = s32[16,1,128]{2,1,0:T(1,128)S(1)} async-done(((s32[16,1,128]{2,1,0:T(1,128)}), s32[16,1,128]{2,1,0:T(1,128)S(1)}, u32[]{:S(2)}, u32[]{:S(2)}) %all-to-all-start) | async-done | bytes 8224 | tf_op jit(solution)/shard_map/all_to_all | solution.py:424
  19.2 2.1 %serve.1 = bf16[240,24,128]{2,1,0:T(8,128)(2,1)} custom-call(s32[16,128]{1,0:T(8,128)S(1)} %bitcast.10, bf16[24,8192]{1,0:T(8,128)(2,1)S(1)} %hold.1.both), custom_call_target="tpu_custom_call" | custom-call | tf_op jit(solution)/shard_map/serve/pallas_call | solution.py:134
  21.3 3.7 %all-to-all-start.1 = ((bf16[240,24,128]{2,1,0:T(8,128)(2,1)}), bf16[240,24,128]{2,1,0:T(8,128)(2,1)S(1)}, u32[]{:S(2)}, u32[]{:S(2)}) async-start(bf16[240,24,128]{2,1,0:T(8,128)(2,1)} %serve.1), calls=%async_computation.1 | async-start | bytes 2949120 | tf_op jit(solution)/shard_map/all_to_all | solution.py:425
  25.0 0.0 copy-start.3
  25.0 0.0 copy-start.4
  25.0 0.0 copy-start.5
  25.0 0.0 copy-start.6
  25.1 0.0 copy-start.7
  25.1 0.0 copy-start.8
  25.1 4.8 %near_mix.1.near_hbm = f32[80,24,128]{2,1,0:T(8,128)} custom-call(s32[2,64]{1,0:T(2,128)} %bitcast.16, s32[2,16]{1,0:T(2,128)} %bitcast.18, bf16[24,4096]{1,0:T(8,128)(2,1)} %f_ref.1, bf16[64,4,128,128]{3,2,1,0:T(8,128)(2,1)} %ot_ref.3, bf16[16,4,128,128]{3,2,1,0:T(8,128)(2,1)} %lt_ref.3), custom_call_target="tpu_custom_call" | custom-call | flops 671088640 | bytes 5242880 | tf_op jit(solution)/shard_map/near_mix/pallas_call | solution.py:171
  29.9 14.9 %all-to-all-done.1.got_hbm = bf16[240,24,128]{2,1,0:T(8,128)(2,1)S(1)} async-done(((bf16[240,24,128]{2,1,0:T(8,128)(2,1)}), bf16[240,24,128]{2,1,0:T(8,128)(2,1)S(1)}, u32[]{:S(2)}, u32[]{:S(2)}) %all-to-all-start.1) | async-done | bytes 1474592 | tf_op jit(solution)/shard_map/all_to_all | solution.py:425
  44.8 0.0 copy-done.3
  44.8 0.0 copy-done.4
  44.8 0.0 copy-done.5
  44.8 0.0 copy-done.6
  44.8 0.0 copy-done.7
  44.8 0.0 copy-done.8
  44.8 0.0 copy-start
  44.8 1.2 %copy-done = f32[80,24,128]{2,1,0:T(8,128)S(1)} copy-done((f32[80,24,128]{2,1,0:T(8,128)S(1)}, f32[80,24,128]{2,1,0:T(8,128)}, u32[]{:S(2)}) %copy-start) | copy-done | bytes 983064
  46.0 7.3 %far.1 = (f32[8,8192]{1,0:T(8,128)}, f32[8,2048]{1,0:T(8,128)}, bf16[240,8,128]{2,1,0:T(8,128)(2,1)}) custom-call(s32[8,128]{1,0:T(8,128)S(1)} %copy-done.8, bf16[240,24,128]{2,1,0:T(8,128)(2,1)S(1)} %all-to-all-done.1.got_hbm, bf16[64,4,128,128]{3,2,1,0:T(8,128)(2,1)} %ot_ref.3, bf16[16,4,128,128]{3,2,1,0:T(8,128)(2,1)} %lt_ref.3, ...), custom_call_target="tpu_custom_call" | custom-call | tf_op jit(solution)/shard_map/far/pallas_call | solution.py:279
  53.3 5.1 %all-to-all-start.2 = ((bf16[240,8,128]{2,1,0:T(8,128)(2,1)}), bf16[240,8,128]{2,1,0:T(8,128)(2,1)S(1)}, u32[]{:S(2)}, u32[]{:S(2)}) async-start(bf16[240,8,128]{2,1,0:T(8,128)(2,1)} %get-tuple-element.12), calls=%async_computation.2 | async-start | bytes 983040 | tf_op jit(solution)/shard_map/all_to_all | solution.py:432
  58.4 4.9 %near_back.1.refs_0_ = f32[8,4096]{1,0:T(8,128)} custom-call(s32[2,64]{1,0:T(2,128)} %bitcast.17, s32[2,16]{1,0:T(2,128)} %bitcast.19, f32[8,8192]{1,0:T(8,128)} %get-tuple-element.8.of_ref, f32[8,2048]{1,0:T(8,128)} %get-tuple-element.9.lf_ref, bf16[64,4,128,128]{3,2,1,0:T(8,128)(2,1)} %ot_ref.3, bf16[16,4,128,128]{3,2,1,0:T(8,128)(2,1)} %lt_ref.3), custom_call_target="tpu_custom_call" | custom-call | flops 671088640 | bytes 5242880 | tf_op jit(solution)/shard_map/near_back/pallas_call | solution.py:330
  63.2 4.1 %all-to-all-done.2.back_ref = bf16[240,8,128]{2,1,0:T(8,128)(2,1)S(1)} async-done(((bf16[240,8,128]{2,1,0:T(8,128)(2,1)}), bf16[240,8,128]{2,1,0:T(8,128)(2,1)S(1)}, u32[]{:S(2)}, u32[]{:S(2)}) %all-to-all-start.2) | async-done | bytes 491552 | tf_op jit(solution)/shard_map/all_to_all | solution.py:432
  67.4 1.2 %collect_far.1 = f32[8,4096]{1,0:T(8,128)S(1)} custom-call(s32[16,128]{1,0:T(8,128)S(1)} %bitcast.11, bf16[240,8,128]{2,1,0:T(8,128)(2,1)S(1)} %all-to-all-done.2.back_ref), custom_call_target="tpu_custom_call" | custom-call | flops 1048576 | bytes 4194304 | tf_op jit(solution)/shard_map/collect_far/pallas_call | solution.py:392
  68.6 5.5 %collective-permute-start.1 = (f32[8,4096]{1,0:T(8,128)S(1)}, f32[8,4096]{1,0:T(8,128)S(1)}, u32[]{:S(2)}, u32[]{:S(2)}) collective-permute-start(f32[8,4096]{1,0:T(8,128)S(1)} %collect_far.1), channel_id=1, source_target_pairs={{112,0},{113,1},{114,2},{115,3},{116,4},{117,5},{118,6},{119,7},{2... | collective-permute-start | bytes 393224 | tf_op jit(solution)/shard_map/ppermute | solution.py:435
  74.0 0.0 copy-start.2
  74.0 0.9 %copy-done.2 = f32[8,4096]{1,0:T(8,128)S(1)} copy-done((f32[8,4096]{1,0:T(8,128)S(1)}, f32[8,4096]{1,0:T(8,128)}, u32[]{:S(2)}) %copy-start.2) | copy-done | bytes 131096
  74.9 1.4 %collect_own.1 = f32[8,4096]{1,0:T(8,128)S(1)} custom-call(s32[16,128]{1,0:T(8,128)S(1)} %bitcast.12, bf16[240,8,128]{2,1,0:T(8,128)(2,1)S(1)} %all-to-all-done.2.back_ref, f32[8,4096]{1,0:T(8,128)S(1)} %copy-done.2), custom_call_target="tpu_custom_call" | custom-call | flops 1048576 | bytes 4194304 | tf_op jit(solution)/shard_map/collect_own/pallas_call | solution.py:392
  76.4 0.0 collective-permute-done.1
  76.4 0.7 add.3
Async XLA Ops:
  0.6 12.2 %collective-permute-start = (bf16[24,4096]{1,0:T(8,128)(2,1)}, bf16[24,4096]{1,0:T(8,128)(2,1)S(1)}, u32[]{:S(2)}, u32[]{:S(2)}) collective-permute-start(bf16[24,4096]{1,0:T(8,128)(2,1)} %f_ref.1), channel_id=1, source_target_pairs={{0,112},{1,113},{2,114},{3,115},{4,116},{5,117},{6,118},{7,119},{8... | collective-permute-start | bytes 589832 | tf_op jit(solution)/shard_map/ppermute | solution.py:422
  3.9 15.3 %all-to-all-start = ((s32[16,1,128]{2,1,0:T(1,128)}), s32[16,1,128]{2,1,0:T(1,128)S(1)}, u32[]{:S(2)}, u32[]{:S(2)}) async-start(s32[16,1,128]{2,1,0:T(1,128)} %bitcast.15), calls=%async_computation | async-start | bytes 16384 | tf_op jit(solution)/shard_map/all_to_all | solution.py:424
  12.9 0.9 %copy-start.1 = (bf16[24,4096]{1,0:T(8,128)(2,1)S(1)}, bf16[24,4096]{1,0:T(8,128)(2,1)}, u32[]{:S(2)}) copy-start(bf16[24,4096]{1,0:T(8,128)(2,1)} %f_ref.1) | copy-start | bytes 589828
  21.3 23.5 %all-to-all-start.1 = ((bf16[240,24,128]{2,1,0:T(8,128)(2,1)}), bf16[240,24,128]{2,1,0:T(8,128)(2,1)S(1)}, u32[]{:S(2)}, u32[]{:S(2)}) async-start(bf16[240,24,128]{2,1,0:T(8,128)(2,1)} %serve.1), calls=%async_computation.1 | async-start | bytes 2949120 | tf_op jit(solution)/shard_map/all_to_all | solution.py:425
  25.0 19.8 %copy-start.3 = (f32[8,8192]{1,0:T(8,128)S(1)}, f32[8,8192]{1,0:T(8,128)}, u32[]{:S(2)}) copy-start(f32[8,8192]{1,0:T(8,128)} %os_hbm.1) | copy-start | bytes 786436
  25.0 19.7 %copy-start.4 = (f32[8,8192]{1,0:T(8,128)S(1)}, f32[8,8192]{1,0:T(8,128)}, u32[]{:S(2)}) copy-start(f32[8,8192]{1,0:T(8,128)} %is_hbm.1) | copy-start | bytes 786436
  25.0 19.7 %copy-start.5 = (f32[8,2048]{1,0:T(8,128)S(1)}, f32[8,2048]{1,0:T(8,128)}, u32[]{:S(2)}) copy-start(f32[8,2048]{1,0:T(8,128)} %ls_hbm.1) | copy-start | bytes 196612
  25.0 19.7 %copy-start.6 = (s32[8192]{0:T(1024)S(1)}, s32[8192]{0:T(1024)}, u32[]{:S(2)}) copy-start(s32[8192]{0:T(1024)} %param.15) | copy-start | bytes 98308
  25.1 19.7 %copy-start.7 = (s32[2048]{0:T(1024)S(1)}, s32[2048]{0:T(1024)}, u32[]{:S(2)}) copy-start(s32[2048]{0:T(1024)} %param.17) | copy-start | bytes 24580
  25.1 19.7 %copy-start.8 = (s32[8,128]{1,0:T(8,128)S(1)}, s32[8,128]{1,0:T(8,128)}, u32[]{:S(2)}) copy-start(s32[8,128]{1,0:T(8,128)} %get-tuple-element.11.slot_ref) | copy-start | bytes 12292
  44.8 1.2 %copy-start = (f32[80,24,128]{2,1,0:T(8,128)S(1)}, f32[80,24,128]{2,1,0:T(8,128)}, u32[]{:S(2)}) copy-start(f32[80,24,128]{2,1,0:T(8,128)} %near_mix.1.near_hbm) | copy-start | bytes 2949124
  53.3 14.1 %all-to-all-start.2 = ((bf16[240,8,128]{2,1,0:T(8,128)(2,1)}), bf16[240,8,128]{2,1,0:T(8,128)(2,1)S(1)}, u32[]{:S(2)}, u32[]{:S(2)}) async-start(bf16[240,8,128]{2,1,0:T(8,128)(2,1)} %get-tuple-element.12), calls=%async_computation.2 | async-start | bytes 983040 | tf_op jit(solution)/shard_map/all_to_all | solution.py:432
  68.6 7.8 %collective-permute-start.1 = (f32[8,4096]{1,0:T(8,128)S(1)}, f32[8,4096]{1,0:T(8,128)S(1)}, u32[]{:S(2)}, u32[]{:S(2)}) collective-permute-start(f32[8,4096]{1,0:T(8,128)S(1)} %collect_far.1), channel_id=1, source_target_pairs={{112,0},{113,1},{114,2},{115,3},{116,4},{117,5},{118,6},{119,7},{2... | collective-permute-start | bytes 393224 | tf_op jit(solution)/shard_map/ppermute | solution.py:435
  74.0 0.9 %copy-start.2 = (f32[8,4096]{1,0:T(8,128)S(1)}, f32[8,4096]{1,0:T(8,128)}, u32[]{:S(2)}) copy-start(f32[8,4096]{1,0:T(8,128)} %near_back.1.refs_0_) | copy-start | bytes 393220

commit v4 on v3

--- a/solution.py
+++ b/solution.py
@@ -13,6 +13,7 @@
 
 BL = 128
 AB = 32
+KR = KL = 2
 CAP = 15
 GRANT, LARGE, SMALL = 60 << 20, 50 << 20, 8 << 20
 CHAINS = 5
@@ -34,12 +35,12 @@
     return pl.BlockSpec(memory_space=space)
 
 
-def column(values):
+def column(values, width):
     row = lax.broadcasted_iota(jnp.int32, (8, BL), 0)
     out = jnp.full((8, BL), values[7], jnp.float32)
     for j in range(7):
         out = jnp.where(row == j, values[j], out)
-    return out
+    return jnp.concatenate([out] * (width // BL), axis=1)
 
 
 def request_kernel(cells, om_ref, lm_ref, req_ref, slot_ref):
@@ -87,25 +88,23 @@
     )(om, lm)
 
 
-def hold_kernel(own_ref, near_ref, out_ref, sems):
-    width = own_ref.shape[1]
-    copies = [
-        pltpu.make_async_copy(ref, out_ref.at[:, pl.ds(k * width, width)], sems.at[k])
-        for k, ref in enumerate((own_ref, near_ref))
-    ]
-    for copy in copies:
-        copy.start()
-    for copy in copies:
-        copy.wait()
+def hold_kernel(own_ref, near_ref, out_ref):
+    nf, width = own_ref.shape
+    rows = lax.broadcasted_iota(jnp.int32, (nf, nf), 0)
+    pick = 3 * (rows % 8) + rows // 8 == lax.broadcasted_iota(jnp.int32, (nf, nf), 1)
+    pick = jnp.where(pick, 1.0, 0.0).astype(own_ref.dtype)
+    for k, ref in enumerate((own_ref, near_ref)):
+        for at in range(0, width, 8 * BL):
+            part = dot(pick, ref[:, at : at + 8 * BL], NN)
+            out_ref[:, k * width + at : k * width + at + 8 * BL] = part.astype(out_ref.dtype)
 
 
 def hold(own, near):
     return pl.pallas_call(
         hold_kernel,
         out_shape=jax.ShapeDtypeStruct((own.shape[0], 2 * own.shape[1]), own.dtype),
-        in_specs=[whole(pl.ANY)] * 2,
+        in_specs=[whole()] * 2,
         out_specs=whole(),
-        scratch_shapes=[pltpu.SemaphoreType.DMA((2,))],
         compiler_params=pltpu.CompilerParams(vmem_limit_bytes=SMALL),
         cost_estimate=pl.CostEstimate(flops=1 << 20, bytes_accessed=4 << 20, transcendentals=0),
         name="hold",
@@ -143,6 +142,7 @@
 
 
 STEPS = 4
+OPARTS, LPARTS = (0, 2, 6, 11, 16), (0, 16)
 
 
 def tile_specs(ob, lb, half):
@@ -179,7 +179,7 @@
             *tile_specs(ob, lb, 1),
         ],
         out_specs=pl.BlockSpec(((ob + lb) // STEPS, nf, BL), lambda i: (i, 0, 0)),
-        compiler_params=pltpu.CompilerParams(vmem_limit_bytes=GRANT),
+        compiler_params=pltpu.CompilerParams(vmem_limit_bytes=52 << 20),
         cost_estimate=pl.CostEstimate(
             flops=2 * (ob + lb) * 2 * BL * BL * 128,
             bytes_accessed=(ob + lb) * 2 * BL * BL * 2,
@@ -189,93 +189,81 @@
     )(ol, ll, fields, ot, lt)
 
 
+def portions(count, parts):
+    cuts = [count * p // 16 for p in parts]
+    return list(zip(cuts[:-1], cuts[1:]))
+
+
 def far_kernel(
-    slot_ref, got_hbm, ot_hbm, lt_hbm, near_hbm, os_hbm, is_hbm, il_hbm, ls_hbm, ll_hbm,
-    of_hbm, lf_hbm, send_hbm,
-    got_ref, ot, lt, near, osv, isv, il, ls, ll, of, lf, send, mixed, in_sems, out_sems,
+    slot_ref, got_ref, near, osv, isv, il, ls, ll, ot_hbm, lt_hbm, of_hbm, lf_hbm, send_hbm,
+    ot, lt, of, lf, send, in_sems, out_sems,
 ):
-    no, nl = ot.shape[0] // STEPS, lt.shape[0] // STEPS
-
-    def ins(i):
-        o, l, n = pl.ds(i * no, no), pl.ds(i * nl, nl), pl.ds(i * (no + nl), no + nl)
-        ow = pl.ds(pl.multiple_of(i * no * BL, no * BL), no * BL)
-        lw = pl.ds(pl.multiple_of(i * nl * BL, nl * BL), nl * BL)
-        pairs = (
-            (ot_hbm.at[o, pl.ds(0, 2)], ot.at[o]),
-            (lt_hbm.at[l, pl.ds(0, 2)], lt.at[l]),
-            (near_hbm.at[n], near.at[n]),
-            (os_hbm.at[:, ow], osv.at[:, ow]),
-            (is_hbm.at[:, ow], isv.at[:, ow]),
-            (ls_hbm.at[:, lw], ls.at[:, lw]),
+    ob, lb = ot.shape[0], lt.shape[0]
+    parts = [(0, *p) for p in portions(ob, OPARTS)] + [(1, *p) for p in portions(lb, LPARTS)]
+    ins, outs = [], []
+    for i, (kind, lo, hi) in enumerate(parts):
+        hbm, on_chip = (lt_hbm, lt) if kind else (ot_hbm, ot)
+        some = pl.ds(lo, hi - lo)
+        copy = pltpu.make_async_copy(
+            hbm.at[some, pl.ds(0, KR)], on_chip.at[some], in_sems.at[i]
         )
-        return [
-            pltpu.make_async_copy(a, b, in_sems.at[k, i]) for k, (a, b) in enumerate(pairs)
+        copy.start()
+        ins.append(copy)
+        flux, flux_hbm = (lf, lf_hbm) if kind else (of, of_hbm)
+        some = pl.ds(lo * BL, (hi - lo) * BL)
+        outs.append(
+            pltpu.make_async_copy(flux.at[:, some], flux_hbm.at[:, some], out_sems.at[i])
+        )
+    send[...] = jnp.zeros(send.shape, send.dtype)
+    for i, (kind, lo, hi) in enumerate(parts):
+        ins[i].wait()
+        few, n = range(lo, hi), hi - lo
+        tiles = lt if kind else ot
+        slots = [[slot_ref[2 * kind + k, b] for k in range(KR)] for b in few]
+        weights = [tiles[b].reshape(KR * BL, BL) for b in few]
+        no, nl = ob // STEPS, lb // STEPS
+        at = [
+            (b // nl) * (no + nl) + no + b % nl if kind else (b // no) * (no + nl) + b % no
+            for b in few
         ]
-
-    levels = [
-        pltpu.make_async_copy(a, b, in_sems.at[6, k])
-        for k, (a, b) in enumerate(((got_hbm, got_ref), (il_hbm, il), (ll_hbm, ll)))
-    ]
-    for copy in levels:
-        copy.start()
-    for i in range(STEPS):
-        for copy in ins(i):
-            copy.start()
-    send[...] = jnp.zeros(send.shape, send.dtype)
-    for copy in levels:
-        copy.wait()
-    ocean, ice, land = column(ocean_coef), column(ice_coef), column(land_coef)
-
-    def body(step, _):
-        for copy in ins(step):
-            copy.wait()
-        blocks = []
-        for b in range(no + nl):
-            is_ocean = b < no
-            at = step * no + b if is_ocean else step * nl + b - no
-            slots = [slot_ref[(0 if is_ocean else 2) + k, at] for k in range(2)]
-            blocks.append((is_ocean, at, slots))
-        for b, (is_ocean, at, slots) in enumerate(blocks):
-            tiles = ot if is_ocean else lt
-            src = jnp.concatenate([got_ref[s] for s in slots], axis=1)
-            mixed[b] = near[step * (no + nl) + b] + dot(src, tiles[at].reshape(2 * BL, BL), NN)
-        for b, (is_ocean, at, slots) in enumerate(blocks):
-            u = mixed[b, pl.ds(0, 8, stride=3), :]
-            v = mixed[b, pl.ds(1, 8, stride=3), :]
-            t = mixed[b, pl.ds(2, 8, stride=3), :]
-            wind = jnp.sqrt(1.0 + u * u + v * v)
-            here = lanes(at)
-            if is_ocean:
-                frac = il[pl.ds(at, 1), :].astype(jnp.float32) / 8.0
-                flux = (1.0 - frac) * (ocean * wind * (t - osv[:, here]))
-                of[:, here] = flux + frac * (ice * wind * (t - isv[:, here]))
-            else:
-                frac = ll[pl.ds(at, 1), :].astype(jnp.float32) / 8.0
-                lf[:, here] = frac * (land * wind * (t - ls[:, here]))
-        for b, (is_ocean, at, slots) in enumerate(blocks):
-            tiles, flux = (ot, of) if is_ocean else (lt, lf)
-            g = flux[:, lanes(at)].astype(jnp.bfloat16)
-            terms = dot(g, tiles[at].reshape(2 * BL, BL), NT).astype(send.dtype)
-            for k in range(2):
-                send[slots[k]] = terms[:, k * BL : (k + 1) * BL]
-        return 0
-
-    lax.fori_loop(0, STEPS, body, 0)
-    outs = [
-        pltpu.make_async_copy(a, b, out_sems.at[k])
-        for k, (a, b) in enumerate(((send, send_hbm), (of, of_hbm), (lf, lf_hbm)))
-    ]
-    for copy in outs:
-        copy.start()
+        rows = []
+        for j in range(n):
+            source = jnp.concatenate([got_ref[s] for s in slots[j]], axis=1)
+            rows.append(near[at[j]] + dot(source, weights[j], NN))
+        u, v, t = (
+            jnp.concatenate([row[8 * j : 8 * j + 8] for row in rows], axis=1) for j in range(3)
+        )
+        wind = jnp.sqrt(1.0 + u * u + v * v)
+        here = slice(lo * BL, hi * BL)
+        level = (ll if kind else il)[lo:hi, :].astype(jnp.float32) * 0.125
+        level = [jnp.broadcast_to(level[j : j + 1], (8, BL)) for j in range(n)]
+        frac = jnp.concatenate(level, axis=1)
+
+        def bulk(factors, state):
+            return column(factors, n * BL) * wind * (t - state[:, here])
+
+        if kind:
+            flux = frac * bulk(land_coef, ls)
+            lf[:, here] = flux
+        else:
+            flux = (1.0 - frac) * bulk(ocean_coef, osv) + frac * bulk(ice_coef, isv)
+            of[:, here] = flux
+        outs[i].start()
+        flux = flux.astype(jnp.bfloat16)
+        for j in range(n):
+            terms = dot(flux[:, j * BL : (j + 1) * BL], weights[j], NT).astype(send.dtype)
+            for k in range(KR):
+                send[slots[j][k]] = terms[:, k * BL : (k + 1) * BL]
+    outs.append(pltpu.make_async_copy(send, send_hbm, out_sems.at[len(parts)]))
+    outs[-1].start()
     for copy in outs:
         copy.wait()
 
 
-def far(slots, got, ot, lt, near, os, ice, il, ls, ll):
-    ob, lb = ot.shape[0], lt.shape[0]
-    nf, ns = near.shape[1], os.shape[0]
+def far(slots, got, near, os, ice, il, ls, ll, ot, lt):
     f32 = jnp.float32
-    back = (got.shape[0], ns, BL)
+    back = (got.shape[0], os.shape[0], BL)
+    count = len(OPARTS) + len(LPARTS) - 2
     return pl.pallas_call(
         far_kernel,
         out_shape=(
@@ -283,28 +271,20 @@
             jax.ShapeDtypeStruct(ls.shape, f32),
             jax.ShapeDtypeStruct(back, jnp.bfloat16),
         ),
-        in_specs=[whole(SMEM), *[whole(pl.ANY)] * 9],
+        in_specs=[whole(SMEM), *[whole()] * 7, *[whole(pl.ANY)] * 2],
         out_specs=[whole(pltpu.HBM)] * 3,
         scratch_shapes=[
-            VMEM(got.shape, got.dtype),
-            VMEM((ob, 2, BL, BL), ot.dtype),
-            VMEM((lb, 2, BL, BL), lt.dtype),
-            VMEM(near.shape, f32),
-            VMEM(os.shape, f32),
-            VMEM(ice.shape, f32),
-            VMEM(il.shape, il.dtype),
-            VMEM(ls.shape, f32),
-            VMEM(ll.shape, ll.dtype),
+            VMEM((ot.shape[0], KR, BL, BL), ot.dtype),
+            VMEM((lt.shape[0], KR, BL, BL), lt.dtype),
             VMEM(os.shape, f32),
             VMEM(ls.shape, f32),
             VMEM(back, jnp.bfloat16),
-            VMEM(((ob + lb) // STEPS, nf, BL), f32),
-            pltpu.SemaphoreType.DMA((7, STEPS)),
-            pltpu.SemaphoreType.DMA((3,)),
+            pltpu.SemaphoreType.DMA((count,)),
+            pltpu.SemaphoreType.DMA((count + 1,)),
         ],
-        compiler_params=pltpu.CompilerParams(vmem_limit_bytes=LARGE),
+        compiler_params=pltpu.CompilerParams(vmem_limit_bytes=50 << 20),
         name="far",
-    )(slots, got, ot, lt, near, os, ice, il, ls, ll)
+    )(slots, got, near, os, ice, il, ls, ll, ot, lt)
 
 
 def near_back_kernel(ol_ref, ll_ref, of_ref, lf_ref, ot_ref, lt_ref, out_ref):
@@ -422,12 +402,13 @@
     near_fields = lax.ppermute(atm_fields, axes, to_server)
     asking, slots = requests(ocn_map.T, lnd_map.T, cells)
     asked = exchange(asking)
-    got = exchange(serve(asked, hold(atm_fields, near_fields), cells))
+    held = hold(atm_fields, near_fields)
+    got = exchange(serve(asked, held, cells))
     ol, ll = ocn_local.T, lnd_local.T
-    near = near_mix(ol, ll, atm_fields, ocn_tiles, lnd_tiles)
+    near = near_mix(ol, ll, held, ocn_tiles, lnd_tiles)
     of, lf, send = far(
-        slots, got, ocn_tiles, lnd_tiles, near, ocn_state, ice_state,
-        ice_level.reshape(-1, BL), lnd_state, lnd_level.reshape(-1, BL),
+        slots, got, near, ocn_state, ice_state, ice_level.reshape(-1, BL), lnd_state,
+        lnd_level.reshape(-1, BL), ocn_tiles, lnd_tiles,
     )
     back = exchange(send)
     acc = near_back(ol, ll, of, lf, ocn_tiles, lnd_tiles)

time: 77.6 us -> 74.5 us (0.960)
  Pallas kernels: 23.6 us -> 20.8 us
  local copies, waits for them, and re-layouts: 3.06 us -> 1.87 us
  waiting for transfers between devices: 24.2 us -> 25.1 us
    pallas_call x1, Pallas kernels: 7.28 us -> 5.43 us  [far(): pl.pallas_call(far_kernel, out_shape=(jax.ShapeDtypeStruct(os.shape, f32)...]
    unnamed x18 -> x20, local copies, waits for them, and re-layouts: 3.06 us -> 1.87 us
    pallas_call x1, Pallas kernels: 4.82 us -> 3.77 us  [near_mix(): pl.pallas_call(near_mix_kernel, grid=(STEPS,), out_shape=jax.ShapeDtypeSt...]
    all_to_all x1, waiting for transfers between devices: 14.9 us -> 15.9 us  [per_device(): got = exchange(serve(asked, held, cells))]
  transfers between devices with their start and end apart: 5 -> 5, of which waited for: 3 -> 3; matrix products, arithmetic and copies ran while one was open for 0% -> 0% of each run, Pallas kernels for 17% -> 16%
where the time goes in v4:
time: 74.5 us; the launch traced here: 74 us
  waiting for transfers between devices  25.1 us (34%)
  starting transfers between devices  24.7 us (33%)
  Pallas kernels  20.8 us (28%)
  local copies, waits for them, and re-layouts  1.87 us (3%)
  between operations  0.82 us (1%)
    all_to_all x1, waiting for transfers between devices, per_device(): got = exchange(serve(asked, held, cells))  15.9 us
    all_to_all x1, starting transfers between devices, per_device(): asked = exchange(asking)  8.95 us
    ppermute x1, starting transfers between devices, per_device(): away = lax.ppermute(collect(asked, back, None, True, cells), axes, to_owner)  5.48 us
    pallas_call x1, Pallas kernels, far(): pl.pallas_call(far_kernel, out_shape=(jax.ShapeDtypeStruct(os.shape, f32)...  5.43 us
    all_to_all x1, waiting for transfers between devices, per_device(): asked = exchange(asking)  5.11 us
    all_to_all x1, starting transfers between devices, per_device(): back = exchange(send)  5.09 us
    pallas_call x1, Pallas kernels, near_back(): pl.pallas_call(near_back_kernel, grid=(STEPS,), out_shape=jax.ShapeDtypeS...  4.85 us
    all_to_all x1, waiting for transfers between devices, per_device(): back = exchange(send)  4.14 us
  transfers between devices with their start and end apart: 5, of which 3 were waited for; matrix products, arithmetic and copies ran while one was open for 0% of the time, Pallas kernels for 16%

profile of v4, /device:TPU:1, one launch (start us, length us, event | category | flops | bytes accessed | tf_op | source)
XLA Modules:
  0.0 74.0 jit_solution(18377719368392882929)
XLA Ops:
  0.6 1.5 %collective-permute-start = (bf16[24,4096]{1,0:T(8,128)(2,1)}, bf16[24,4096]{1,0:T(8,128)(2,1)S(1)}, u32[]{:S(2)}, u32[]{:S(2)}) collective-permute-start(bf16[24,4096]{1,0:T(8,128)(2,1)} %own_ref.1), channel_id=1, source_target_pairs={{0,112},{1,113},{2,114},{3,115},{4,116},{5,117},{6,118},{7,119},{8... | collective-permute-start | bytes 589832 | tf_op jit(solution)/shard_map/ppermute | solution.py:402
  2.1 1.8 %requests.1 = (s32[16,128]{1,0:T(8,128)}, s32[8,128]{1,0:T(8,128)}) custom-call(s32[2,64]{1,0:T(2,128)} %bitcast.20, s32[2,16]{1,0:T(2,128)} %bitcast.21), custom_call_target="tpu_custom_call" | custom-call | tf_op jit(solution)/shard_map/requests/pallas_call | solution.py:78
  3.9 8.9 %all-to-all-start = ((s32[16,1,128]{2,1,0:T(1,128)}), s32[16,1,128]{2,1,0:T(1,128)S(1)}, u32[]{:S(2)}, u32[]{:S(2)}) async-start(s32[16,1,128]{2,1,0:T(1,128)} %bitcast.19), calls=%async_computation | async-start | bytes 16384 | tf_op jit(solution)/shard_map/all_to_all | solution.py:404
  12.9 0.0 collective-permute-done.near_ref
  12.9 0.0 copy-start.3
  12.9 0.9 %copy-done.3 = bf16[24,4096]{1,0:T(8,128)(2,1)S(1)} copy-done((bf16[24,4096]{1,0:T(8,128)(2,1)S(1)}, bf16[24,4096]{1,0:T(8,128)(2,1)}, u32[]{:S(2)}) %copy-start.3) | copy-done | bytes 196632
  13.8 0.3 hold.1.both.f_ref
  14.1 5.1 %all-to-all-done = s32[16,1,128]{2,1,0:T(1,128)S(1)} async-done(((s32[16,1,128]{2,1,0:T(1,128)}), s32[16,1,128]{2,1,0:T(1,128)S(1)}, u32[]{:S(2)}, u32[]{:S(2)}) %all-to-all-start) | async-done | bytes 8224 | tf_op jit(solution)/shard_map/all_to_all | solution.py:404
  19.2 0.0 copy-start.8
  19.2 0.0 copy-start.9
  19.2 2.1 %serve.1 = bf16[240,24,128]{2,1,0:T(8,128)(2,1)} custom-call(s32[16,128]{1,0:T(8,128)S(1)} %bitcast.10, bf16[24,8192]{1,0:T(8,128)(2,1)S(1)} %hold.1.both.f_ref), custom_call_target="tpu_custom_call" | custom-call | tf_op jit(solution)/shard_map/serve/pallas_call | solution.py:133
  21.3 3.7 %all-to-all-start.1 = ((bf16[240,24,128]{2,1,0:T(8,128)(2,1)}), bf16[240,24,128]{2,1,0:T(8,128)(2,1)S(1)}, u32[]{:S(2)}, u32[]{:S(2)}) async-start(bf16[240,24,128]{2,1,0:T(8,128)(2,1)} %serve.1), calls=%async_computation.1 | async-start | bytes 2949120 | tf_op jit(solution)/shard_map/all_to_all | solution.py:406
  25.0 0.0 copy-done.8
  25.0 0.0 copy-done.9
  25.0 0.0 copy-start.1
  25.0 0.0 copy-start.2
  25.1 0.0 copy-start.4
  25.1 0.0 copy-start.5
  25.1 0.0 copy-start.6
  25.1 0.0 copy-start.7
  25.1 3.8 %near_mix.1.near = f32[80,24,128]{2,1,0:T(8,128)S(1)} custom-call(s32[2,64]{1,0:T(2,128)S(1)} %bitcast.16, s32[2,16]{1,0:T(2,128)S(1)} %bitcast.18, bf16[24,8192]{1,0:T(8,128)(2,1)S(1)} %hold.1.both.f_ref, bf16[64,4,128,128]{3,2,1,0:T(8,128)(2,1)} %ot_ref.3, bf16[16,4,128,128]{3,2,1,0:T(8,128)(2,1)} %lt_ref.3), custom_call_target="tpu_custom_call" | custom-call | flops 671088640 | bytes 5242880 | tf_op jit(solution)/shard_map/near_mix/pallas_call | solution.py:171
  28.9 15.9 %all-to-all-done.1.got_ref = bf16[240,24,128]{2,1,0:T(8,128)(2,1)S(1)} async-done(((bf16[240,24,128]{2,1,0:T(8,128)(2,1)}), bf16[240,24,128]{2,1,0:T(8,128)(2,1)S(1)}, u32[]{:S(2)}, u32[]{:S(2)}) %all-to-all-start.1) | async-done | bytes 1474592 | tf_op jit(solution)/shard_map/all_to_all | solution.py:406
  44.8 0.0 copy-done.1
  44.8 0.0 copy-done.2
  44.8 0.0 copy-done.4
  44.8 0.0 copy-done.5
  44.8 0.0 copy-done.6
  44.8 0.0 copy-done.7
  44.8 5.4 %far.1 = (f32[8,8192]{1,0:T(8,128)}, f32[8,2048]{1,0:T(8,128)}, bf16[240,8,128]{2,1,0:T(8,128)(2,1)}) custom-call(s32[8,128]{1,0:T(8,128)S(1)} %copy-done.7, bf16[240,24,128]{2,1,0:T(8,128)(2,1)S(1)} %all-to-all-done.1.got_ref, f32[80,24,128]{2,1,0:T(8,128)S(1)} %near_mix.1.near, f32[8,8192]{1,0:T(8,128)S(1)} %copy-done.1, f32[8,8192]{1,0:T(8,128)S(1)} %copy-done.2, ...), custom_call_target="tpu_custom_call" | custom-call | tf_op jit(solution)/shard_map/far/pallas_call | solution.py:267
  50.2 5.1 %all-to-all-start.2 = ((bf16[240,8,128]{2,1,0:T(8,128)(2,1)}), bf16[240,8,128]{2,1,0:T(8,128)(2,1)S(1)}, u32[]{:S(2)}, u32[]{:S(2)}) async-start(bf16[240,8,128]{2,1,0:T(8,128)(2,1)} %get-tuple-element.12), calls=%async_computation.2 | async-start | bytes 983040 | tf_op jit(solution)/shard_map/all_to_all | solution.py:413
  55.3 4.9 %near_back.1.refs_0_ = f32[8,4096]{1,0:T(8,128)} custom-call(s32[2,64]{1,0:T(2,128)} %bitcast.15, s32[2,16]{1,0:T(2,128)} %bitcast.17, f32[8,8192]{1,0:T(8,128)} %get-tuple-element.8.of_ref, f32[8,2048]{1,0:T(8,128)} %get-tuple-element.9.lf_ref, bf16[64,4,128,128]{3,2,1,0:T(8,128)(2,1)} %ot_ref.3, bf16[16,4,128,128]{3,2,1,0:T(8,128)(2,1)} %lt_ref.3), custom_call_target="tpu_custom_call" | custom-call | flops 671088640 | bytes 5242880 | tf_op jit(solution)/shard_map/near_back/pallas_call | solution.py:310
  60.2 4.1 %all-to-all-done.2.back_ref = bf16[240,8,128]{2,1,0:T(8,128)(2,1)S(1)} async-done(((bf16[240,8,128]{2,1,0:T(8,128)(2,1)}), bf16[240,8,128]{2,1,0:T(8,128)(2,1)S(1)}, u32[]{:S(2)}, u32[]{:S(2)}) %all-to-all-start.2) | async-done | bytes 491552 | tf_op jit(solution)/shard_map/all_to_all | solution.py:413
  64.3 1.2 %collect_far.1 = f32[8,4096]{1,0:T(8,128)S(1)} custom-call(s32[16,128]{1,0:T(8,128)S(1)} %bitcast.11, bf16[240,8,128]{2,1,0:T(8,128)(2,1)S(1)} %all-to-all-done.2.back_ref), custom_call_target="tpu_custom_call" | custom-call | flops 1048576 | bytes 4194304 | tf_op jit(solution)/shard_map/collect_far/pallas_call | solution.py:372
  65.5 5.5 %collective-permute-start.1 = (f32[8,4096]{1,0:T(8,128)S(1)}, f32[8,4096]{1,0:T(8,128)S(1)}, u32[]{:S(2)}, u32[]{:S(2)}) collective-permute-start(f32[8,4096]{1,0:T(8,128)S(1)} %collect_far.1), channel_id=1, source_target_pairs={{112,0},{113,1},{114,2},{115,3},{116,4},{117,5},{118,6},{119,7},{2... | collective-permute-start | bytes 393224 | tf_op jit(solution)/shard_map/ppermute | solution.py:416
  71.0 0.0 copy-start
  71.0 0.9 %copy-done = f32[8,4096]{1,0:T(8,128)S(1)} copy-done((f32[8,4096]{1,0:T(8,128)S(1)}, f32[8,4096]{1,0:T(8,128)}, u32[]{:S(2)}) %copy-start) | copy-done | bytes 131096
  71.9 1.4 %collect_own.1 = f32[8,4096]{1,0:T(8,128)S(1)} custom-call(s32[16,128]{1,0:T(8,128)S(1)} %bitcast.12, bf16[240,8,128]{2,1,0:T(8,128)(2,1)S(1)} %all-to-all-done.2.back_ref, f32[8,4096]{1,0:T(8,128)S(1)} %copy-done), custom_call_target="tpu_custom_call" | custom-call | flops 1048576 | bytes 4194304 | tf_op jit(solution)/shard_map/collect_own/pallas_call | solution.py:372
  73.3 0.0 collective-permute-done.1
  73.4 0.7 add.3
Async XLA Ops:
  0.6 12.2 %collective-permute-start = (bf16[24,4096]{1,0:T(8,128)(2,1)}, bf16[24,4096]{1,0:T(8,128)(2,1)S(1)}, u32[]{:S(2)}, u32[]{:S(2)}) collective-permute-start(bf16[24,4096]{1,0:T(8,128)(2,1)} %own_ref.1), channel_id=1, source_target_pairs={{0,112},{1,113},{2,114},{3,115},{4,116},{5,117},{6,118},{7,119},{8... | collective-permute-start | bytes 589832 | tf_op jit(solution)/shard_map/ppermute | solution.py:402
  3.9 15.3 %all-to-all-start = ((s32[16,1,128]{2,1,0:T(1,128)}), s32[16,1,128]{2,1,0:T(1,128)S(1)}, u32[]{:S(2)}, u32[]{:S(2)}) async-start(s32[16,1,128]{2,1,0:T(1,128)} %bitcast.19), calls=%async_computation | async-start | bytes 16384 | tf_op jit(solution)/shard_map/all_to_all | solution.py:404
  12.9 0.9 %copy-start.3 = (bf16[24,4096]{1,0:T(8,128)(2,1)S(1)}, bf16[24,4096]{1,0:T(8,128)(2,1)}, u32[]{:S(2)}) copy-start(bf16[24,4096]{1,0:T(8,128)(2,1)} %own_ref.1) | copy-start | bytes 589828
  19.2 5.8 %copy-start.8 = (s32[64,2]{0,1:T(2,128)S(1)}, s32[64,2]{0,1:T(2,128)}, u32[]{:S(2)}) copy-start(s32[64,2]{0,1:T(2,128)} %param.19) | copy-start | bytes 1540
  19.2 5.8 %copy-start.9 = (s32[16,2]{0,1:T(2,128)S(1)}, s32[16,2]{0,1:T(2,128)}, u32[]{:S(2)}) copy-start(s32[16,2]{0,1:T(2,128)} %param.22) | copy-start | bytes 388
  21.3 23.5 %all-to-all-start.1 = ((bf16[240,24,128]{2,1,0:T(8,128)(2,1)}), bf16[240,24,128]{2,1,0:T(8,128)(2,1)S(1)}, u32[]{:S(2)}, u32[]{:S(2)}) async-start(bf16[240,24,128]{2,1,0:T(8,128)(2,1)} %serve.1), calls=%async_computation.1 | async-start | bytes 2949120 | tf_op jit(solution)/shard_map/all_to_all | solution.py:406
  25.0 19.7 %copy-start.1 = (f32[8,8192]{1,0:T(8,128)S(1)}, f32[8,8192]{1,0:T(8,128)}, u32[]{:S(2)}) copy-start(f32[8,8192]{1,0:T(8,128)} %osv.1) | copy-start | bytes 786436
  25.0 19.7 %copy-start.2 = (f32[8,8192]{1,0:T(8,128)S(1)}, f32[8,8192]{1,0:T(8,128)}, u32[]{:S(2)}) copy-start(f32[8,8192]{1,0:T(8,128)} %isv.1) | copy-start | bytes 786436
  25.1 19.7 %copy-start.4 = (f32[8,2048]{1,0:T(8,128)S(1)}, f32[8,2048]{1,0:T(8,128)}, u32[]{:S(2)}) copy-start(f32[8,2048]{1,0:T(8,128)} %ls.1) | copy-start | bytes 196612
  25.1 19.7 %copy-start.5 = (s32[8192]{0:T(1024)S(1)}, s32[8192]{0:T(1024)}, u32[]{:S(2)}) copy-start(s32[8192]{0:T(1024)} %param.15) | copy-start | bytes 98308
  25.1 19.7 %copy-start.6 = (s32[2048]{0:T(1024)S(1)}, s32[2048]{0:T(1024)}, u32[]{:S(2)}) copy-start(s32[2048]{0:T(1024)} %param.17) | copy-start | bytes 24580
  25.1 19.7 %copy-start.7 = (s32[8,128]{1,0:T(8,128)S(1)}, s32[8,128]{1,0:T(8,128)}, u32[]{:S(2)}) copy-start(s32[8,128]{1,0:T(8,128)} %get-tuple-element.11.slot_ref) | copy-start | bytes 12292
  50.2 14.1 %all-to-all-start.2 = ((bf16[240,8,128]{2,1,0:T(8,128)(2,1)}), bf16[240,8,128]{2,1,0:T(8,128)(2,1)S(1)}, u32[]{:S(2)}, u32[]{:S(2)}) async-start(bf16[240,8,128]{2,1,0:T(8,128)(2,1)} %get-tuple-element.12), calls=%async_computation.2 | async-start | bytes 983040 | tf_op jit(solution)/shard_map/all_to_all | solution.py:413
  65.5 7.8 %collective-permute-start.1 = (f32[8,4096]{1,0:T(8,128)S(1)}, f32[8,4096]{1,0:T(8,128)S(1)}, u32[]{:S(2)}, u32[]{:S(2)}) collective-permute-start(f32[8,4096]{1,0:T(8,128)S(1)} %collect_far.1), channel_id=1, source_target_pairs={{112,0},{113,1},{114,2},{115,3},{116,4},{117,5},{118,6},{119,7},{2... | collective-permute-start | bytes 393224 | tf_op jit(solution)/shard_map/ppermute | solution.py:416
  71.0 0.9 %copy-start = (f32[8,4096]{1,0:T(8,128)S(1)}, f32[8,4096]{1,0:T(8,128)}, u32[]{:S(2)}) copy-start(f32[8,4096]{1,0:T(8,128)} %near_back.1.refs_0_) | copy-start | bytes 393220

commit v5 on v4

--- a/solution.py
+++ b/solution.py
@@ -12,7 +12,8 @@
 land_coef = (0.8, 1.1, 0.6, 1.5, 0.7, 1.2, 1.0, 0.5)
 
 BL = 128
-AB = 32
+AB_BITS = 5
+AB = 1 << AB_BITS
 KR = KL = 2
 CAP = 15
 GRANT, LARGE, SMALL = 60 << 20, 50 << 20, 8 << 20
@@ -45,6 +46,7 @@
 
 def request_kernel(cells, om_ref, lm_ref, req_ref, slot_ref):
     sect = lax.axis_index("sect")
+    cell_bits = cells.bit_length() - 1
     before = jnp.zeros((cells, 1), jnp.float32)
     req = jnp.zeros((cells, BL), jnp.float32)
     slot_ref[...] = jnp.zeros(slot_ref.shape, jnp.int32)
@@ -57,9 +59,9 @@
         earlier = jnp.where(earlier, 1.0, 0.0).astype(jnp.bfloat16)
         for k in range(ref.shape[0]):
             src = ref[k : k + 1, :]
-            owner = src // AB
-            col = owner % cells
-            value = src % AB + jnp.where(owner // cells == sect, 0, AB)
+            owner = src >> AB_BITS
+            col = owner & (cells - 1)
+            value = (src & (AB - 1)) + jnp.where(owner >> cell_bits == sect, 0, AB)
             chosen = lax.broadcasted_iota(jnp.int32, (cells, n), 0) == col
             onehot = jnp.where(chosen, 1.0, 0.0)
             ranks = before + dot(onehot.astype(jnp.bfloat16), earlier, NN)
@@ -91,7 +93,7 @@
 def hold_kernel(own_ref, near_ref, out_ref):
     nf, width = own_ref.shape
     rows = lax.broadcasted_iota(jnp.int32, (nf, nf), 0)
-    pick = 3 * (rows % 8) + rows // 8 == lax.broadcasted_iota(jnp.int32, (nf, nf), 1)
+    pick = 3 * (rows & 7) + (rows >> 3) == lax.broadcasted_iota(jnp.int32, (nf, nf), 1)
     pick = jnp.where(pick, 1.0, 0.0).astype(own_ref.dtype)
     for k, ref in enumerate((own_ref, near_ref)):
         for at in range(0, width, 8 * BL):
@@ -152,8 +154,14 @@
     ]
 
 
-def near_mix_kernel(ol_ref, ll_ref, f_ref, ot_ref, lt_ref, out_ref):
+def near_mix_kernel(ol_ref, ll_ref, f_ref, ot_ref, lt_ref, lt_hbm, out_ref, bring_ref, sem):
     step = pl.program_id(0)
+    bring = pltpu.make_async_copy(lt_hbm.at[:, pl.ds(0, KR)], bring_ref, sem)
+
+    @pl.when(step == 0)
+    def _():
+        bring.start()
+
     at = 0
     for ids, tiles in ((ol_ref, ot_ref), (ll_ref, lt_ref)):
         n = tiles.shape[0]
@@ -164,6 +172,10 @@
             )
             at += 1
 
+    @pl.when(step == STEPS - 1)
+    def _():
+        bring.wait()
+
 
 def near_mix(ol, ll, fields, ot, lt):
     ob, lb = ot.shape[0], lt.shape[0]
@@ -171,22 +183,30 @@
     return pl.pallas_call(
         near_mix_kernel,
         grid=(STEPS,),
-        out_shape=jax.ShapeDtypeStruct((ob + lb, nf, BL), jnp.float32),
+        out_shape=(
+            jax.ShapeDtypeStruct((ob + lb, nf, BL), jnp.float32),
+            jax.ShapeDtypeStruct((lb, KR, BL, BL), lt.dtype),
+        ),
         in_specs=[
             whole(SMEM),
             whole(SMEM),
             pl.BlockSpec(fields.shape, lambda i: (0, 0)),
             *tile_specs(ob, lb, 1),
+            whole(pl.ANY),
         ],
-        out_specs=pl.BlockSpec(((ob + lb) // STEPS, nf, BL), lambda i: (i, 0, 0)),
-        compiler_params=pltpu.CompilerParams(vmem_limit_bytes=52 << 20),
+        out_specs=[
+            pl.BlockSpec(((ob + lb) // STEPS, nf, BL), lambda i: (i, 0, 0)),
+            whole(),
+        ],
+        scratch_shapes=[pltpu.SemaphoreType.DMA(())],
+        compiler_params=pltpu.CompilerParams(vmem_limit_bytes=51 << 20),
         cost_estimate=pl.CostEstimate(
             flops=2 * (ob + lb) * 2 * BL * BL * 128,
             bytes_accessed=(ob + lb) * 2 * BL * BL * 2,
             transcendentals=0,
         ),
         name="near_mix",
-    )(ol, ll, fields, ot, lt)
+    )(ol, ll, fields, ot, lt, lt)
 
 
 def portions(count, parts):
@@ -195,20 +215,20 @@
 
 
 def far_kernel(
-    slot_ref, got_ref, near, osv, isv, il, ls, ll, ot_hbm, lt_hbm, of_hbm, lf_hbm, send_hbm,
-    ot, lt, of, lf, send, in_sems, out_sems,
+    slot_ref, got_ref, near, osv, isv, il, ls, ll, lt, ot_hbm, of_hbm, lf_hbm, send_hbm,
+    ot, of, lf, send, in_sems, out_sems,
 ):
     ob, lb = ot.shape[0], lt.shape[0]
-    parts = [(0, *p) for p in portions(ob, OPARTS)] + [(1, *p) for p in portions(lb, LPARTS)]
+    parts = [(1, *p) for p in portions(lb, LPARTS)] + [(0, *p) for p in portions(ob, OPARTS)]
     ins, outs = [], []
     for i, (kind, lo, hi) in enumerate(parts):
-        hbm, on_chip = (lt_hbm, lt) if kind else (ot_hbm, ot)
         some = pl.ds(lo, hi - lo)
-        copy = pltpu.make_async_copy(
-            hbm.at[some, pl.ds(0, KR)], on_chip.at[some], in_sems.at[i]
-        )
-        copy.start()
-        ins.append(copy)
+        if not kind:
+            copy = pltpu.make_async_copy(
+                ot_hbm.at[some, pl.ds(0, KR)], ot.at[some], in_sems.at[i]
+            )
+            copy.start()
+        ins.append(None if kind else copy)
         flux, flux_hbm = (lf, lf_hbm) if kind else (of, of_hbm)
         some = pl.ds(lo * BL, (hi - lo) * BL)
         outs.append(
@@ -216,7 +236,8 @@
         )
     send[...] = jnp.zeros(send.shape, send.dtype)
     for i, (kind, lo, hi) in enumerate(parts):
-        ins[i].wait()
+        if not kind:
+            ins[i].wait()
         few, n = range(lo, hi), hi - lo
         tiles = lt if kind else ot
         slots = [[slot_ref[2 * kind + k, b] for k in range(KR)] for b in few]
@@ -260,7 +281,7 @@
         copy.wait()
 
 
-def far(slots, got, near, os, ice, il, ls, ll, ot, lt):
+def far(slots, got, near, os, ice, il, ls, ll, lt, ot):
     f32 = jnp.float32
     back = (got.shape[0], os.shape[0], BL)
     count = len(OPARTS) + len(LPARTS) - 2
@@ -271,11 +292,10 @@
             jax.ShapeDtypeStruct(ls.shape, f32),
             jax.ShapeDtypeStruct(back, jnp.bfloat16),
         ),
-        in_specs=[whole(SMEM), *[whole()] * 7, *[whole(pl.ANY)] * 2],
+        in_specs=[whole(SMEM), *[whole()] * 8, whole(pl.ANY)],
         out_specs=[whole(pltpu.HBM)] * 3,
         scratch_shapes=[
             VMEM((ot.shape[0], KR, BL, BL), ot.dtype),
-            VMEM((lt.shape[0], KR, BL, BL), lt.dtype),
             VMEM(os.shape, f32),
             VMEM(ls.shape, f32),
             VMEM(back, jnp.bfloat16),
@@ -284,7 +304,7 @@
         ],
         compiler_params=pltpu.CompilerParams(vmem_limit_bytes=50 << 20),
         name="far",
-    )(slots, got, near, os, ice, il, ls, ll, ot, lt)
+    )(slots, got, near, os, ice, il, ls, ll, lt, ot)
 
 
 def near_back_kernel(ol_ref, ll_ref, of_ref, lf_ref, ot_ref, lt_ref, out_ref):
@@ -360,7 +380,8 @@
         load.wait()
     for b in range(AB):
         here = slice(b * BL, (b + 1) * BL)
-        out_ref[:, here] = functools.reduce(jnp.add, [ref[:, here] for ref in totals])
+        total = functools.reduce(jnp.add, [ref[:, here] for ref in totals])
+        out_ref[:, here] = total.astype(out_ref.dtype)
 
 
 def collect(asked, back, acc, neighbours, cells):
@@ -371,7 +392,7 @@
         accs, more = (acc,), [VMEM(shape, jnp.float32), pltpu.SemaphoreType.DMA(())]
     return pl.pallas_call(
         functools.partial(collect_kernel, cells, neighbours),
-        out_shape=jax.ShapeDtypeStruct(shape, jnp.float32),
+        out_shape=jax.ShapeDtypeStruct(shape, jnp.float32 if accs else back.dtype),
         in_specs=[whole(SMEM), whole(), *[whole(pltpu.HBM)] * len(accs)],
         out_specs=whole(),
         scratch_shapes=[*more, *[VMEM((ns, (AB + 1) * BL), jnp.float32)] * CHAINS],
@@ -405,17 +426,17 @@
     held = hold(atm_fields, near_fields)
     got = exchange(serve(asked, held, cells))
     ol, ll = ocn_local.T, lnd_local.T
-    near = near_mix(ol, ll, held, ocn_tiles, lnd_tiles)
+    near, lt = near_mix(ol, ll, held, ocn_tiles, lnd_tiles)
     of, lf, send = far(
         slots, got, near, ocn_state, ice_state, ice_level.reshape(-1, BL), lnd_state,
-        lnd_level.reshape(-1, BL), ocn_tiles, lnd_tiles,
+        lnd_level.reshape(-1, BL), lt, ocn_tiles,
     )
     back = exchange(send)
     acc = near_back(ol, ll, of, lf, ocn_tiles, lnd_tiles)
     back, acc = lax.optimization_barrier((back, acc))
     away = lax.ppermute(collect(asked, back, None, True, cells), axes, to_owner)
     own = collect(asked, back, acc, False, cells)
-    return own + away, of, lf
+    return own + away.astype(jnp.float32), of, lf
 
 
 def solution(mesh):

time: 74.5 us -> 76 us (1.020)
  Pallas kernels: 20.8 us -> 21.7 us
where the time goes in v5:
time: 76 us; the launch traced here: 75.5 us
  starting transfers between devices  25.4 us (33%)
  waiting for transfers between devices  25 us (33%)
  Pallas kernels  21.7 us (29%)
  local copies, waits for them, and re-layouts  1.87 us (2%)
  between operations  0.82 us (1%)
    all_to_all x1, waiting for transfers between devices, per_device(): got = exchange(serve(asked, held, cells))  15.7 us
    all_to_all x1, starting transfers between devices, per_device(): asked = exchange(asking)  8.95 us
    pallas_call x1, Pallas kernels, far(): pl.pallas_call(far_kernel, out_shape=(jax.ShapeDtypeStruct(os.shape, f32)...  6.13 us
    ppermute x1, starting transfers between devices, per_device(): away = lax.ppermute(collect(asked, back, None, True, cells), axes, to_owner)  5.48 us
    all_to_all x1, waiting for transfers between devices, per_device(): asked = exchange(asking)  5.12 us
    all_to_all x1, starting transfers between devices, per_device(): back = exchange(send)  5.09 us
    pallas_call x1, Pallas kernels, near_back(): pl.pallas_call(near_back_kernel, grid=(STEPS,), out_shape=jax.ShapeDtypeS...  4.85 us
    all_to_all x1, starting transfers between devices, per_device(): got = exchange(serve(asked, held, cells))  4.42 us
  transfers between devices with their start and end apart: 5, of which 3 were waited for; matrix products, arithmetic and copies ran while one was open for 0% of the time, Pallas kernels for 16%

profile of v5, /device:TPU:1, one launch (start us, length us, event | category | flops | bytes accessed | tf_op | source)
XLA Modules:
  0.0 75.5 jit_solution(7638201848502057332)
XLA Ops:
  0.6 1.5 %collective-permute-start = (bf16[24,4096]{1,0:T(8,128)(2,1)}, bf16[24,4096]{1,0:T(8,128)(2,1)S(1)}, u32[]{:S(2)}, u32[]{:S(2)}) collective-permute-start(bf16[24,4096]{1,0:T(8,128)(2,1)} %own_ref.1), channel_id=1, source_target_pairs={{0,112},{1,113},{2,114},{3,115},{4,116},{5,117},{6,118},{7,119},{8... | collective-permute-start | bytes 589832 | tf_op jit(solution)/shard_map/ppermute | solution.py:423
  2.1 1.8 %requests.1 = (s32[16,128]{1,0:T(8,128)}, s32[8,128]{1,0:T(8,128)}) custom-call(s32[2,64]{1,0:T(2,128)} %bitcast.20, s32[2,16]{1,0:T(2,128)} %bitcast.21), custom_call_target="tpu_custom_call" | custom-call | tf_op jit(solution)/shard_map/requests/pallas_call | solution.py:80
  3.9 8.9 %all-to-all-start = ((s32[16,1,128]{2,1,0:T(1,128)}), s32[16,1,128]{2,1,0:T(1,128)S(1)}, u32[]{:S(2)}, u32[]{:S(2)}) async-start(s32[16,1,128]{2,1,0:T(1,128)} %bitcast.19), calls=%async_computation | async-start | bytes 16384 | tf_op jit(solution)/shard_map/all_to_all | solution.py:425
  12.9 0.0 collective-permute-done.near_ref
  12.9 0.0 copy-start.3
  12.9 0.9 %copy-done.3 = bf16[24,4096]{1,0:T(8,128)(2,1)S(1)} copy-done((bf16[24,4096]{1,0:T(8,128)(2,1)S(1)}, bf16[24,4096]{1,0:T(8,128)(2,1)}, u32[]{:S(2)}) %copy-start.3) | copy-done | bytes 196632
  13.8 0.3 hold.1.both.f_ref
  14.1 5.1 %all-to-all-done = s32[16,1,128]{2,1,0:T(1,128)S(1)} async-done(((s32[16,1,128]{2,1,0:T(1,128)}), s32[16,1,128]{2,1,0:T(1,128)S(1)}, u32[]{:S(2)}, u32[]{:S(2)}) %all-to-all-start) | async-done | bytes 8224 | tf_op jit(solution)/shard_map/all_to_all | solution.py:425
  19.2 0.0 copy-start.8
  19.2 0.0 copy-start.9
  19.2 2.1 %serve.1 = bf16[240,24,128]{2,1,0:T(8,128)(2,1)} custom-call(s32[16,128]{1,0:T(8,128)S(1)} %bitcast.10, bf16[24,8192]{1,0:T(8,128)(2,1)S(1)} %hold.1.both.f_ref), custom_call_target="tpu_custom_call" | custom-call | tf_op jit(solution)/shard_map/serve/pallas_call | solution.py:135
  21.3 4.4 %all-to-all-start.1 = ((bf16[240,24,128]{2,1,0:T(8,128)(2,1)}), bf16[240,24,128]{2,1,0:T(8,128)(2,1)}, u32[]{:S(2)}, u32[]{:S(2)}) async-start(bf16[240,24,128]{2,1,0:T(8,128)(2,1)} %serve.1), calls=%async_computation.1 | async-start | bytes 2949120 | tf_op jit(solution)/shard_map/all_to_all | solution.py:427
  25.7 0.0 copy-done.8
  25.7 0.0 copy-done.9
  25.7 0.0 copy-start.1
  25.7 0.0 copy-start.2
  25.7 0.0 copy-start.4
  25.8 0.0 copy-start.5
  25.8 0.0 copy-start.6
  25.8 0.0 copy-start.7
  25.8 4.0 %near_mix.1 = (f32[80,24,128]{2,1,0:T(8,128)S(1)}, bf16[16,2,128,128]{3,2,1,0:T(8,128)(2,1)S(1)}) custom-call(s32[2,64]{1,0:T(2,128)S(1)} %bitcast.16, s32[2,16]{1,0:T(2,128)S(1)} %bitcast.18, bf16[24,8192]{1,0:T(8,128)(2,1)S(1)} %hold.1.both.f_ref, bf16[64,4,128,128]{3,2,1,0:T(8,128)(2,1)} %ot_ref.3, bf16[16,4,128,128]{3,2,1,0:T(8,128)(2,1)} %lt_ref.3, ...), custom_call_target="tpu_custom_call" | custom-call | flops 671088640 | bytes 5242880 | tf_op jit(solution)/shard_map/near_mix/pallas_call | solution.py:183
  29.8 15.7 %all-to-all-done.1.got_ref = bf16[240,24,128]{2,1,0:T(8,128)(2,1)} async-done(((bf16[240,24,128]{2,1,0:T(8,128)(2,1)}), bf16[240,24,128]{2,1,0:T(8,128)(2,1)}, u32[]{:S(2)}, u32[]{:S(2)}) %all-to-all-start.1) | async-done | bytes 1474592 | tf_op jit(solution)/shard_map/all_to_all | solution.py:427
  45.5 0.0 copy-done.1
  45.5 0.0 copy-done.2
  45.5 0.0 copy-done.4
  45.5 0.0 copy-done.5
  45.5 0.0 copy-done.6
  45.5 0.0 copy-done.7
  45.5 6.1 %far.1 = (f32[8,8192]{1,0:T(8,128)}, f32[8,2048]{1,0:T(8,128)}, bf16[240,8,128]{2,1,0:T(8,128)(2,1)}) custom-call(s32[8,128]{1,0:T(8,128)S(1)} %copy-done.7, bf16[240,24,128]{2,1,0:T(8,128)(2,1)} %all-to-all-done.1.got_ref, f32[80,24,128]{2,1,0:T(8,128)S(1)} %get-tuple-element.14.near, f32[8,8192]{1,0:T(8,128)S(1)} %copy-done.1, f32[8,8192]{1,0:T(8,128)S(1)} %copy-done.2, ...), custom_call_target="tpu_custom_call" | custom-call | tf_op jit(solution)/shard_map/far/pallas_call | solution.py:288
  51.7 5.1 %all-to-all-start.2 = ((bf16[240,8,128]{2,1,0:T(8,128)(2,1)}), bf16[240,8,128]{2,1,0:T(8,128)(2,1)S(1)}, u32[]{:S(2)}, u32[]{:S(2)}) async-start(bf16[240,8,128]{2,1,0:T(8,128)(2,1)} %get-tuple-element.16), calls=%async_computation.2 | async-start | bytes 983040 | tf_op jit(solution)/shard_map/all_to_all | solution.py:434
  56.8 4.9 %near_back.1.refs_0_ = f32[8,4096]{1,0:T(8,128)} custom-call(s32[2,64]{1,0:T(2,128)} %bitcast.15, s32[2,16]{1,0:T(2,128)} %bitcast.17, f32[8,8192]{1,0:T(8,128)} %get-tuple-element.10.of_ref, f32[8,2048]{1,0:T(8,128)} %get-tuple-element.11.lf_ref, bf16[64,4,128,128]{3,2,1,0:T(8,128)(2,1)} %ot_ref.3, bf16[16,4,128,128]{3,2,1,0:T(8,128)(2,1)} %lt_ref.3), custom_call_target="tpu_custom_call" | custom-call | flops 671088640 | bytes 5242880 | tf_op jit(solution)/shard_map/near_back/pallas_call | solution.py:330
  61.6 4.1 %all-to-all-done.2.back_ref = bf16[240,8,128]{2,1,0:T(8,128)(2,1)S(1)} async-done(((bf16[240,8,128]{2,1,0:T(8,128)(2,1)}), bf16[240,8,128]{2,1,0:T(8,128)(2,1)S(1)}, u32[]{:S(2)}, u32[]{:S(2)}) %all-to-all-start.2) | async-done | bytes 491552 | tf_op jit(solution)/shard_map/all_to_all | solution.py:434
  65.8 1.2 %collect_far.1 = bf16[8,4096]{1,0:T(8,128)(2,1)S(1)} custom-call(s32[16,128]{1,0:T(8,128)S(1)} %bitcast.11, bf16[240,8,128]{2,1,0:T(8,128)(2,1)S(1)} %all-to-all-done.2.back_ref), custom_call_target="tpu_custom_call" | custom-call | flops 1048576 | bytes 4194304 | tf_op jit(solution)/shard_map/collect_far/pallas_call | solution.py:393
  67.0 5.5 %collective-permute-start.1 = (bf16[8,4096]{1,0:T(8,128)(2,1)S(1)}, bf16[8,4096]{1,0:T(8,128)(2,1)S(1)}, u32[]{:S(2)}, u32[]{:S(2)}) collective-permute-start(bf16[8,4096]{1,0:T(8,128)(2,1)S(1)} %collect_far.1), channel_id=1, source_target_pairs={{112,0},{113,1},{114,2},{115,3},{116,4},{117,5},{118,6},{119,7},{2... | collective-permute-start | bytes 196616 | tf_op jit(solution)/shard_map/ppermute | solution.py:437
  72.4 0.0 copy-start
  72.4 0.9 %copy-done = f32[8,4096]{1,0:T(8,128)S(1)} copy-done((f32[8,4096]{1,0:T(8,128)S(1)}, f32[8,4096]{1,0:T(8,128)}, u32[]{:S(2)}) %copy-start) | copy-done | bytes 131096
  73.3 1.4 %collect_own.1 = f32[8,4096]{1,0:T(8,128)S(1)} custom-call(s32[16,128]{1,0:T(8,128)S(1)} %bitcast.12, bf16[240,8,128]{2,1,0:T(8,128)(2,1)S(1)} %all-to-all-done.2.back_ref, f32[8,4096]{1,0:T(8,128)S(1)} %copy-done), custom_call_target="tpu_custom_call" | custom-call | flops 1048576 | bytes 4194304 | tf_op jit(solution)/shard_map/collect_own/pallas_call | solution.py:393
  74.8 0.0 collective-permute-done.1
  74.8 0.7 convert_add_fusion
Async XLA Ops:
  0.6 12.2 %collective-permute-start = (bf16[24,4096]{1,0:T(8,128)(2,1)}, bf16[24,4096]{1,0:T(8,128)(2,1)S(1)}, u32[]{:S(2)}, u32[]{:S(2)}) collective-permute-start(bf16[24,4096]{1,0:T(8,128)(2,1)} %own_ref.1), channel_id=1, source_target_pairs={{0,112},{1,113},{2,114},{3,115},{4,116},{5,117},{6,118},{7,119},{8... | collective-permute-start | bytes 589832 | tf_op jit(solution)/shard_map/ppermute | solution.py:423
  3.9 15.3 %all-to-all-start = ((s32[16,1,128]{2,1,0:T(1,128)}), s32[16,1,128]{2,1,0:T(1,128)S(1)}, u32[]{:S(2)}, u32[]{:S(2)}) async-start(s32[16,1,128]{2,1,0:T(1,128)} %bitcast.19), calls=%async_computation | async-start | bytes 16384 | tf_op jit(solution)/shard_map/all_to_all | solution.py:425
  12.9 0.9 %copy-start.3 = (bf16[24,4096]{1,0:T(8,128)(2,1)S(1)}, bf16[24,4096]{1,0:T(8,128)(2,1)}, u32[]{:S(2)}) copy-start(bf16[24,4096]{1,0:T(8,128)(2,1)} %own_ref.1) | copy-start | bytes 589828
  19.2 6.5 %copy-start.8 = (s32[64,2]{0,1:T(2,128)S(1)}, s32[64,2]{0,1:T(2,128)}, u32[]{:S(2)}) copy-start(s32[64,2]{0,1:T(2,128)} %param.19) | copy-start | bytes 1540
  19.2 6.5 %copy-start.9 = (s32[16,2]{0,1:T(2,128)S(1)}, s32[16,2]{0,1:T(2,128)}, u32[]{:S(2)}) copy-start(s32[16,2]{0,1:T(2,128)} %param.22) | copy-start | bytes 388
  21.3 24.2 %all-to-all-start.1 = ((bf16[240,24,128]{2,1,0:T(8,128)(2,1)}), bf16[240,24,128]{2,1,0:T(8,128)(2,1)}, u32[]{:S(2)}, u32[]{:S(2)}) async-start(bf16[240,24,128]{2,1,0:T(8,128)(2,1)} %serve.1), calls=%async_computation.1 | async-start | bytes 2949120 | tf_op jit(solution)/shard_map/all_to_all | solution.py:427
  25.7 19.8 %copy-start.1 = (f32[8,8192]{1,0:T(8,128)S(1)}, f32[8,8192]{1,0:T(8,128)}, u32[]{:S(2)}) copy-start(f32[8,8192]{1,0:T(8,128)} %osv.1) | copy-start | bytes 786436
  25.7 19.8 %copy-start.2 = (f32[8,8192]{1,0:T(8,128)S(1)}, f32[8,8192]{1,0:T(8,128)}, u32[]{:S(2)}) copy-start(f32[8,8192]{1,0:T(8,128)} %isv.1) | copy-start | bytes 786436
  25.7 19.8 %copy-start.4 = (f32[8,2048]{1,0:T(8,128)S(1)}, f32[8,2048]{1,0:T(8,128)}, u32[]{:S(2)}) copy-start(f32[8,2048]{1,0:T(8,128)} %ls.1) | copy-start | bytes 196612
  25.8 19.8 %copy-start.5 = (s32[8192]{0:T(1024)S(1)}, s32[8192]{0:T(1024)}, u32[]{:S(2)}) copy-start(s32[8192]{0:T(1024)} %param.15) | copy-start | bytes 98308
  25.8 19.8 %copy-start.6 = (s32[2048]{0:T(1024)S(1)}, s32[2048]{0:T(1024)}, u32[]{:S(2)}) copy-start(s32[2048]{0:T(1024)} %param.17) | copy-start | bytes 24580
  25.8 19.8 %copy-start.7 = (s32[8,128]{1,0:T(8,128)S(1)}, s32[8,128]{1,0:T(8,128)}, u32[]{:S(2)}) copy-start(s32[8,128]{1,0:T(8,128)} %get-tuple-element.13.slot_ref) | copy-start | bytes 12292
  51.7 14.1 %all-to-all-start.2 = ((bf16[240,8,128]{2,1,0:T(8,128)(2,1)}), bf16[240,8,128]{2,1,0:T(8,128)(2,1)S(1)}, u32[]{:S(2)}, u32[]{:S(2)}) async-start(bf16[240,8,128]{2,1,0:T(8,128)(2,1)} %get-tuple-element.16), calls=%async_computation.2 | async-start | bytes 983040 | tf_op jit(solution)/shard_map/all_to_all | solution.py:434
  67.0 7.8 %collective-permute-start.1 = (bf16[8,4096]{1,0:T(8,128)(2,1)S(1)}, bf16[8,4096]{1,0:T(8,128)(2,1)S(1)}, u32[]{:S(2)}, u32[]{:S(2)}) collective-permute-start(bf16[8,4096]{1,0:T(8,128)(2,1)S(1)} %collect_far.1), channel_id=1, source_target_pairs={{112,0},{113,1},{114,2},{115,3},{116,4},{117,5},{118,6},{119,7},{2... | collective-permute-start | bytes 196616 | tf_op jit(solution)/shard_map/ppermute | solution.py:437
  72.4 0.9 %copy-start = (f32[8,4096]{1,0:T(8,128)S(1)}, f32[8,4096]{1,0:T(8,128)}, u32[]{:S(2)}) copy-start(f32[8,4096]{1,0:T(8,128)} %near_back.1.refs_0_) | copy-start | bytes 393220

commit v6 on v4

--- a/solution.py
+++ b/solution.py
@@ -12,7 +12,8 @@
 land_coef = (0.8, 1.1, 0.6, 1.5, 0.7, 1.2, 1.0, 0.5)
 
 BL = 128
-AB = 32
+AB_BITS = 5
+AB = 1 << AB_BITS
 KR = KL = 2
 CAP = 15
 GRANT, LARGE, SMALL = 60 << 20, 50 << 20, 8 << 20
@@ -45,6 +46,7 @@
 
 def request_kernel(cells, om_ref, lm_ref, req_ref, slot_ref):
     sect = lax.axis_index("sect")
+    cell_bits = cells.bit_length() - 1
     before = jnp.zeros((cells, 1), jnp.float32)
     req = jnp.zeros((cells, BL), jnp.float32)
     slot_ref[...] = jnp.zeros(slot_ref.shape, jnp.int32)
@@ -57,9 +59,9 @@
         earlier = jnp.where(earlier, 1.0, 0.0).astype(jnp.bfloat16)
         for k in range(ref.shape[0]):
             src = ref[k : k + 1, :]
-            owner = src // AB
-            col = owner % cells
-            value = src % AB + jnp.where(owner // cells == sect, 0, AB)
+            owner = src >> AB_BITS
+            col = owner & (cells - 1)
+            value = (src & (AB - 1)) + jnp.where(owner >> cell_bits == sect, 0, AB)
             chosen = lax.broadcasted_iota(jnp.int32, (cells, n), 0) == col
             onehot = jnp.where(chosen, 1.0, 0.0)
             ranks = before + dot(onehot.astype(jnp.bfloat16), earlier, NN)
@@ -91,7 +93,7 @@
 def hold_kernel(own_ref, near_ref, out_ref):
     nf, width = own_ref.shape
     rows = lax.broadcasted_iota(jnp.int32, (nf, nf), 0)
-    pick = 3 * (rows % 8) + rows // 8 == lax.broadcasted_iota(jnp.int32, (nf, nf), 1)
+    pick = 3 * (rows & 7) + (rows >> 3) == lax.broadcasted_iota(jnp.int32, (nf, nf), 1)
     pick = jnp.where(pick, 1.0, 0.0).astype(own_ref.dtype)
     for k, ref in enumerate((own_ref, near_ref)):
         for at in range(0, width, 8 * BL):
@@ -142,7 +144,7 @@
 
 
 STEPS = 4
-OPARTS, LPARTS = (0, 2, 6, 11, 16), (0, 16)
+PARTS = (0, 4, 10, 16)
 
 
 def tile_specs(ob, lb, half):
@@ -189,9 +191,11 @@
     )(ol, ll, fields, ot, lt)
 
 
-def portions(count, parts):
-    cuts = [count * p // 16 for p in parts]
-    return list(zip(cuts[:-1], cuts[1:]))
+def portions(ob, lb):
+    cuts = [ob * p // 16 for p in PARTS]
+    out = [[(0, lo, hi)] for lo, hi in zip(cuts[:-1], cuts[1:])]
+    out[-1].append((1, 0, lb))
+    return out
 
 
 def far_kernel(
@@ -199,62 +203,66 @@
     ot, lt, of, lf, send, in_sems, out_sems,
 ):
     ob, lb = ot.shape[0], lt.shape[0]
-    parts = [(0, *p) for p in portions(ob, OPARTS)] + [(1, *p) for p in portions(lb, LPARTS)]
+    no, nl = ob // STEPS, lb // STEPS
+    parts = portions(ob, lb)
     ins, outs = [], []
-    for i, (kind, lo, hi) in enumerate(parts):
-        hbm, on_chip = (lt_hbm, lt) if kind else (ot_hbm, ot)
-        some = pl.ds(lo, hi - lo)
-        copy = pltpu.make_async_copy(
-            hbm.at[some, pl.ds(0, KR)], on_chip.at[some], in_sems.at[i]
-        )
-        copy.start()
-        ins.append(copy)
-        flux, flux_hbm = (lf, lf_hbm) if kind else (of, of_hbm)
-        some = pl.ds(lo * BL, (hi - lo) * BL)
-        outs.append(
-            pltpu.make_async_copy(flux.at[:, some], flux_hbm.at[:, some], out_sems.at[i])
-        )
+    for part in parts:
+        for kind, lo, hi in part:
+            hbm, on_chip = (lt_hbm, lt) if kind else (ot_hbm, ot)
+            some = pl.ds(lo, hi - lo)
+            copy = pltpu.make_async_copy(
+                hbm.at[some, pl.ds(0, KR)], on_chip.at[some], in_sems.at[len(ins)]
+            )
+            copy.start()
+            ins.append(copy)
+            flux, flux_hbm = (lf, lf_hbm) if kind else (of, of_hbm)
+            some = pl.ds(lo * BL, (hi - lo) * BL)
+            outs.append(
+                pltpu.make_async_copy(flux.at[:, some], flux_hbm.at[:, some], out_sems.at[len(outs)])
+            )
     send[...] = jnp.zeros(send.shape, send.dtype)
-    for i, (kind, lo, hi) in enumerate(parts):
-        ins[i].wait()
-        few, n = range(lo, hi), hi - lo
-        tiles = lt if kind else ot
-        slots = [[slot_ref[2 * kind + k, b] for k in range(KR)] for b in few]
-        weights = [tiles[b].reshape(KR * BL, BL) for b in few]
-        no, nl = ob // STEPS, lb // STEPS
-        at = [
-            (b // nl) * (no + nl) + no + b % nl if kind else (b // no) * (no + nl) + b % no
-            for b in few
-        ]
+    waits, sends = iter(ins), iter(outs)
+    for part in parts:
+        for _ in part:
+            next(waits).wait()
+        work = [(kind, b) for kind, lo, hi in part for b in range(lo, hi)]
+        slots = [[slot_ref[2 * kind + k, b] for k in range(KR)] for kind, b in work]
+        weights = [(lt if kind else ot)[b].reshape(KR * BL, BL) for kind, b in work]
         rows = []
-        for j in range(n):
-            source = jnp.concatenate([got_ref[s] for s in slots[j]], axis=1)
-            rows.append(near[at[j]] + dot(source, weights[j], NN))
-        u, v, t = (
-            jnp.concatenate([row[8 * j : 8 * j + 8] for row in rows], axis=1) for j in range(3)
-        )
-        wind = jnp.sqrt(1.0 + u * u + v * v)
-        here = slice(lo * BL, hi * BL)
-        level = (ll if kind else il)[lo:hi, :].astype(jnp.float32) * 0.125
-        level = [jnp.broadcast_to(level[j : j + 1], (8, BL)) for j in range(n)]
-        frac = jnp.concatenate(level, axis=1)
-
-        def bulk(factors, state):
-            return column(factors, n * BL) * wind * (t - state[:, here])
-
-        if kind:
-            flux = frac * bulk(land_coef, ls)
-            lf[:, here] = flux
-        else:
-            flux = (1.0 - frac) * bulk(ocean_coef, osv) + frac * bulk(ice_coef, isv)
-            of[:, here] = flux
-        outs[i].start()
-        flux = flux.astype(jnp.bfloat16)
-        for j in range(n):
-            terms = dot(flux[:, j * BL : (j + 1) * BL], weights[j], NT).astype(send.dtype)
+        for (kind, b), pair, weight in zip(work, slots, weights):
+            at = (b // nl) * (no + nl) + no + b % nl if kind else (b // no) * (no + nl) + b % no
+            source = jnp.concatenate([got_ref[s] for s in pair], axis=1)
+            rows.append(near[at] + dot(source, weight, NN))
+        fluxes = []
+        for kind, lo, hi in part:
+            n = hi - lo
+            mine = rows[len(fluxes) : len(fluxes) + n]
+            u, v, t = (
+                jnp.concatenate([row[8 * j : 8 * j + 8] for row in mine], axis=1) for j in range(3)
+            )
+            wind = jnp.sqrt(1.0 + u * u + v * v)
+            here = slice(lo * BL, hi * BL)
+            level = (ll if kind else il)[lo:hi, :].astype(jnp.float32) * 0.125
+            level = [jnp.broadcast_to(level[j : j + 1], (8, BL)) for j in range(n)]
+            frac = jnp.concatenate(level, axis=1)
+
+            def bulk(factors, state):
+                return column(factors, n * BL) * wind * (t - state[:, here])
+
+            if kind:
+                flux = frac * bulk(land_coef, ls)
+                lf[:, here] = flux
+            else:
+                flux = (1.0 - frac) * bulk(ocean_coef, osv) + frac * bulk(ice_coef, isv)
+                of[:, here] = flux
+            next(sends).start()
+            flux = flux.astype(jnp.bfloat16)
+            fluxes += [flux[:, j * BL : (j + 1) * BL] for j in range(n)]
+        for flux, pair, weight in zip(fluxes, slots, weights):
+            terms = dot(flux, weight, NT).astype(send.dtype)
             for k in range(KR):
-                send[slots[j][k]] = terms[:, k * BL : (k + 1) * BL]
-    outs.append(pltpu.make_async_copy(send, send_hbm, out_sems.at[len(parts)]))
+                send[pair[k]] = terms[:, k * BL : (k + 1) * BL]
+    outs.append(pltpu.make_async_copy(send, send_hbm, out_sems.at[len(outs)]))
     outs[-1].start()
     for copy in outs:
         copy.wait()
@@ -263,7 +271,7 @@
 def far(slots, got, near, os, ice, il, ls, ll, ot, lt):
     f32 = jnp.float32
     back = (got.shape[0], os.shape[0], BL)
-    count = len(OPARTS) + len(LPARTS) - 2
+    count = len(PARTS)
     return pl.pallas_call(
         far_kernel,
         out_shape=(
@@ -360,7 +368,8 @@
         load.wait()
     for b in range(AB):
         here = slice(b * BL, (b + 1) * BL)
-        out_ref[:, here] = functools.reduce(jnp.add, [ref[:, here] for ref in totals])
+        total = functools.reduce(jnp.add, [ref[:, here] for ref in totals])
+        out_ref[:, here] = total.astype(out_ref.dtype)
 
 
 def collect(asked, back, acc, neighbours, cells):
@@ -371,7 +380,7 @@
         accs, more = (acc,), [VMEM(shape, jnp.float32), pltpu.SemaphoreType.DMA(())]
     return pl.pallas_call(
         functools.partial(collect_kernel, cells, neighbours),
-        out_shape=jax.ShapeDtypeStruct(shape, jnp.float32),
+        out_shape=jax.ShapeDtypeStruct(shape, jnp.float32 if accs else back.dtype),
         in_specs=[whole(SMEM), whole(), *[whole(pltpu.HBM)] * len(accs)],
         out_specs=whole(),
         scratch_shapes=[*more, *[VMEM((ns, (AB + 1) * BL), jnp.float32)] * CHAINS],
@@ -415,7 +424,7 @@
     back, acc = lax.optimization_barrier((back, acc))
     away = lax.ppermute(collect(asked, back, None, True, cells), axes, to_owner)
     own = collect(asked, back, acc, False, cells)
-    return own + away, of, lf
+    return own + away.astype(jnp.float32), of, lf
 
 
 def solution(mesh):

time: 74.5 us -> 74.4 us (level)
  no operation moved by 1% of the time
where the time goes in v6:
time: 74.4 us; the launch traced here: 73.9 us
  waiting for transfers between devices  25.1 us (34%)
  starting transfers between devices  24.7 us (33%)
  Pallas kernels  20.7 us (28%)
  local copies, waits for them, and re-layouts  1.87 us (3%)
  between operations  0.82 us (1%)
    all_to_all x1, waiting for transfers between devices, per_device(): got = exchange(serve(asked, held, cells))  15.9 us
    all_to_all x1, starting transfers between devices, per_device(): asked = exchange(asking)  8.95 us
    ppermute x1, starting transfers between devices, per_device(): away = lax.ppermute(collect(asked, back, None, True, cells), axes, to_owner)  5.48 us
    pallas_call x1, Pallas kernels, far(): pl.pallas_call(far_kernel, out_shape=(jax.ShapeDtypeStruct(os.shape, f32)...  5.3 us
    all_to_all x1, waiting for transfers between devices, per_device(): asked = exchange(asking)  5.12 us
    all_to_all x1, starting transfers between devices, per_device(): back = exchange(send)  5.09 us
    pallas_call x1, Pallas kernels, near_back(): pl.pallas_call(near_back_kernel, grid=(STEPS,), out_shape=jax.ShapeDtypeS...  4.86 us
    all_to_all x1, waiting for transfers between devices, per_device(): back = exchange(send)  4.14 us
  transfers between devices with their start and end apart: 5, of which 3 were waited for; matrix products, arithmetic and copies ran while one was open for 0% of the time, Pallas kernels for 16%

profile of v6, /device:TPU:1, one launch (start us, length us, event | category | flops | bytes accessed | tf_op | source)
XLA Modules:
  0.0 73.9 jit_solution(9049697044684451984)
XLA Ops:
  0.6 1.5 %collective-permute-start = (bf16[24,4096]{1,0:T(8,128)(2,1)}, bf16[24,4096]{1,0:T(8,128)(2,1)S(1)}, u32[]{:S(2)}, u32[]{:S(2)}) collective-permute-start(bf16[24,4096]{1,0:T(8,128)(2,1)} %own_ref.1), channel_id=1, source_target_pairs={{0,112},{1,113},{2,114},{3,115},{4,116},{5,117},{6,118},{7,119},{8... | collective-permute-start | bytes 589832 | tf_op jit(solution)/shard_map/ppermute | solution.py:411
  2.1 1.8 %requests.1 = (s32[16,128]{1,0:T(8,128)}, s32[8,128]{1,0:T(8,128)}) custom-call(s32[2,64]{1,0:T(2,128)} %bitcast.20, s32[2,16]{1,0:T(2,128)} %bitcast.21), custom_call_target="tpu_custom_call" | custom-call | tf_op jit(solution)/shard_map/requests/pallas_call | solution.py:80
  3.9 8.9 %all-to-all-start = ((s32[16,1,128]{2,1,0:T(1,128)}), s32[16,1,128]{2,1,0:T(1,128)S(1)}, u32[]{:S(2)}, u32[]{:S(2)}) async-start(s32[16,1,128]{2,1,0:T(1,128)} %bitcast.19), calls=%async_computation | async-start | bytes 16384 | tf_op jit(solution)/shard_map/all_to_all | solution.py:413
  12.9 0.0 collective-permute-done.near_ref
  12.9 0.0 copy-start.3
  12.9 0.9 %copy-done.3 = bf16[24,4096]{1,0:T(8,128)(2,1)S(1)} copy-done((bf16[24,4096]{1,0:T(8,128)(2,1)S(1)}, bf16[24,4096]{1,0:T(8,128)(2,1)}, u32[]{:S(2)}) %copy-start.3) | copy-done | bytes 196632
  13.8 0.3 hold.1.both.f_ref
  14.1 5.1 %all-to-all-done = s32[16,1,128]{2,1,0:T(1,128)S(1)} async-done(((s32[16,1,128]{2,1,0:T(1,128)}), s32[16,1,128]{2,1,0:T(1,128)S(1)}, u32[]{:S(2)}, u32[]{:S(2)}) %all-to-all-start) | async-done | bytes 8224 | tf_op jit(solution)/shard_map/all_to_all | solution.py:413
  19.2 0.0 copy-start.8
  19.2 0.0 copy-start.9
  19.2 2.1 %serve.1 = bf16[240,24,128]{2,1,0:T(8,128)(2,1)} custom-call(s32[16,128]{1,0:T(8,128)S(1)} %bitcast.10, bf16[24,8192]{1,0:T(8,128)(2,1)S(1)} %hold.1.both.f_ref), custom_call_target="tpu_custom_call" | custom-call | tf_op jit(solution)/shard_map/serve/pallas_call | solution.py:135
  21.3 3.7 %all-to-all-start.1 = ((bf16[240,24,128]{2,1,0:T(8,128)(2,1)}), bf16[240,24,128]{2,1,0:T(8,128)(2,1)S(1)}, u32[]{:S(2)}, u32[]{:S(2)}) async-start(bf16[240,24,128]{2,1,0:T(8,128)(2,1)} %serve.1), calls=%async_computation.1 | async-start | bytes 2949120 | tf_op jit(solution)/shard_map/all_to_all | solution.py:415
  25.0 0.0 copy-done.8
  25.0 0.0 copy-done.9
  25.0 0.0 copy-start.1
  25.0 0.0 copy-start.2
  25.0 0.0 copy-start.4
  25.1 0.0 copy-start.5
  25.1 0.0 copy-start.6
  25.1 0.0 copy-start.7
  25.1 3.8 %near_mix.1.near = f32[80,24,128]{2,1,0:T(8,128)S(1)} custom-call(s32[2,64]{1,0:T(2,128)S(1)} %bitcast.16, s32[2,16]{1,0:T(2,128)S(1)} %bitcast.18, bf16[24,8192]{1,0:T(8,128)(2,1)S(1)} %hold.1.both.f_ref, bf16[64,4,128,128]{3,2,1,0:T(8,128)(2,1)} %ot_ref.3, bf16[16,4,128,128]{3,2,1,0:T(8,128)(2,1)} %lt_ref.3), custom_call_target="tpu_custom_call" | custom-call | flops 671088640 | bytes 5242880 | tf_op jit(solution)/shard_map/near_mix/pallas_call | solution.py:173
  28.9 15.9 %all-to-all-done.1.got_ref = bf16[240,24,128]{2,1,0:T(8,128)(2,1)S(1)} async-done(((bf16[240,24,128]{2,1,0:T(8,128)(2,1)}), bf16[240,24,128]{2,1,0:T(8,128)(2,1)S(1)}, u32[]{:S(2)}, u32[]{:S(2)}) %all-to-all-start.1) | async-done | bytes 1474592 | tf_op jit(solution)/shard_map/all_to_all | solution.py:415
  44.8 0.0 copy-done.1
  44.8 0.0 copy-done.2
  44.8 0.0 copy-done.4
  44.8 0.0 copy-done.5
  44.8 0.0 copy-done.6
  44.8 0.0 copy-done.7
  44.8 5.3 %far.1 = (f32[8,8192]{1,0:T(8,128)}, f32[8,2048]{1,0:T(8,128)}, bf16[240,8,128]{2,1,0:T(8,128)(2,1)}) custom-call(s32[8,128]{1,0:T(8,128)S(1)} %copy-done.7, bf16[240,24,128]{2,1,0:T(8,128)(2,1)S(1)} %all-to-all-done.1.got_ref, f32[80,24,128]{2,1,0:T(8,128)S(1)} %near_mix.1.near, f32[8,8192]{1,0:T(8,128)S(1)} %copy-done.1, f32[8,8192]{1,0:T(8,128)S(1)} %copy-done.2, ...), custom_call_target="tpu_custom_call" | custom-call | tf_op jit(solution)/shard_map/far/pallas_call | solution.py:275
  50.1 5.1 %all-to-all-start.2 = ((bf16[240,8,128]{2,1,0:T(8,128)(2,1)}), bf16[240,8,128]{2,1,0:T(8,128)(2,1)S(1)}, u32[]{:S(2)}, u32[]{:S(2)}) async-start(bf16[240,8,128]{2,1,0:T(8,128)(2,1)} %get-tuple-element.12), calls=%async_computation.2 | async-start | bytes 983040 | tf_op jit(solution)/shard_map/all_to_all | solution.py:422
  55.2 4.9 %near_back.1.refs_0_ = f32[8,4096]{1,0:T(8,128)} custom-call(s32[2,64]{1,0:T(2,128)} %bitcast.15, s32[2,16]{1,0:T(2,128)} %bitcast.17, f32[8,8192]{1,0:T(8,128)} %get-tuple-element.8.of_ref, f32[8,2048]{1,0:T(8,128)} %get-tuple-element.9.lf_ref, bf16[64,4,128,128]{3,2,1,0:T(8,128)(2,1)} %ot_ref.3, bf16[16,4,128,128]{3,2,1,0:T(8,128)(2,1)} %lt_ref.3), custom_call_target="tpu_custom_call" | custom-call | flops 671088640 | bytes 5242880 | tf_op jit(solution)/shard_map/near_back/pallas_call | solution.py:318
  60.1 4.1 %all-to-all-done.2.back_ref = bf16[240,8,128]{2,1,0:T(8,128)(2,1)S(1)} async-done(((bf16[240,8,128]{2,1,0:T(8,128)(2,1)}), bf16[240,8,128]{2,1,0:T(8,128)(2,1)S(1)}, u32[]{:S(2)}, u32[]{:S(2)}) %all-to-all-start.2) | async-done | bytes 491552 | tf_op jit(solution)/shard_map/all_to_all | solution.py:422
  64.2 1.2 %collect_far.1 = bf16[8,4096]{1,0:T(8,128)(2,1)S(1)} custom-call(s32[16,128]{1,0:T(8,128)S(1)} %bitcast.11, bf16[240,8,128]{2,1,0:T(8,128)(2,1)S(1)} %all-to-all-done.2.back_ref), custom_call_target="tpu_custom_call" | custom-call | flops 1048576 | bytes 4194304 | tf_op jit(solution)/shard_map/collect_far/pallas_call | solution.py:381
  65.4 5.5 %collective-permute-start.1 = (bf16[8,4096]{1,0:T(8,128)(2,1)S(1)}, bf16[8,4096]{1,0:T(8,128)(2,1)S(1)}, u32[]{:S(2)}, u32[]{:S(2)}) collective-permute-start(bf16[8,4096]{1,0:T(8,128)(2,1)S(1)} %collect_far.1), channel_id=1, source_target_pairs={{112,0},{113,1},{114,2},{115,3},{116,4},{117,5},{118,6},{119,7},{2... | collective-permute-start | bytes 196616 | tf_op jit(solution)/shard_map/ppermute | solution.py:425
  70.9 0.0 copy-start
  70.9 0.9 %copy-done = f32[8,4096]{1,0:T(8,128)S(1)} copy-done((f32[8,4096]{1,0:T(8,128)S(1)}, f32[8,4096]{1,0:T(8,128)}, u32[]{:S(2)}) %copy-start) | copy-done | bytes 131096
  71.8 1.4 %collect_own.1 = f32[8,4096]{1,0:T(8,128)S(1)} custom-call(s32[16,128]{1,0:T(8,128)S(1)} %bitcast.12, bf16[240,8,128]{2,1,0:T(8,128)(2,1)S(1)} %all-to-all-done.2.back_ref, f32[8,4096]{1,0:T(8,128)S(1)} %copy-done), custom_call_target="tpu_custom_call" | custom-call | flops 1048576 | bytes 4194304 | tf_op jit(solution)/shard_map/collect_own/pallas_call | solution.py:381
  73.2 0.0 collective-permute-done.1
  73.2 0.7 convert_add_fusion
Async XLA Ops:
  0.6 12.2 %collective-permute-start = (bf16[24,4096]{1,0:T(8,128)(2,1)}, bf16[24,4096]{1,0:T(8,128)(2,1)S(1)}, u32[]{:S(2)}, u32[]{:S(2)}) collective-permute-start(bf16[24,4096]{1,0:T(8,128)(2,1)} %own_ref.1), channel_id=1, source_target_pairs={{0,112},{1,113},{2,114},{3,115},{4,116},{5,117},{6,118},{7,119},{8... | collective-permute-start | bytes 589832 | tf_op jit(solution)/shard_map/ppermute | solution.py:411
  3.9 15.3 %all-to-all-start = ((s32[16,1,128]{2,1,0:T(1,128)}), s32[16,1,128]{2,1,0:T(1,128)S(1)}, u32[]{:S(2)}, u32[]{:S(2)}) async-start(s32[16,1,128]{2,1,0:T(1,128)} %bitcast.19), calls=%async_computation | async-start | bytes 16384 | tf_op jit(solution)/shard_map/all_to_all | solution.py:413
  12.9 0.9 %copy-start.3 = (bf16[24,4096]{1,0:T(8,128)(2,1)S(1)}, bf16[24,4096]{1,0:T(8,128)(2,1)}, u32[]{:S(2)}) copy-start(bf16[24,4096]{1,0:T(8,128)(2,1)} %own_ref.1) | copy-start | bytes 589828
  19.2 5.8 %copy-start.8 = (s32[64,2]{0,1:T(2,128)S(1)}, s32[64,2]{0,1:T(2,128)}, u32[]{:S(2)}) copy-start(s32[64,2]{0,1:T(2,128)} %param.19) | copy-start | bytes 1540
  19.2 5.8 %copy-start.9 = (s32[16,2]{0,1:T(2,128)S(1)}, s32[16,2]{0,1:T(2,128)}, u32[]{:S(2)}) copy-start(s32[16,2]{0,1:T(2,128)} %param.22) | copy-start | bytes 388
  21.3 23.5 %all-to-all-start.1 = ((bf16[240,24,128]{2,1,0:T(8,128)(2,1)}), bf16[240,24,128]{2,1,0:T(8,128)(2,1)S(1)}, u32[]{:S(2)}, u32[]{:S(2)}) async-start(bf16[240,24,128]{2,1,0:T(8,128)(2,1)} %serve.1), calls=%async_computation.1 | async-start | bytes 2949120 | tf_op jit(solution)/shard_map/all_to_all | solution.py:415
  25.0 19.7 %copy-start.1 = (f32[8,8192]{1,0:T(8,128)S(1)}, f32[8,8192]{1,0:T(8,128)}, u32[]{:S(2)}) copy-start(f32[8,8192]{1,0:T(8,128)} %osv.1) | copy-start | bytes 786436
  25.0 19.7 %copy-start.2 = (f32[8,8192]{1,0:T(8,128)S(1)}, f32[8,8192]{1,0:T(8,128)}, u32[]{:S(2)}) copy-start(f32[8,8192]{1,0:T(8,128)} %isv.1) | copy-start | bytes 786436
  25.0 19.7 %copy-start.4 = (f32[8,2048]{1,0:T(8,128)S(1)}, f32[8,2048]{1,0:T(8,128)}, u32[]{:S(2)}) copy-start(f32[8,2048]{1,0:T(8,128)} %ls.1) | copy-start | bytes 196612
  25.1 19.7 %copy-start.5 = (s32[8192]{0:T(1024)S(1)}, s32[8192]{0:T(1024)}, u32[]{:S(2)}) copy-start(s32[8192]{0:T(1024)} %param.15) | copy-start | bytes 98308
  25.1 19.7 %copy-start.6 = (s32[2048]{0:T(1024)S(1)}, s32[2048]{0:T(1024)}, u32[]{:S(2)}) copy-start(s32[2048]{0:T(1024)} %param.17) | copy-start | bytes 24580
  25.1 19.7 %copy-start.7 = (s32[8,128]{1,0:T(8,128)S(1)}, s32[8,128]{1,0:T(8,128)}, u32[]{:S(2)}) copy-start(s32[8,128]{1,0:T(8,128)} %get-tuple-element.11.slot_ref) | copy-start | bytes 12292
  50.1 14.1 %all-to-all-start.2 = ((bf16[240,8,128]{2,1,0:T(8,128)(2,1)}), bf16[240,8,128]{2,1,0:T(8,128)(2,1)S(1)}, u32[]{:S(2)}, u32[]{:S(2)}) async-start(bf16[240,8,128]{2,1,0:T(8,128)(2,1)} %get-tuple-element.12), calls=%async_computation.2 | async-start | bytes 983040 | tf_op jit(solution)/shard_map/all_to_all | solution.py:422
  65.4 7.8 %collective-permute-start.1 = (bf16[8,4096]{1,0:T(8,128)(2,1)S(1)}, bf16[8,4096]{1,0:T(8,128)(2,1)S(1)}, u32[]{:S(2)}, u32[]{:S(2)}) collective-permute-start(bf16[8,4096]{1,0:T(8,128)(2,1)S(1)} %collect_far.1), channel_id=1, source_target_pairs={{112,0},{113,1},{114,2},{115,3},{116,4},{117,5},{118,6},{119,7},{2... | collective-permute-start | bytes 196616 | tf_op jit(solution)/shard_map/ppermute | solution.py:425
  70.9 0.9 %copy-start = (f32[8,4096]{1,0:T(8,128)S(1)}, f32[8,4096]{1,0:T(8,128)}, u32[]{:S(2)}) copy-start(f32[8,4096]{1,0:T(8,128)} %near_back.1.refs_0_) | copy-start | bytes 393220

commit v7 on v6

--- a/solution.py
+++ b/solution.py
@@ -199,8 +199,8 @@
 
 
 def far_kernel(
-    slot_ref, got_ref, near, osv, isv, il, ls, ll, ot_hbm, lt_hbm, of_hbm, lf_hbm, send_hbm,
-    ot, lt, of, lf, send, in_sems, out_sems,
+    slot_hbm, got_ref, near, osv, isv, il, ls, ll, ot_hbm, lt_hbm, of_hbm, lf_hbm, send_hbm,
+    slot_ref, ot, lt, of, lf, send, in_sems, out_sems, slot_sem,
 ):
     ob, lb = ot.shape[0], lt.shape[0]
     no, nl = ob // STEPS, lb // STEPS
@@ -220,7 +220,11 @@
             outs.append(
                 pltpu.make_async_copy(flux.at[:, some], flux_hbm.at[:, some], out_sems.at[len(outs)])
             )
+        if part is parts[0]:
+            load = pltpu.make_async_copy(slot_hbm, slot_ref, slot_sem)
+            load.start()
     send[...] = jnp.zeros(send.shape, send.dtype)
+    load.wait()
     waits, sends = iter(ins), iter(outs)
     for part in parts:
         for _ in part:
@@ -279,9 +283,10 @@
             jax.ShapeDtypeStruct(ls.shape, f32),
             jax.ShapeDtypeStruct(back, jnp.bfloat16),
         ),
-        in_specs=[whole(SMEM), *[whole()] * 7, *[whole(pl.ANY)] * 2],
+        in_specs=[whole(pl.ANY), *[whole()] * 7, *[whole(pl.ANY)] * 2],
         out_specs=[whole(pltpu.HBM)] * 3,
         scratch_shapes=[
+            SMEM(slots.shape, slots.dtype),
             VMEM((ot.shape[0], KR, BL, BL), ot.dtype),
             VMEM((lt.shape[0], KR, BL, BL), lt.dtype),
             VMEM(os.shape, f32),
@@ -289,6 +294,7 @@
             VMEM(back, jnp.bfloat16),
             pltpu.SemaphoreType.DMA((count,)),
             pltpu.SemaphoreType.DMA((count + 1,)),
+            pltpu.SemaphoreType.DMA(()),
         ],
         compiler_params=pltpu.CompilerParams(vmem_limit_bytes=50 << 20),
         name="far",
@@ -337,7 +343,10 @@
     )(ol, ll, of, lf, ot, lt)
 
 
-def collect_kernel(cells, neighbours, asked_ref, back_ref, *refs):
+def collect_kernel(cells, neighbours, asked_hbm, back_ref, *refs):
+    asked_ref, asked_sem, *refs = refs[-2:] + refs[:-2]
+    ask = pltpu.make_async_copy(asked_hbm, asked_ref, asked_sem)
+    ask.start()
     if neighbours:
         out_ref, *totals = refs
     else:
@@ -349,6 +358,7 @@
     half = cells // 2
     for total in totals[-CHAINS:]:
         total[...] = jnp.zeros(total.shape, jnp.float32)
+    ask.wait()
 
     def body(c, _):
         far_one = jnp.logical_or(c <= cell - half, c > cell + half)
@@ -381,9 +391,14 @@
     return pl.pallas_call(
         functools.partial(collect_kernel, cells, neighbours),
         out_shape=jax.ShapeDtypeStruct(shape, jnp.float32 if accs else back.dtype),
-        in_specs=[whole(SMEM), whole(), *[whole(pltpu.HBM)] * len(accs)],
+        in_specs=[whole(pl.ANY), whole(), *[whole(pltpu.HBM)] * len(accs)],
         out_specs=whole(),
-        scratch_shapes=[*more, *[VMEM((ns, (AB + 1) * BL), jnp.float32)] * CHAINS],
+        scratch_shapes=[
+            *more,
+            *[VMEM((ns, (AB + 1) * BL), jnp.float32)] * CHAINS,
+            SMEM(asked.shape, asked.dtype),
+            pltpu.SemaphoreType.DMA(()),
+        ],
         compiler_params=pltpu.CompilerParams(vmem_limit_bytes=SMALL),
         cost_estimate=pl.CostEstimate(
             flops=1 << 20, bytes_accessed=4 << 20, transcendentals=0

time: 74.4 us -> 73.6 us (0.989)
  Pallas kernels: 20.7 us -> 19.9 us
where the time goes in v7:
time: 73.6 us; the launch traced here: 73.1 us
  waiting for transfers between devices  25.1 us (34%)
  starting transfers between devices  24.7 us (34%)
  Pallas kernels  19.9 us (27%)
  local copies, waits for them, and re-layouts  1.87 us (3%)
  between operations  0.82 us (1%)
    all_to_all x1, waiting for transfers between devices, per_device(): got = exchange(serve(asked, held, cells))  15.9 us
    all_to_all x1, starting transfers between devices, per_device(): asked = exchange(asking)  8.95 us
    ppermute x1, starting transfers between devices, per_device(): away = lax.ppermute(collect(asked, back, None, True, cells), axes, to_owner)  5.49 us
    all_to_all x1, waiting for transfers between devices, per_device(): asked = exchange(asking)  5.12 us
    all_to_all x1, starting transfers between devices, per_device(): back = exchange(send)  5.08 us
    pallas_call x1, Pallas kernels, near_back(): pl.pallas_call(near_back_kernel, grid=(STEPS,), out_shape=jax.ShapeDtypeS...  4.86 us
    pallas_call x1, Pallas kernels, far(): pl.pallas_call(far_kernel, out_shape=(jax.ShapeDtypeStruct(os.shape, f32)...  4.71 us
    all_to_all x1, waiting for transfers between devices, per_device(): back = exchange(send)  4.13 us
  transfers between devices with their start and end apart: 5, of which 3 were waited for; matrix products, arithmetic and copies ran while one was open for 0% of the time, Pallas kernels for 16%

profile of v7, /device:TPU:1, one launch (start us, length us, event | category | flops | bytes accessed | tf_op | source)
XLA Modules:
  0.0 73.1 jit_solution(17834887021002256515)
XLA Ops:
  0.6 1.5 %collective-permute-start = (bf16[24,4096]{1,0:T(8,128)(2,1)}, bf16[24,4096]{1,0:T(8,128)(2,1)S(1)}, u32[]{:S(2)}, u32[]{:S(2)}) collective-permute-start(bf16[24,4096]{1,0:T(8,128)(2,1)} %own_ref.1), channel_id=1, source_target_pairs={{0,112},{1,113},{2,114},{3,115},{4,116},{5,117},{6,118},{7,119},{8... | collective-permute-start | bytes 589832 | tf_op jit(solution)/shard_map/ppermute | solution.py:426
  2.1 1.8 %requests.1 = (s32[16,128]{1,0:T(8,128)}, s32[8,128]{1,0:T(8,128)}) custom-call(s32[2,64]{1,0:T(2,128)} %bitcast.20, s32[2,16]{1,0:T(2,128)} %bitcast.21), custom_call_target="tpu_custom_call" | custom-call | tf_op jit(solution)/shard_map/requests/pallas_call | solution.py:80
  3.9 8.9 %all-to-all-start = ((s32[16,1,128]{2,1,0:T(1,128)}), s32[16,1,128]{2,1,0:T(1,128)S(1)}, u32[]{:S(2)}, u32[]{:S(2)}) async-start(s32[16,1,128]{2,1,0:T(1,128)} %bitcast.19), calls=%async_computation | async-start | bytes 16384 | tf_op jit(solution)/shard_map/all_to_all | solution.py:428
  12.9 0.0 collective-permute-done.near_ref
  12.9 0.0 copy-start.3
  12.9 0.9 %copy-done.3 = bf16[24,4096]{1,0:T(8,128)(2,1)S(1)} copy-done((bf16[24,4096]{1,0:T(8,128)(2,1)S(1)}, bf16[24,4096]{1,0:T(8,128)(2,1)}, u32[]{:S(2)}) %copy-start.3) | copy-done | bytes 196632
  13.8 0.3 hold.1.both.f_ref
  14.1 5.1 %all-to-all-done = s32[16,1,128]{2,1,0:T(1,128)S(1)} async-done(((s32[16,1,128]{2,1,0:T(1,128)}), s32[16,1,128]{2,1,0:T(1,128)S(1)}, u32[]{:S(2)}, u32[]{:S(2)}) %all-to-all-start) | async-done | bytes 8224 | tf_op jit(solution)/shard_map/all_to_all | solution.py:428
  19.2 0.0 copy-start.8
  19.2 0.0 copy-start.9
  19.2 2.1 %serve.1 = bf16[240,24,128]{2,1,0:T(8,128)(2,1)} custom-call(s32[16,128]{1,0:T(8,128)S(1)} %bitcast.10, bf16[24,8192]{1,0:T(8,128)(2,1)S(1)} %hold.1.both.f_ref), custom_call_target="tpu_custom_call" | custom-call | tf_op jit(solution)/shard_map/serve/pallas_call | solution.py:135
  21.3 3.7 %all-to-all-start.1 = ((bf16[240,24,128]{2,1,0:T(8,128)(2,1)}), bf16[240,24,128]{2,1,0:T(8,128)(2,1)S(1)}, u32[]{:S(2)}, u32[]{:S(2)}) async-start(bf16[240,24,128]{2,1,0:T(8,128)(2,1)} %serve.1), calls=%async_computation.1 | async-start | bytes 2949120 | tf_op jit(solution)/shard_map/all_to_all | solution.py:430
  25.0 0.0 copy-done.8
  25.0 0.0 copy-done.9
  25.0 0.0 copy-start.1
  25.0 0.0 copy-start.2
  25.0 0.0 copy-start.4
  25.1 0.0 copy-start.5
  25.1 0.0 copy-start.6
  25.1 0.0 copy-start.7
  25.1 3.8 %near_mix.1.near = f32[80,24,128]{2,1,0:T(8,128)S(1)} custom-call(s32[2,64]{1,0:T(2,128)S(1)} %bitcast.16, s32[2,16]{1,0:T(2,128)S(1)} %bitcast.18, bf16[24,8192]{1,0:T(8,128)(2,1)S(1)} %hold.1.both.f_ref, bf16[64,4,128,128]{3,2,1,0:T(8,128)(2,1)} %ot_ref.3, bf16[16,4,128,128]{3,2,1,0:T(8,128)(2,1)} %lt_ref.3), custom_call_target="tpu_custom_call" | custom-call | flops 671088640 | bytes 5242880 | tf_op jit(solution)/shard_map/near_mix/pallas_call | solution.py:173
  28.9 15.9 %all-to-all-done.1.got_ref = bf16[240,24,128]{2,1,0:T(8,128)(2,1)S(1)} async-done(((bf16[240,24,128]{2,1,0:T(8,128)(2,1)}), bf16[240,24,128]{2,1,0:T(8,128)(2,1)S(1)}, u32[]{:S(2)}, u32[]{:S(2)}) %all-to-all-start.1) | async-done | bytes 1474592 | tf_op jit(solution)/shard_map/all_to_all | solution.py:430
  44.8 0.0 copy-done.1
  44.8 0.0 copy-done.2
  44.8 0.0 copy-done.4
  44.8 0.0 copy-done.5
  44.8 0.0 copy-done.6
  44.8 0.0 copy-done.7
  44.8 4.7 %far.1 = (f32[8,8192]{1,0:T(8,128)}, f32[8,2048]{1,0:T(8,128)}, bf16[240,8,128]{2,1,0:T(8,128)(2,1)}) custom-call(s32[8,128]{1,0:T(8,128)S(1)} %copy-done.7, bf16[240,24,128]{2,1,0:T(8,128)(2,1)S(1)} %all-to-all-done.1.got_ref, f32[80,24,128]{2,1,0:T(8,128)S(1)} %near_mix.1.near, f32[8,8192]{1,0:T(8,128)S(1)} %copy-done.1, f32[8,8192]{1,0:T(8,128)S(1)} %copy-done.2, ...), custom_call_target="tpu_custom_call" | custom-call | tf_op jit(solution)/shard_map/far/pallas_call | solution.py:279
  49.5 5.1 %all-to-all-start.2 = ((bf16[240,8,128]{2,1,0:T(8,128)(2,1)}), bf16[240,8,128]{2,1,0:T(8,128)(2,1)S(1)}, u32[]{:S(2)}, u32[]{:S(2)}) async-start(bf16[240,8,128]{2,1,0:T(8,128)(2,1)} %get-tuple-element.12), calls=%async_computation.2 | async-start | bytes 983040 | tf_op jit(solution)/shard_map/all_to_all | solution.py:437
  54.6 4.9 %near_back.1.refs_0_ = f32[8,4096]{1,0:T(8,128)} custom-call(s32[2,64]{1,0:T(2,128)} %bitcast.15, s32[2,16]{1,0:T(2,128)} %bitcast.17, f32[8,8192]{1,0:T(8,128)} %get-tuple-element.8.of_ref, f32[8,2048]{1,0:T(8,128)} %get-tuple-element.9.lf_ref, bf16[64,4,128,128]{3,2,1,0:T(8,128)(2,1)} %ot_ref.3, bf16[16,4,128,128]{3,2,1,0:T(8,128)(2,1)} %lt_ref.3), custom_call_target="tpu_custom_call" | custom-call | flops 671088640 | bytes 5242880 | tf_op jit(solution)/shard_map/near_back/pallas_call | solution.py:324
  59.5 4.1 %all-to-all-done.2.back_ref = bf16[240,8,128]{2,1,0:T(8,128)(2,1)S(1)} async-done(((bf16[240,8,128]{2,1,0:T(8,128)(2,1)}), bf16[240,8,128]{2,1,0:T(8,128)(2,1)S(1)}, u32[]{:S(2)}, u32[]{:S(2)}) %all-to-all-start.2) | async-done | bytes 491552 | tf_op jit(solution)/shard_map/all_to_all | solution.py:437
  63.6 1.1 %collect_far.1 = bf16[8,4096]{1,0:T(8,128)(2,1)S(1)} custom-call(s32[16,128]{1,0:T(8,128)S(1)} %bitcast.11, bf16[240,8,128]{2,1,0:T(8,128)(2,1)S(1)} %all-to-all-done.2.back_ref), custom_call_target="tpu_custom_call" | custom-call | flops 1048576 | bytes 4194304 | tf_op jit(solution)/shard_map/collect_far/pallas_call | solution.py:391
  64.7 5.5 %collective-permute-start.1 = (bf16[8,4096]{1,0:T(8,128)(2,1)S(1)}, bf16[8,4096]{1,0:T(8,128)(2,1)S(1)}, u32[]{:S(2)}, u32[]{:S(2)}) collective-permute-start(bf16[8,4096]{1,0:T(8,128)(2,1)S(1)} %collect_far.1), channel_id=1, source_target_pairs={{112,0},{113,1},{114,2},{115,3},{116,4},{117,5},{118,6},{119,7},{2... | collective-permute-start | bytes 196616 | tf_op jit(solution)/shard_map/ppermute | solution.py:440
  70.2 0.0 copy-start
  70.2 0.9 %copy-done = f32[8,4096]{1,0:T(8,128)S(1)} copy-done((f32[8,4096]{1,0:T(8,128)S(1)}, f32[8,4096]{1,0:T(8,128)}, u32[]{:S(2)}) %copy-start) | copy-done | bytes 131096
  71.1 1.2 %collect_own.1 = f32[8,4096]{1,0:T(8,128)S(1)} custom-call(s32[16,128]{1,0:T(8,128)S(1)} %bitcast.12, bf16[240,8,128]{2,1,0:T(8,128)(2,1)S(1)} %all-to-all-done.2.back_ref, f32[8,4096]{1,0:T(8,128)S(1)} %copy-done), custom_call_target="tpu_custom_call" | custom-call | flops 1048576 | bytes 4194304 | tf_op jit(solution)/shard_map/collect_own/pallas_call | solution.py:391
  72.4 0.0 collective-permute-done.1
  72.4 0.7 convert_add_fusion
Async XLA Ops:
  0.6 12.2 %collective-permute-start = (bf16[24,4096]{1,0:T(8,128)(2,1)}, bf16[24,4096]{1,0:T(8,128)(2,1)S(1)}, u32[]{:S(2)}, u32[]{:S(2)}) collective-permute-start(bf16[24,4096]{1,0:T(8,128)(2,1)} %own_ref.1), channel_id=1, source_target_pairs={{0,112},{1,113},{2,114},{3,115},{4,116},{5,117},{6,118},{7,119},{8... | collective-permute-start | bytes 589832 | tf_op jit(solution)/shard_map/ppermute | solution.py:426
  3.9 15.3 %all-to-all-start = ((s32[16,1,128]{2,1,0:T(1,128)}), s32[16,1,128]{2,1,0:T(1,128)S(1)}, u32[]{:S(2)}, u32[]{:S(2)}) async-start(s32[16,1,128]{2,1,0:T(1,128)} %bitcast.19), calls=%async_computation | async-start | bytes 16384 | tf_op jit(solution)/shard_map/all_to_all | solution.py:428
  12.9 0.9 %copy-start.3 = (bf16[24,4096]{1,0:T(8,128)(2,1)S(1)}, bf16[24,4096]{1,0:T(8,128)(2,1)}, u32[]{:S(2)}) copy-start(bf16[24,4096]{1,0:T(8,128)(2,1)} %own_ref.1) | copy-start | bytes 589828
  19.2 5.8 %copy-start.8 = (s32[64,2]{0,1:T(2,128)S(1)}, s32[64,2]{0,1:T(2,128)}, u32[]{:S(2)}) copy-start(s32[64,2]{0,1:T(2,128)} %param.19) | copy-start | bytes 1540
  19.2 5.8 %copy-start.9 = (s32[16,2]{0,1:T(2,128)S(1)}, s32[16,2]{0,1:T(2,128)}, u32[]{:S(2)}) copy-start(s32[16,2]{0,1:T(2,128)} %param.22) | copy-start | bytes 388
  21.3 23.5 %all-to-all-start.1 = ((bf16[240,24,128]{2,1,0:T(8,128)(2,1)}), bf16[240,24,128]{2,1,0:T(8,128)(2,1)S(1)}, u32[]{:S(2)}, u32[]{:S(2)}) async-start(bf16[240,24,128]{2,1,0:T(8,128)(2,1)} %serve.1), calls=%async_computation.1 | async-start | bytes 2949120 | tf_op jit(solution)/shard_map/all_to_all | solution.py:430
  25.0 19.7 %copy-start.1 = (f32[8,8192]{1,0:T(8,128)S(1)}, f32[8,8192]{1,0:T(8,128)}, u32[]{:S(2)}) copy-start(f32[8,8192]{1,0:T(8,128)} %osv.1) | copy-start | bytes 786436
  25.0 19.7 %copy-start.2 = (f32[8,8192]{1,0:T(8,128)S(1)}, f32[8,8192]{1,0:T(8,128)}, u32[]{:S(2)}) copy-start(f32[8,8192]{1,0:T(8,128)} %isv.1) | copy-start | bytes 786436
  25.0 19.7 %copy-start.4 = (f32[8,2048]{1,0:T(8,128)S(1)}, f32[8,2048]{1,0:T(8,128)}, u32[]{:S(2)}) copy-start(f32[8,2048]{1,0:T(8,128)} %ls.1) | copy-start | bytes 196612
  25.1 19.7 %copy-start.5 = (s32[8192]{0:T(1024)S(1)}, s32[8192]{0:T(1024)}, u32[]{:S(2)}) copy-start(s32[8192]{0:T(1024)} %param.15) | copy-start | bytes 98308
  25.1 19.7 %copy-start.6 = (s32[2048]{0:T(1024)S(1)}, s32[2048]{0:T(1024)}, u32[]{:S(2)}) copy-start(s32[2048]{0:T(1024)} %param.17) | copy-start | bytes 24580
  25.1 19.7 %copy-start.7 = (s32[8,128]{1,0:T(8,128)S(1)}, s32[8,128]{1,0:T(8,128)}, u32[]{:S(2)}) copy-start(s32[8,128]{1,0:T(8,128)} %get-tuple-element.11.slot_hbm) | copy-start | bytes 12292
  49.5 14.1 %all-to-all-start.2 = ((bf16[240,8,128]{2,1,0:T(8,128)(2,1)}), bf16[240,8,128]{2,1,0:T(8,128)(2,1)S(1)}, u32[]{:S(2)}, u32[]{:S(2)}) async-start(bf16[240,8,128]{2,1,0:T(8,128)(2,1)} %get-tuple-element.12), calls=%async_computation.2 | async-start | bytes 983040 | tf_op jit(solution)/shard_map/all_to_all | solution.py:437
  64.7 7.6 %collective-permute-start.1 = (bf16[8,4096]{1,0:T(8,128)(2,1)S(1)}, bf16[8,4096]{1,0:T(8,128)(2,1)S(1)}, u32[]{:S(2)}, u32[]{:S(2)}) collective-permute-start(bf16[8,4096]{1,0:T(8,128)(2,1)S(1)} %collect_far.1), channel_id=1, source_target_pairs={{112,0},{113,1},{114,2},{115,3},{116,4},{117,5},{118,6},{119,7},{2... | collective-permute-start | bytes 196616 | tf_op jit(solution)/shard_map/ppermute | solution.py:440
  70.2 0.9 %copy-start = (f32[8,4096]{1,0:T(8,128)S(1)}, f32[8,4096]{1,0:T(8,128)}, u32[]{:S(2)}) copy-start(f32[8,4096]{1,0:T(8,128)} %near_back.1.refs_0_) | copy-start | bytes 393220

commit v8 on v7

--- a/solution.py
+++ b/solution.py
@@ -30,6 +30,10 @@
 
 def lanes(i):
     return pl.ds(pl.multiple_of(i * BL, BL), BL)
+
+
+def lanes_from(first):
+    return pl.ds(pl.multiple_of(first, BL), BL)
 
 
 def whole(space=VMEM):
@@ -73,7 +77,8 @@
             req = req + dot(asked.astype(jnp.bfloat16), place, NT)
             slot_ref[row : row + 1, :n] = col * CAP + rank.astype(jnp.int32)
             row += 1
-    req_ref[...] = req.astype(jnp.int32) - 1
+    asked = req.astype(jnp.int32)
+    req_ref[...] = jnp.where(asked == 0, 2 * AB, asked - 1) * BL
 
 
 def requests(om, lm, cells):
@@ -99,12 +104,13 @@
         for at in range(0, width, 8 * BL):
             part = dot(pick, ref[:, at : at + 8 * BL], NN)
             out_ref[:, k * width + at : k * width + at + 8 * BL] = part.astype(out_ref.dtype)
+    out_ref[:, 2 * width :] = jnp.zeros((nf, BL), out_ref.dtype)
 
 
 def hold(own, near):
     return pl.pallas_call(
         hold_kernel,
-        out_shape=jax.ShapeDtypeStruct((own.shape[0], 2 * own.shape[1]), own.dtype),
+        out_shape=jax.ShapeDtypeStruct((own.shape[0], 2 * own.shape[1] + BL), own.dtype),
         in_specs=[whole()] * 2,
         out_specs=whole(),
         compiler_params=pltpu.CompilerParams(vmem_limit_bytes=SMALL),
@@ -120,8 +126,7 @@
 
     def body(c, _):
         for r in range(CAP):
-            i = jnp.maximum(asked_ref[c, r], 0)
-            made[c * CAP + r] = both[:, lanes(i)]
+            made[c * CAP + r] = both[:, lanes_from(asked_ref[c, r])]
         out(c).start()
         return 0
 
@@ -367,8 +372,9 @@
         def _():
             for r in range(CAP):
                 total = totals[r % CHAINS - CHAINS]
-                i = asked_ref[c, r]
-                at = lanes(jnp.where(i < 0, AB, i & (AB - 1)))
+                first = asked_ref[c, r]
+                at = first - AB * BL if neighbours else jnp.minimum(first, AB * BL)
+                at = lanes_from(at)
                 total[:, at] = total[:, at] + back_ref[c * CAP + r].astype(jnp.float32)
 
         return 0

time: 73.6 us -> 73.4 us (level)
  no operation moved by 1% of the time
where the time goes in v8:
time: 73.4 us; the launch traced here: 72.9 us
  waiting for transfers between devices  25.1 us (34%)
  starting transfers between devices  24.7 us (34%)
  Pallas kernels  19.7 us (27%)
  local copies, waits for them, and re-layouts  1.87 us (3%)
  between operations  0.82 us (1%)
    all_to_all x1, waiting for transfers between devices, per_device(): got = exchange(serve(asked, held, cells))  15.9 us
    all_to_all x1, starting transfers between devices, per_device(): asked = exchange(asking)  8.95 us
    ppermute x1, starting transfers between devices, per_device(): away = lax.ppermute(collect(asked, back, None, True, cells), axes, to_owner)  5.47 us
    all_to_all x1, waiting for transfers between devices, per_device(): asked = exchange(asking)  5.11 us
    all_to_all x1, starting transfers between devices, per_device(): back = exchange(send)  5.08 us
    pallas_call x1, Pallas kernels, near_back(): pl.pallas_call(near_back_kernel, grid=(STEPS,), out_shape=jax.ShapeDtypeS...  4.86 us
    pallas_call x1, Pallas kernels, far(): pl.pallas_call(far_kernel, out_shape=(jax.ShapeDtypeStruct(os.shape, f32)...  4.72 us
    all_to_all x1, waiting for transfers between devices, per_device(): back = exchange(send)  4.14 us
  transfers between devices with their start and end apart: 5, of which 3 were waited for; matrix products, arithmetic and copies ran while one was open for 0% of the time, Pallas kernels for 16%

profile of v8, /device:TPU:1, one launch (start us, length us, event | category | flops | bytes accessed | tf_op | source)
XLA Modules:
  0.0 72.9 jit_solution(14112145863159538851)
XLA Ops:
  0.6 1.5 %collective-permute-start = (bf16[24,4096]{1,0:T(8,128)(2,1)}, bf16[24,4096]{1,0:T(8,128)(2,1)S(1)}, u32[]{:S(2)}, u32[]{:S(2)}) collective-permute-start(bf16[24,4096]{1,0:T(8,128)(2,1)} %own_ref.1), channel_id=1, source_target_pairs={{0,112},{1,113},{2,114},{3,115},{4,116},{5,117},{6,118},{7,119},{8... | collective-permute-start | bytes 589832 | tf_op jit(solution)/shard_map/ppermute | solution.py:432
  2.1 1.8 %requests.1 = (s32[16,128]{1,0:T(8,128)}, s32[8,128]{1,0:T(8,128)}) custom-call(s32[2,64]{1,0:T(2,128)} %bitcast.20, s32[2,16]{1,0:T(2,128)} %bitcast.21), custom_call_target="tpu_custom_call" | custom-call | tf_op jit(solution)/shard_map/requests/pallas_call | solution.py:85
  3.9 8.9 %all-to-all-start = ((s32[16,1,128]{2,1,0:T(1,128)}), s32[16,1,128]{2,1,0:T(1,128)S(1)}, u32[]{:S(2)}, u32[]{:S(2)}) async-start(s32[16,1,128]{2,1,0:T(1,128)} %bitcast.19), calls=%async_computation | async-start | bytes 16384 | tf_op jit(solution)/shard_map/all_to_all | solution.py:434
  12.9 0.0 collective-permute-done.near_ref
  12.9 0.0 copy-start.3
  12.9 0.9 %copy-done.3 = bf16[24,4096]{1,0:T(8,128)(2,1)S(1)} copy-done((bf16[24,4096]{1,0:T(8,128)(2,1)S(1)}, bf16[24,4096]{1,0:T(8,128)(2,1)}, u32[]{:S(2)}) %copy-start.3) | copy-done | bytes 196632
  13.8 0.3 hold.1.both.f_ref
  14.1 5.1 %all-to-all-done = s32[16,1,128]{2,1,0:T(1,128)S(1)} async-done(((s32[16,1,128]{2,1,0:T(1,128)}), s32[16,1,128]{2,1,0:T(1,128)S(1)}, u32[]{:S(2)}, u32[]{:S(2)}) %all-to-all-start) | async-done | bytes 8224 | tf_op jit(solution)/shard_map/all_to_all | solution.py:434
  19.2 0.0 copy-start.8
  19.2 0.0 copy-start.9
  19.2 2.0 %serve.1 = bf16[240,24,128]{2,1,0:T(8,128)(2,1)} custom-call(s32[16,128]{1,0:T(8,128)S(1)} %bitcast.10, bf16[24,8320]{1,0:T(8,128)(2,1)S(1)} %hold.1.both.f_ref), custom_call_target="tpu_custom_call" | custom-call | tf_op jit(solution)/shard_map/serve/pallas_call | solution.py:140
  21.3 3.7 %all-to-all-start.1 = ((bf16[240,24,128]{2,1,0:T(8,128)(2,1)}), bf16[240,24,128]{2,1,0:T(8,128)(2,1)S(1)}, u32[]{:S(2)}, u32[]{:S(2)}) async-start(bf16[240,24,128]{2,1,0:T(8,128)(2,1)} %serve.1), calls=%async_computation.1 | async-start | bytes 2949120 | tf_op jit(solution)/shard_map/all_to_all | solution.py:436
  25.0 0.0 copy-done.8
  25.0 0.0 copy-done.9
  25.0 0.0 copy-start.1
  25.0 0.0 copy-start.2
  25.0 0.0 copy-start.4
  25.0 0.0 copy-start.5
  25.1 0.0 copy-start.6
  25.1 0.0 copy-start.7
  25.1 3.8 %near_mix.1.near = f32[80,24,128]{2,1,0:T(8,128)S(1)} custom-call(s32[2,64]{1,0:T(2,128)S(1)} %bitcast.16, s32[2,16]{1,0:T(2,128)S(1)} %bitcast.18, bf16[24,8320]{1,0:T(8,128)(2,1)S(1)} %hold.1.both.f_ref, bf16[64,4,128,128]{3,2,1,0:T(8,128)(2,1)} %ot_ref.3, bf16[16,4,128,128]{3,2,1,0:T(8,128)(2,1)} %lt_ref.3), custom_call_target="tpu_custom_call" | custom-call | flops 671088640 | bytes 5242880 | tf_op jit(solution)/shard_map/near_mix/pallas_call | solution.py:178
  28.8 15.9 %all-to-all-done.1.got_ref = bf16[240,24,128]{2,1,0:T(8,128)(2,1)S(1)} async-done(((bf16[240,24,128]{2,1,0:T(8,128)(2,1)}), bf16[240,24,128]{2,1,0:T(8,128)(2,1)S(1)}, u32[]{:S(2)}, u32[]{:S(2)}) %all-to-all-start.1) | async-done | bytes 1474592 | tf_op jit(solution)/shard_map/all_to_all | solution.py:436
  44.7 0.0 copy-done.1
  44.7 0.0 copy-done.2
  44.7 0.0 copy-done.4
  44.7 0.0 copy-done.5
  44.8 0.0 copy-done.6
  44.8 0.0 copy-done.7
  44.8 4.7 %far.1 = (f32[8,8192]{1,0:T(8,128)}, f32[8,2048]{1,0:T(8,128)}, bf16[240,8,128]{2,1,0:T(8,128)(2,1)}) custom-call(s32[8,128]{1,0:T(8,128)S(1)} %copy-done.7, bf16[240,24,128]{2,1,0:T(8,128)(2,1)S(1)} %all-to-all-done.1.got_ref, f32[80,24,128]{2,1,0:T(8,128)S(1)} %near_mix.1.near, f32[8,8192]{1,0:T(8,128)S(1)} %copy-done.1, f32[8,8192]{1,0:T(8,128)S(1)} %copy-done.2, ...), custom_call_target="tpu_custom_call" | custom-call | tf_op jit(solution)/shard_map/far/pallas_call | solution.py:284
  49.5 5.1 %all-to-all-start.2 = ((bf16[240,8,128]{2,1,0:T(8,128)(2,1)}), bf16[240,8,128]{2,1,0:T(8,128)(2,1)S(1)}, u32[]{:S(2)}, u32[]{:S(2)}) async-start(bf16[240,8,128]{2,1,0:T(8,128)(2,1)} %get-tuple-element.12), calls=%async_computation.2 | async-start | bytes 983040 | tf_op jit(solution)/shard_map/all_to_all | solution.py:443
  54.6 4.9 %near_back.1.refs_0_ = f32[8,4096]{1,0:T(8,128)} custom-call(s32[2,64]{1,0:T(2,128)} %bitcast.15, s32[2,16]{1,0:T(2,128)} %bitcast.17, f32[8,8192]{1,0:T(8,128)} %get-tuple-element.8.of_ref, f32[8,2048]{1,0:T(8,128)} %get-tuple-element.9.lf_ref, bf16[64,4,128,128]{3,2,1,0:T(8,128)(2,1)} %ot_ref.3, bf16[16,4,128,128]{3,2,1,0:T(8,128)(2,1)} %lt_ref.3), custom_call_target="tpu_custom_call" | custom-call | flops 671088640 | bytes 5242880 | tf_op jit(solution)/shard_map/near_back/pallas_call | solution.py:329
  59.5 4.1 %all-to-all-done.2.back_ref = bf16[240,8,128]{2,1,0:T(8,128)(2,1)S(1)} async-done(((bf16[240,8,128]{2,1,0:T(8,128)(2,1)}), bf16[240,8,128]{2,1,0:T(8,128)(2,1)S(1)}, u32[]{:S(2)}, u32[]{:S(2)}) %all-to-all-start.2) | async-done | bytes 491552 | tf_op jit(solution)/shard_map/all_to_all | solution.py:443
  63.6 1.1 %collect_far.1 = bf16[8,4096]{1,0:T(8,128)(2,1)S(1)} custom-call(s32[16,128]{1,0:T(8,128)S(1)} %bitcast.11, bf16[240,8,128]{2,1,0:T(8,128)(2,1)S(1)} %all-to-all-done.2.back_ref), custom_call_target="tpu_custom_call" | custom-call | flops 1048576 | bytes 4194304 | tf_op jit(solution)/shard_map/collect_far/pallas_call | solution.py:397
  64.7 5.5 %collective-permute-start.1 = (bf16[8,4096]{1,0:T(8,128)(2,1)S(1)}, bf16[8,4096]{1,0:T(8,128)(2,1)S(1)}, u32[]{:S(2)}, u32[]{:S(2)}) collective-permute-start(bf16[8,4096]{1,0:T(8,128)(2,1)S(1)} %collect_far.1), channel_id=1, source_target_pairs={{112,0},{113,1},{114,2},{115,3},{116,4},{117,5},{118,6},{119,7},{2... | collective-permute-start | bytes 196616 | tf_op jit(solution)/shard_map/ppermute | solution.py:446
  70.1 0.0 copy-start
  70.1 0.9 %copy-done = f32[8,4096]{1,0:T(8,128)S(1)} copy-done((f32[8,4096]{1,0:T(8,128)S(1)}, f32[8,4096]{1,0:T(8,128)}, u32[]{:S(2)}) %copy-start) | copy-done | bytes 131096
  71.0 1.2 %collect_own.1 = f32[8,4096]{1,0:T(8,128)S(1)} custom-call(s32[16,128]{1,0:T(8,128)S(1)} %bitcast.12, bf16[240,8,128]{2,1,0:T(8,128)(2,1)S(1)} %all-to-all-done.2.back_ref, f32[8,4096]{1,0:T(8,128)S(1)} %copy-done), custom_call_target="tpu_custom_call" | custom-call | flops 1048576 | bytes 4194304 | tf_op jit(solution)/shard_map/collect_own/pallas_call | solution.py:397
  72.2 0.0 collective-permute-done.1
  72.2 0.7 convert_add_fusion
Async XLA Ops:
  0.6 12.2 %collective-permute-start = (bf16[24,4096]{1,0:T(8,128)(2,1)}, bf16[24,4096]{1,0:T(8,128)(2,1)S(1)}, u32[]{:S(2)}, u32[]{:S(2)}) collective-permute-start(bf16[24,4096]{1,0:T(8,128)(2,1)} %own_ref.1), channel_id=1, source_target_pairs={{0,112},{1,113},{2,114},{3,115},{4,116},{5,117},{6,118},{7,119},{8... | collective-permute-start | bytes 589832 | tf_op jit(solution)/shard_map/ppermute | solution.py:432
  3.9 15.3 %all-to-all-start = ((s32[16,1,128]{2,1,0:T(1,128)}), s32[16,1,128]{2,1,0:T(1,128)S(1)}, u32[]{:S(2)}, u32[]{:S(2)}) async-start(s32[16,1,128]{2,1,0:T(1,128)} %bitcast.19), calls=%async_computation | async-start | bytes 16384 | tf_op jit(solution)/shard_map/all_to_all | solution.py:434
  12.9 0.9 %copy-start.3 = (bf16[24,4096]{1,0:T(8,128)(2,1)S(1)}, bf16[24,4096]{1,0:T(8,128)(2,1)}, u32[]{:S(2)}) copy-start(bf16[24,4096]{1,0:T(8,128)(2,1)} %own_ref.1) | copy-start | bytes 589828
  19.2 5.8 %copy-start.8 = (s32[64,2]{0,1:T(2,128)S(1)}, s32[64,2]{0,1:T(2,128)}, u32[]{:S(2)}) copy-start(s32[64,2]{0,1:T(2,128)} %param.19) | copy-start | bytes 1540
  19.2 5.8 %copy-start.9 = (s32[16,2]{0,1:T(2,128)S(1)}, s32[16,2]{0,1:T(2,128)}, u32[]{:S(2)}) copy-start(s32[16,2]{0,1:T(2,128)} %param.22) | copy-start | bytes 388
  21.3 23.5 %all-to-all-start.1 = ((bf16[240,24,128]{2,1,0:T(8,128)(2,1)}), bf16[240,24,128]{2,1,0:T(8,128)(2,1)S(1)}, u32[]{:S(2)}, u32[]{:S(2)}) async-start(bf16[240,24,128]{2,1,0:T(8,128)(2,1)} %serve.1), calls=%async_computation.1 | async-start | bytes 2949120 | tf_op jit(solution)/shard_map/all_to_all | solution.py:436
  25.0 19.7 %copy-start.1 = (f32[8,8192]{1,0:T(8,128)S(1)}, f32[8,8192]{1,0:T(8,128)}, u32[]{:S(2)}) copy-start(f32[8,8192]{1,0:T(8,128)} %osv.1) | copy-start | bytes 786436
  25.0 19.7 %copy-start.2 = (f32[8,8192]{1,0:T(8,128)S(1)}, f32[8,8192]{1,0:T(8,128)}, u32[]{:S(2)}) copy-start(f32[8,8192]{1,0:T(8,128)} %isv.1) | copy-start | bytes 786436
  25.0 19.7 %copy-start.4 = (f32[8,2048]{1,0:T(8,128)S(1)}, f32[8,2048]{1,0:T(8,128)}, u32[]{:S(2)}) copy-start(f32[8,2048]{1,0:T(8,128)} %ls.1) | copy-start | bytes 196612
  25.0 19.7 %copy-start.5 = (s32[8192]{0:T(1024)S(1)}, s32[8192]{0:T(1024)}, u32[]{:S(2)}) copy-start(s32[8192]{0:T(1024)} %param.15) | copy-start | bytes 98308
  25.1 19.7 %copy-start.6 = (s32[2048]{0:T(1024)S(1)}, s32[2048]{0:T(1024)}, u32[]{:S(2)}) copy-start(s32[2048]{0:T(1024)} %param.17) | copy-start | bytes 24580
  25.1 19.7 %copy-start.7 = (s32[8,128]{1,0:T(8,128)S(1)}, s32[8,128]{1,0:T(8,128)}, u32[]{:S(2)}) copy-start(s32[8,128]{1,0:T(8,128)} %get-tuple-element.11.slot_hbm) | copy-start | bytes 12292
  49.5 14.1 %all-to-all-start.2 = ((bf16[240,8,128]{2,1,0:T(8,128)(2,1)}), bf16[240,8,128]{2,1,0:T(8,128)(2,1)S(1)}, u32[]{:S(2)}, u32[]{:S(2)}) async-start(bf16[240,8,128]{2,1,0:T(8,128)(2,1)} %get-tuple-element.12), calls=%async_computation.2 | async-start | bytes 983040 | tf_op jit(solution)/shard_map/all_to_all | solution.py:443
  64.7 7.6 %collective-permute-start.1 = (bf16[8,4096]{1,0:T(8,128)(2,1)S(1)}, bf16[8,4096]{1,0:T(8,128)(2,1)S(1)}, u32[]{:S(2)}, u32[]{:S(2)}) collective-permute-start(bf16[8,4096]{1,0:T(8,128)(2,1)S(1)} %collect_far.1), channel_id=1, source_target_pairs={{112,0},{113,1},{114,2},{115,3},{116,4},{117,5},{118,6},{119,7},{2... | collective-permute-start | bytes 196616 | tf_op jit(solution)/shard_map/ppermute | solution.py:446
  70.1 0.9 %copy-start = (f32[8,4096]{1,0:T(8,128)S(1)}, f32[8,4096]{1,0:T(8,128)}, u32[]{:S(2)}) copy-start(f32[8,4096]{1,0:T(8,128)} %near_back.1.refs_0_) | copy-start | bytes 393220

commit v9 on v7

--- a/solution.py
+++ b/solution.py
@@ -199,8 +199,8 @@
 
 
 def far_kernel(
-    slot_hbm, got_ref, near, osv, isv, il, ls, ll, ot_hbm, lt_hbm, of_hbm, lf_hbm, send_hbm,
-    slot_ref, ot, lt, of, lf, send, in_sems, out_sems, slot_sem,
+    slot_hbm, got_ref, near, osv, isv, il, ls, ll, ot_hbm, lt_hbm, of_hbm, lf_hbm, send,
+    slot_ref, ot, lt, of, lf, in_sems, out_sems, slot_sem,
 ):
     ob, lb = ot.shape[0], lt.shape[0]
     no, nl = ob // STEPS, lb // STEPS
@@ -266,8 +266,6 @@
             terms = dot(flux, weight, NT).astype(send.dtype)
             for k in range(KR):
                 send[pair[k]] = terms[:, k * BL : (k + 1) * BL]
-    outs.append(pltpu.make_async_copy(send, send_hbm, out_sems.at[len(outs)]))
-    outs[-1].start()
     for copy in outs:
         copy.wait()
 
@@ -284,14 +282,13 @@
             jax.ShapeDtypeStruct(back, jnp.bfloat16),
         ),
         in_specs=[whole(pl.ANY), *[whole()] * 7, *[whole(pl.ANY)] * 2],
-        out_specs=[whole(pltpu.HBM)] * 3,
+        out_specs=[whole(pltpu.HBM), whole(pltpu.HBM), whole()],
         scratch_shapes=[
             SMEM(slots.shape, slots.dtype),
             VMEM((ot.shape[0], KR, BL, BL), ot.dtype),
             VMEM((lt.shape[0], KR, BL, BL), lt.dtype),
             VMEM(os.shape, f32),
             VMEM(ls.shape, f32),
-            VMEM(back, jnp.bfloat16),
             pltpu.SemaphoreType.DMA((count,)),
             pltpu.SemaphoreType.DMA((count + 1,)),
             pltpu.SemaphoreType.DMA(()),
@@ -301,38 +298,45 @@
     )(slots, got, near, os, ice, il, ls, ll, ot, lt)
 
 
-def near_back_kernel(ol_ref, ll_ref, of_ref, lf_ref, ot_ref, lt_ref, out_ref):
-    step = pl.program_id(0)
-
-    @pl.when(step == 0)
-    def _():
-        out_ref[...] = jnp.zeros(out_ref.shape, out_ref.dtype)
-
-    for ids, flux, tiles in ((ol_ref, of_ref, ot_ref), (ll_ref, lf_ref, lt_ref)):
-        n = tiles.shape[0]
-        for b in range(n):
-            g = flux[:, b * BL : (b + 1) * BL].astype(jnp.bfloat16)
-            terms = dot(g, tiles[b].reshape(2 * BL, BL), NT)
-            for k in range(2):
-                at = lanes(ids[k, step * n + b])
-                out_ref[:, at] = out_ref[:, at] + terms[:, k * BL : (k + 1) * BL]
+def near_back_kernel(ol_ref, ll_ref, of_ref, lf_ref, ot_hbm, lt_hbm, out_ref, ot, lt, sems):
+    ob, lb = ot.shape[0], lt.shape[0]
+    parts = portions(ob, lb)
+    ins = []
+    for i, part in enumerate(parts):
+        for kind, lo, hi in part:
+            hbm, on_chip = (lt_hbm, lt) if kind else (ot_hbm, ot)
+            some = pl.ds(lo, hi - lo)
+            copy = pltpu.make_async_copy(
+                hbm.at[some, pl.ds(KR, KL)], on_chip.at[some], sems.at[len(ins)]
+            )
+            copy.start()
+            ins.append(copy)
+    out_ref[...] = jnp.zeros(out_ref.shape, out_ref.dtype)
+    waits = iter(ins)
+    for part in parts:
+        for kind, lo, hi in part:
+            next(waits).wait()
+            ids, flux, tiles = (ll_ref, lf_ref, lt) if kind else (ol_ref, of_ref, ot)
+            for b in range(lo, hi):
+                g = flux[:, b * BL : (b + 1) * BL].astype(jnp.bfloat16)
+                terms = dot(g, tiles[b].reshape(KL * BL, BL), NT)
+                for k in range(KL):
+                    to = lanes(ids[k, b])
+                    out_ref[:, to] = out_ref[:, to] + terms[:, k * BL : (k + 1) * BL]
 
 
 def near_back(ol, ll, of, lf, ot, lt):
     ob, lb = ot.shape[0], lt.shape[0]
-    ns = of.shape[0]
     return pl.pallas_call(
         near_back_kernel,
-        grid=(STEPS,),
-        out_shape=jax.ShapeDtypeStruct((ns, AB * BL), jnp.float32),
-        in_specs=[
-            whole(SMEM),
-            whole(SMEM),
-            pl.BlockSpec((ns, ob // STEPS * BL), lambda i: (0, i)),
-            pl.BlockSpec((ns, lb // STEPS * BL), lambda i: (0, i)),
-            *tile_specs(ob, lb, 1),
+        out_shape=jax.ShapeDtypeStruct((of.shape[0], AB * BL), jnp.float32),
+        in_specs=[whole(SMEM), whole(SMEM), whole(), whole(), whole(pl.ANY), whole(pl.ANY)],
+        out_specs=whole(),
+        scratch_shapes=[
+            VMEM((ob, KL, BL, BL), ot.dtype),
+            VMEM((lb, KL, BL, BL), lt.dtype),
+            pltpu.SemaphoreType.DMA((len(PARTS),)),
         ],
-        out_specs=pl.BlockSpec((ns, AB * BL), lambda i: (0, 0)),
         compiler_params=pltpu.CompilerParams(vmem_limit_bytes=GRANT),
         cost_estimate=pl.CostEstimate(
             flops=2 * (ob + lb) * 2 * BL * BL * 128,
@@ -436,7 +440,6 @@
     )
     back = exchange(send)
     acc = near_back(ol, ll, of, lf, ocn_tiles, lnd_tiles)
-    back, acc = lax.optimization_barrier((back, acc))
     away = lax.ppermute(collect(asked, back, None, True, cells), axes, to_owner)
     own = collect(asked, back, acc, False, cells)
     return own + away.astype(jnp.float32), of, lf

time: 73.6 us -> 77.6 us (1.054)
  blocking collectives: 0 us -> 13.9 us
  starting transfers between devices: 24.7 us -> 19.3 us
  waiting for transfers between devices: 25.1 us -> 21 us
    all_to_all x0 -> x1, blocking collectives: none -> 13.9 us  [per_device(): back = exchange(send)]
    all_to_all x1 -> x0, starting transfers between devices: 5.08 us -> none  [per_device(): back = exchange(send)]
    all_to_all x1 -> x0, waiting for transfers between devices: 4.13 us -> none  [per_device(): back = exchange(send)]
  transfers between devices with their start and end apart: 5 -> 4, of which waited for: 3 -> 2; matrix products, arithmetic and copies ran while one was open for 0% -> 0% of each run, Pallas kernels for 16% -> 15%
where the time goes in v9:
time: 77.6 us; the launch traced here: 77.2 us
  waiting for transfers between devices  21 us (27%)
  Pallas kernels  19.7 us (25%)
  starting transfers between devices  19.3 us (25%)
  blocking collectives  13.9 us (18%)
  local copies, waits for them, and re-layouts  1.87 us (2%)
  between operations  0.83 us (1%)
    all_to_all x1, waiting for transfers between devices, per_device(): got = exchange(serve(asked, held, cells))  15.9 us
    all_to_all x1, blocking collectives, per_device(): back = exchange(send)  13.9 us
    all_to_all x1, starting transfers between devices, per_device(): asked = exchange(asking)  8.95 us
    ppermute x1, starting transfers between devices, per_device(): away = lax.ppermute(collect(asked, back, None, True, cells), axes, to_owner)  5.19 us
    all_to_all x1, waiting for transfers between devices, per_device(): asked = exchange(asking)  5.12 us
    pallas_call x1, Pallas kernels, near_back(): pl.pallas_call(near_back_kernel, out_shape=jax.ShapeDtypeStruct((of.shape...  4.85 us
    pallas_call x1, Pallas kernels, far(): pl.pallas_call(far_kernel, out_shape=(jax.ShapeDtypeStruct(os.shape, f32)...  4.52 us
    pallas_call x1, Pallas kernels, near_mix(): pl.pallas_call(near_mix_kernel, grid=(STEPS,), out_shape=jax.ShapeDtypeSt...  3.78 us
  transfers between devices with their start and end apart: 4, of which 2 were waited for; matrix products, arithmetic and copies ran while one was open for 0% of the time, Pallas kernels for 15%

profile of v9, /device:TPU:1, one launch (start us, length us, event | category | flops | bytes accessed | tf_op | source)
XLA Modules:
  0.0 77.2 jit_solution(1497910492530005081)
XLA Ops:
  0.6 1.5 %collective-permute-start = (bf16[24,4096]{1,0:T(8,128)(2,1)}, bf16[24,4096]{1,0:T(8,128)(2,1)S(1)}, u32[]{:S(2)}, u32[]{:S(2)}) collective-permute-start(bf16[24,4096]{1,0:T(8,128)(2,1)} %own_ref.1), channel_id=1, source_target_pairs={{0,112},{1,113},{2,114},{3,115},{4,116},{5,117},{6,118},{7,119},{8... | collective-permute-start | bytes 589832 | tf_op jit(solution)/shard_map/ppermute | solution.py:430
  2.1 1.8 %requests.1 = (s32[16,128]{1,0:T(8,128)}, s32[8,128]{1,0:T(8,128)}) custom-call(s32[2,64]{1,0:T(2,128)} %bitcast.20, s32[2,16]{1,0:T(2,128)} %bitcast.21), custom_call_target="tpu_custom_call" | custom-call | tf_op jit(solution)/shard_map/requests/pallas_call | solution.py:80
  3.9 8.9 %all-to-all-start = ((s32[16,1,128]{2,1,0:T(1,128)}), s32[16,1,128]{2,1,0:T(1,128)S(1)}, u32[]{:S(2)}, u32[]{:S(2)}) async-start(s32[16,1,128]{2,1,0:T(1,128)} %bitcast.19), calls=%async_computation | async-start | bytes 16384 | tf_op jit(solution)/shard_map/all_to_all | solution.py:432
  12.9 0.0 collective-permute-done.near_ref
  12.9 0.0 copy-start.3
  12.9 0.9 %copy-done.3 = bf16[24,4096]{1,0:T(8,128)(2,1)S(1)} copy-done((bf16[24,4096]{1,0:T(8,128)(2,1)S(1)}, bf16[24,4096]{1,0:T(8,128)(2,1)}, u32[]{:S(2)}) %copy-start.3) | copy-done | bytes 196632
  13.8 0.3 hold.1.both.f_ref
  14.1 5.1 %all-to-all-done = s32[16,1,128]{2,1,0:T(1,128)S(1)} async-done(((s32[16,1,128]{2,1,0:T(1,128)}), s32[16,1,128]{2,1,0:T(1,128)S(1)}, u32[]{:S(2)}, u32[]{:S(2)}) %all-to-all-start) | async-done | bytes 8224 | tf_op jit(solution)/shard_map/all_to_all | solution.py:432
  19.2 0.0 copy-start.8
  19.2 0.0 copy-start.9
  19.2 2.1 %serve.1 = bf16[240,24,128]{2,1,0:T(8,128)(2,1)} custom-call(s32[16,128]{1,0:T(8,128)S(1)} %bitcast.10, bf16[24,8192]{1,0:T(8,128)(2,1)S(1)} %hold.1.both.f_ref), custom_call_target="tpu_custom_call" | custom-call | tf_op jit(solution)/shard_map/serve/pallas_call | solution.py:135
  21.3 3.7 %all-to-all-start.1 = ((bf16[240,24,128]{2,1,0:T(8,128)(2,1)}), bf16[240,24,128]{2,1,0:T(8,128)(2,1)S(1)}, u32[]{:S(2)}, u32[]{:S(2)}) async-start(bf16[240,24,128]{2,1,0:T(8,128)(2,1)} %serve.1), calls=%async_computation.1 | async-start | bytes 2949120 | tf_op jit(solution)/shard_map/all_to_all | solution.py:434
  25.0 0.0 copy-done.8
  25.0 0.0 copy-done.9
  25.0 0.0 copy-start.1
  25.0 0.0 copy-start.2
  25.0 0.0 copy-start.4
  25.1 0.0 copy-start.5
  25.1 0.0 copy-start.6
  25.1 0.0 copy-start.7
  25.1 3.8 %near_mix.1.near = f32[80,24,128]{2,1,0:T(8,128)S(1)} custom-call(s32[2,64]{1,0:T(2,128)S(1)} %bitcast.16, s32[2,16]{1,0:T(2,128)S(1)} %bitcast.18, bf16[24,8192]{1,0:T(8,128)(2,1)S(1)} %hold.1.both.f_ref, bf16[64,4,128,128]{3,2,1,0:T(8,128)(2,1)} %ot_hbm.3, bf16[16,4,128,128]{3,2,1,0:T(8,128)(2,1)} %lt_hbm.3), custom_call_target="tpu_custom_call" | custom-call | flops 671088640 | bytes 5242880 | tf_op jit(solution)/shard_map/near_mix/pallas_call | solution.py:173
  28.9 15.9 %all-to-all-done.1.got_ref = bf16[240,24,128]{2,1,0:T(8,128)(2,1)S(1)} async-done(((bf16[240,24,128]{2,1,0:T(8,128)(2,1)}), bf16[240,24,128]{2,1,0:T(8,128)(2,1)S(1)}, u32[]{:S(2)}, u32[]{:S(2)}) %all-to-all-start.1) | async-done | bytes 1474592 | tf_op jit(solution)/shard_map/all_to_all | solution.py:434
  44.8 0.0 copy-done.1
  44.8 0.0 copy-done.2
  44.8 0.0 copy-done.4
  44.8 0.0 copy-done.5
  44.8 0.0 copy-done.6
  44.8 0.0 copy-done.7
  44.8 4.5 %far.1 = (f32[8,8192]{1,0:T(8,128)}, f32[8,2048]{1,0:T(8,128)}, bf16[240,8,128]{2,1,0:T(8,128)(2,1)S(1)}) custom-call(s32[8,128]{1,0:T(8,128)S(1)} %copy-done.7, bf16[240,24,128]{2,1,0:T(8,128)(2,1)S(1)} %all-to-all-done.1.got_ref, f32[80,24,128]{2,1,0:T(8,128)S(1)} %near_mix.1.near, f32[8,8192]{1,0:T(8,128)S(1)} %copy-done.1, f32[8,8192]{1,0:T(8,128)S(1)} %copy-done.2, ...), custom_call_target="tpu_custom_call" | custom-call | tf_op jit(solution)/shard_map/far/pallas_call | solution.py:277
  49.3 13.9 %all_to_all.21.back_ref = bf16[240,8,128]{2,1,0:T(8,128)(2,1)S(1)} all-to-all(bf16[240,8,128]{2,1,0:T(8,128)(2,1)S(1)} %get-tuple-element.10), channel_id=1, replica_groups=mesh['sect'=8,'cell'=16] {'cell'}, dimensions={0} | all-to-all | bytes 983040 | tf_op jit(solution)/shard_map/all_to_all | solution.py:441
  63.2 1.1 %collect_far.1 = bf16[8,4096]{1,0:T(8,128)(2,1)S(1)} custom-call(s32[16,128]{1,0:T(8,128)S(1)} %bitcast.11, bf16[240,8,128]{2,1,0:T(8,128)(2,1)S(1)} %all_to_all.21.back_ref), custom_call_target="tpu_custom_call" | custom-call | flops 1048576 | bytes 4194304 | tf_op jit(solution)/shard_map/collect_far/pallas_call | solution.py:395
  64.3 5.2 %collective-permute-start.1 = (bf16[8,4096]{1,0:T(8,128)(2,1)S(1)}, bf16[8,4096]{1,0:T(8,128)(2,1)S(1)}, u32[]{:S(2)}, u32[]{:S(2)}) collective-permute-start(bf16[8,4096]{1,0:T(8,128)(2,1)S(1)} %collect_far.1), channel_id=1, source_target_pairs={{112,0},{113,1},{114,2},{115,3},{116,4},{117,5},{118,6},{119,7},{2... | collective-permute-start | bytes 196616 | tf_op jit(solution)/shard_map/ppermute | solution.py:443
  69.5 4.9 %near_back.1.refs_0_ = f32[8,4096]{1,0:T(8,128)} custom-call(s32[2,64]{1,0:T(2,128)} %bitcast.15, s32[2,16]{1,0:T(2,128)} %bitcast.17, f32[8,8192]{1,0:T(8,128)} %get-tuple-element.6.of_ref, f32[8,2048]{1,0:T(8,128)} %get-tuple-element.7.lf_ref, bf16[64,4,128,128]{3,2,1,0:T(8,128)(2,1)} %ot_hbm.3, bf16[16,4,128,128]{3,2,1,0:T(8,128)(2,1)} %lt_hbm.3), custom_call_target="tpu_custom_call" | custom-call | flops 671088640 | bytes 5242880 | tf_op jit(solution)/shard_map/near_back/pallas_call | solution.py:330
  74.4 0.0 copy-start
  74.4 0.9 %copy-done = f32[8,4096]{1,0:T(8,128)S(1)} copy-done((f32[8,4096]{1,0:T(8,128)S(1)}, f32[8,4096]{1,0:T(8,128)}, u32[]{:S(2)}) %copy-start) | copy-done | bytes 131096
  75.3 1.2 %collect_own.1 = f32[8,4096]{1,0:T(8,128)S(1)} custom-call(s32[16,128]{1,0:T(8,128)S(1)} %bitcast.12, bf16[240,8,128]{2,1,0:T(8,128)(2,1)S(1)} %all_to_all.21.back_ref, f32[8,4096]{1,0:T(8,128)S(1)} %copy-done), custom_call_target="tpu_custom_call" | custom-call | flops 1048576 | bytes 4194304 | tf_op jit(solution)/shard_map/collect_own/pallas_call | solution.py:395
  76.5 0.0 collective-permute-done.1
  76.6 0.7 convert_add_fusion
Async XLA Ops:
  0.6 12.2 %collective-permute-start = (bf16[24,4096]{1,0:T(8,128)(2,1)}, bf16[24,4096]{1,0:T(8,128)(2,1)S(1)}, u32[]{:S(2)}, u32[]{:S(2)}) collective-permute-start(bf16[24,4096]{1,0:T(8,128)(2,1)} %own_ref.1), channel_id=1, source_target_pairs={{0,112},{1,113},{2,114},{3,115},{4,116},{5,117},{6,118},{7,119},{8... | collective-permute-start | bytes 589832 | tf_op jit(solution)/shard_map/ppermute | solution.py:430
  3.9 15.3 %all-to-all-start = ((s32[16,1,128]{2,1,0:T(1,128)}), s32[16,1,128]{2,1,0:T(1,128)S(1)}, u32[]{:S(2)}, u32[]{:S(2)}) async-start(s32[16,1,128]{2,1,0:T(1,128)} %bitcast.19), calls=%async_computation | async-start | bytes 16384 | tf_op jit(solution)/shard_map/all_to_all | solution.py:432
  12.9 0.9 %copy-start.3 = (bf16[24,4096]{1,0:T(8,128)(2,1)S(1)}, bf16[24,4096]{1,0:T(8,128)(2,1)}, u32[]{:S(2)}) copy-start(bf16[24,4096]{1,0:T(8,128)(2,1)} %own_ref.1) | copy-start | bytes 589828
  19.2 5.8 %copy-start.8 = (s32[64,2]{0,1:T(2,128)S(1)}, s32[64,2]{0,1:T(2,128)}, u32[]{:S(2)}) copy-start(s32[64,2]{0,1:T(2,128)} %param.19) | copy-start | bytes 1540
  19.2 5.8 %copy-start.9 = (s32[16,2]{0,1:T(2,128)S(1)}, s32[16,2]{0,1:T(2,128)}, u32[]{:S(2)}) copy-start(s32[16,2]{0,1:T(2,128)} %param.22) | copy-start | bytes 388
  21.3 23.5 %all-to-all-start.1 = ((bf16[240,24,128]{2,1,0:T(8,128)(2,1)}), bf16[240,24,128]{2,1,0:T(8,128)(2,1)S(1)}, u32[]{:S(2)}, u32[]{:S(2)}) async-start(bf16[240,24,128]{2,1,0:T(8,128)(2,1)} %serve.1), calls=%async_computation.1 | async-start | bytes 2949120 | tf_op jit(solution)/shard_map/all_to_all | solution.py:434
  25.0 19.7 %copy-start.1 = (f32[8,8192]{1,0:T(8,128)S(1)}, f32[8,8192]{1,0:T(8,128)}, u32[]{:S(2)}) copy-start(f32[8,8192]{1,0:T(8,128)} %osv.1) | copy-start | bytes 786436
  25.0 19.7 %copy-start.2 = (f32[8,8192]{1,0:T(8,128)S(1)}, f32[8,8192]{1,0:T(8,128)}, u32[]{:S(2)}) copy-start(f32[8,8192]{1,0:T(8,128)} %isv.1) | copy-start | bytes 786436
  25.0 19.7 %copy-start.4 = (f32[8,2048]{1,0:T(8,128)S(1)}, f32[8,2048]{1,0:T(8,128)}, u32[]{:S(2)}) copy-start(f32[8,2048]{1,0:T(8,128)} %ls.1) | copy-start | bytes 196612
  25.1 19.7 %copy-start.5 = (s32[8192]{0:T(1024)S(1)}, s32[8192]{0:T(1024)}, u32[]{:S(2)}) copy-start(s32[8192]{0:T(1024)} %param.15) | copy-start | bytes 98308
  25.1 19.7 %copy-start.6 = (s32[2048]{0:T(1024)S(1)}, s32[2048]{0:T(1024)}, u32[]{:S(2)}) copy-start(s32[2048]{0:T(1024)} %param.17) | copy-start | bytes 24580
  25.1 19.7 %copy-start.7 = (s32[8,128]{1,0:T(8,128)S(1)}, s32[8,128]{1,0:T(8,128)}, u32[]{:S(2)}) copy-start(s32[8,128]{1,0:T(8,128)} %get-tuple-element.9.slot_hbm) | copy-start | bytes 12292
  64.3 12.2 %collective-permute-start.1 = (bf16[8,4096]{1,0:T(8,128)(2,1)S(1)}, bf16[8,4096]{1,0:T(8,128)(2,1)S(1)}, u32[]{:S(2)}, u32[]{:S(2)}) collective-permute-start(bf16[8,4096]{1,0:T(8,128)(2,1)S(1)} %collect_far.1), channel_id=1, source_target_pairs={{112,0},{113,1},{114,2},{115,3},{116,4},{117,5},{118,6},{119,7},{2... | collective-permute-start | bytes 196616 | tf_op jit(solution)/shard_map/ppermute | solution.py:443
  74.4 0.9 %copy-start = (f32[8,4096]{1,0:T(8,128)S(1)}, f32[8,4096]{1,0:T(8,128)}, u32[]{:S(2)}) copy-start(f32[8,4096]{1,0:T(8,128)} %near_back.1.refs_0_) | copy-start | bytes 393220

commit v10 on v8

--- a/solution.py
+++ b/solution.py
@@ -17,7 +17,7 @@
 KR = KL = 2
 CAP = 15
 GRANT, LARGE, SMALL = 60 << 20, 50 << 20, 8 << 20
-CHAINS = 5
+CHAINS = 3
 VMEM = pltpu.VMEM
 SMEM = pltpu.SMEM
 NN = (((1,), (0,)), ((), ()))

time: 73.4 us -> 73.4 us (level)
  no operation moved by 1% of the time
where the time goes in v10:
time: 73.4 us; the launch traced here: 72.9 us
  waiting for transfers between devices  25.1 us (34%)
  starting transfers between devices  24.7 us (34%)
  Pallas kernels  19.6 us (27%)
  local copies, waits for them, and re-layouts  1.87 us (3%)
  between operations  0.82 us (1%)
    all_to_all x1, waiting for transfers between devices, per_device(): got = exchange(serve(asked, held, cells))  15.9 us
    all_to_all x1, starting transfers between devices, per_device(): asked = exchange(asking)  8.95 us
    ppermute x1, starting transfers between devices, per_device(): away = lax.ppermute(collect(asked, back, None, True, cells), axes, to_owner)  5.5 us
    all_to_all x1, waiting for transfers between devices, per_device(): asked = exchange(asking)  5.11 us
    all_to_all x1, starting transfers between devices, per_device(): back = exchange(send)  5.09 us
    pallas_call x1, Pallas kernels, near_back(): pl.pallas_call(near_back_kernel, grid=(STEPS,), out_shape=jax.ShapeDtypeS...  4.86 us
    pallas_call x1, Pallas kernels, far(): pl.pallas_call(far_kernel, out_shape=(jax.ShapeDtypeStruct(os.shape, f32)...  4.71 us
    all_to_all x1, waiting for transfers between devices, per_device(): back = exchange(send)  4.13 us
  transfers between devices with their start and end apart: 5, of which 3 were waited for; matrix products, arithmetic and copies ran while one was open for 0% of the time, Pallas kernels for 16%

profile of v10, /device:TPU:1, one launch (start us, length us, event | category | flops | bytes accessed | tf_op | source)
XLA Modules:
  0.0 72.9 jit_solution(7402620286039291061)
XLA Ops:
  0.6 1.5 %collective-permute-start = (bf16[24,4096]{1,0:T(8,128)(2,1)}, bf16[24,4096]{1,0:T(8,128)(2,1)S(1)}, u32[]{:S(2)}, u32[]{:S(2)}) collective-permute-start(bf16[24,4096]{1,0:T(8,128)(2,1)} %own_ref.1), channel_id=1, source_target_pairs={{0,112},{1,113},{2,114},{3,115},{4,116},{5,117},{6,118},{7,119},{8... | collective-permute-start | bytes 589832 | tf_op jit(solution)/shard_map/ppermute | solution.py:432
  2.1 1.8 %requests.1 = (s32[16,128]{1,0:T(8,128)}, s32[8,128]{1,0:T(8,128)}) custom-call(s32[2,64]{1,0:T(2,128)} %bitcast.20, s32[2,16]{1,0:T(2,128)} %bitcast.21), custom_call_target="tpu_custom_call" | custom-call | tf_op jit(solution)/shard_map/requests/pallas_call | solution.py:85
  3.9 8.9 %all-to-all-start = ((s32[16,1,128]{2,1,0:T(1,128)}), s32[16,1,128]{2,1,0:T(1,128)S(1)}, u32[]{:S(2)}, u32[]{:S(2)}) async-start(s32[16,1,128]{2,1,0:T(1,128)} %bitcast.19), calls=%async_computation | async-start | bytes 16384 | tf_op jit(solution)/shard_map/all_to_all | solution.py:434
  12.9 0.0 collective-permute-done.near_ref
  12.9 0.0 copy-start.3
  12.9 0.9 %copy-done.3 = bf16[24,4096]{1,0:T(8,128)(2,1)S(1)} copy-done((bf16[24,4096]{1,0:T(8,128)(2,1)S(1)}, bf16[24,4096]{1,0:T(8,128)(2,1)}, u32[]{:S(2)}) %copy-start.3) | copy-done | bytes 196632
  13.8 0.3 hold.1.both.f_ref
  14.1 5.1 %all-to-all-done = s32[16,1,128]{2,1,0:T(1,128)S(1)} async-done(((s32[16,1,128]{2,1,0:T(1,128)}), s32[16,1,128]{2,1,0:T(1,128)S(1)}, u32[]{:S(2)}, u32[]{:S(2)}) %all-to-all-start) | async-done | bytes 8224 | tf_op jit(solution)/shard_map/all_to_all | solution.py:434
  19.2 0.0 copy-start.8
  19.2 0.0 copy-start.9
  19.2 2.0 %serve.1 = bf16[240,24,128]{2,1,0:T(8,128)(2,1)} custom-call(s32[16,128]{1,0:T(8,128)S(1)} %bitcast.10, bf16[24,8320]{1,0:T(8,128)(2,1)S(1)} %hold.1.both.f_ref), custom_call_target="tpu_custom_call" | custom-call | tf_op jit(solution)/shard_map/serve/pallas_call | solution.py:140
  21.3 3.7 %all-to-all-start.1 = ((bf16[240,24,128]{2,1,0:T(8,128)(2,1)}), bf16[240,24,128]{2,1,0:T(8,128)(2,1)S(1)}, u32[]{:S(2)}, u32[]{:S(2)}) async-start(bf16[240,24,128]{2,1,0:T(8,128)(2,1)} %serve.1), calls=%async_computation.1 | async-start | bytes 2949120 | tf_op jit(solution)/shard_map/all_to_all | solution.py:436
  25.0 0.0 copy-done.8
  25.0 0.0 copy-done.9
  25.0 0.0 copy-start.1
  25.0 0.0 copy-start.2
  25.0 0.0 copy-start.4
  25.0 0.0 copy-start.5
  25.1 0.0 copy-start.6
  25.1 0.0 copy-start.7
  25.1 3.7 %near_mix.1.near = f32[80,24,128]{2,1,0:T(8,128)S(1)} custom-call(s32[2,64]{1,0:T(2,128)S(1)} %bitcast.16, s32[2,16]{1,0:T(2,128)S(1)} %bitcast.18, bf16[24,8320]{1,0:T(8,128)(2,1)S(1)} %hold.1.both.f_ref, bf16[64,4,128,128]{3,2,1,0:T(8,128)(2,1)} %ot_ref.3, bf16[16,4,128,128]{3,2,1,0:T(8,128)(2,1)} %lt_ref.3), custom_call_target="tpu_custom_call" | custom-call | flops 671088640 | bytes 5242880 | tf_op jit(solution)/shard_map/near_mix/pallas_call | solution.py:178
  28.8 15.9 %all-to-all-done.1.got_ref = bf16[240,24,128]{2,1,0:T(8,128)(2,1)S(1)} async-done(((bf16[240,24,128]{2,1,0:T(8,128)(2,1)}), bf16[240,24,128]{2,1,0:T(8,128)(2,1)S(1)}, u32[]{:S(2)}, u32[]{:S(2)}) %all-to-all-start.1) | async-done | bytes 1474592 | tf_op jit(solution)/shard_map/all_to_all | solution.py:436
  44.7 0.0 copy-done.1
  44.7 0.0 copy-done.2
  44.7 0.0 copy-done.4
  44.7 0.0 copy-done.5
  44.8 0.0 copy-done.6
  44.8 0.0 copy-done.7
  44.8 4.7 %far.1 = (f32[8,8192]{1,0:T(8,128)}, f32[8,2048]{1,0:T(8,128)}, bf16[240,8,128]{2,1,0:T(8,128)(2,1)}) custom-call(s32[8,128]{1,0:T(8,128)S(1)} %copy-done.7, bf16[240,24,128]{2,1,0:T(8,128)(2,1)S(1)} %all-to-all-done.1.got_ref, f32[80,24,128]{2,1,0:T(8,128)S(1)} %near_mix.1.near, f32[8,8192]{1,0:T(8,128)S(1)} %copy-done.1, f32[8,8192]{1,0:T(8,128)S(1)} %copy-done.2, ...), custom_call_target="tpu_custom_call" | custom-call | tf_op jit(solution)/shard_map/far/pallas_call | solution.py:284
  49.5 5.1 %all-to-all-start.2 = ((bf16[240,8,128]{2,1,0:T(8,128)(2,1)}), bf16[240,8,128]{2,1,0:T(8,128)(2,1)S(1)}, u32[]{:S(2)}, u32[]{:S(2)}) async-start(bf16[240,8,128]{2,1,0:T(8,128)(2,1)} %get-tuple-element.12), calls=%async_computation.2 | async-start | bytes 983040 | tf_op jit(solution)/shard_map/all_to_all | solution.py:443
  54.6 4.9 %near_back.1.refs_0_ = f32[8,4096]{1,0:T(8,128)} custom-call(s32[2,64]{1,0:T(2,128)} %bitcast.15, s32[2,16]{1,0:T(2,128)} %bitcast.17, f32[8,8192]{1,0:T(8,128)} %get-tuple-element.8.of_ref, f32[8,2048]{1,0:T(8,128)} %get-tuple-element.9.lf_ref, bf16[64,4,128,128]{3,2,1,0:T(8,128)(2,1)} %ot_ref.3, bf16[16,4,128,128]{3,2,1,0:T(8,128)(2,1)} %lt_ref.3), custom_call_target="tpu_custom_call" | custom-call | flops 671088640 | bytes 5242880 | tf_op jit(solution)/shard_map/near_back/pallas_call | solution.py:329
  59.4 4.1 %all-to-all-done.2.back_ref = bf16[240,8,128]{2,1,0:T(8,128)(2,1)S(1)} async-done(((bf16[240,8,128]{2,1,0:T(8,128)(2,1)}), bf16[240,8,128]{2,1,0:T(8,128)(2,1)S(1)}, u32[]{:S(2)}, u32[]{:S(2)}) %all-to-all-start.2) | async-done | bytes 491552 | tf_op jit(solution)/shard_map/all_to_all | solution.py:443
  63.6 1.1 %collect_far.1 = bf16[8,4096]{1,0:T(8,128)(2,1)S(1)} custom-call(s32[16,128]{1,0:T(8,128)S(1)} %bitcast.11, bf16[240,8,128]{2,1,0:T(8,128)(2,1)S(1)} %all-to-all-done.2.back_ref), custom_call_target="tpu_custom_call" | custom-call | flops 1048576 | bytes 4194304 | tf_op jit(solution)/shard_map/collect_far/pallas_call | solution.py:397
  64.6 5.5 %collective-permute-start.1 = (bf16[8,4096]{1,0:T(8,128)(2,1)S(1)}, bf16[8,4096]{1,0:T(8,128)(2,1)S(1)}, u32[]{:S(2)}, u32[]{:S(2)}) collective-permute-start(bf16[8,4096]{1,0:T(8,128)(2,1)S(1)} %collect_far.1), channel_id=1, source_target_pairs={{112,0},{113,1},{114,2},{115,3},{116,4},{117,5},{118,6},{119,7},{2... | collective-permute-start | bytes 196616 | tf_op jit(solution)/shard_map/ppermute | solution.py:446
  70.1 0.0 copy-start
  70.1 0.9 %copy-done = f32[8,4096]{1,0:T(8,128)S(1)} copy-done((f32[8,4096]{1,0:T(8,128)S(1)}, f32[8,4096]{1,0:T(8,128)}, u32[]{:S(2)}) %copy-start) | copy-done | bytes 131096
  71.0 1.2 %collect_own.1 = f32[8,4096]{1,0:T(8,128)S(1)} custom-call(s32[16,128]{1,0:T(8,128)S(1)} %bitcast.12, bf16[240,8,128]{2,1,0:T(8,128)(2,1)S(1)} %all-to-all-done.2.back_ref, f32[8,4096]{1,0:T(8,128)S(1)} %copy-done), custom_call_target="tpu_custom_call" | custom-call | flops 1048576 | bytes 4194304 | tf_op jit(solution)/shard_map/collect_own/pallas_call | solution.py:397
  72.2 0.0 collective-permute-done.1
  72.2 0.7 convert_add_fusion
Async XLA Ops:
  0.6 12.2 %collective-permute-start = (bf16[24,4096]{1,0:T(8,128)(2,1)}, bf16[24,4096]{1,0:T(8,128)(2,1)S(1)}, u32[]{:S(2)}, u32[]{:S(2)}) collective-permute-start(bf16[24,4096]{1,0:T(8,128)(2,1)} %own_ref.1), channel_id=1, source_target_pairs={{0,112},{1,113},{2,114},{3,115},{4,116},{5,117},{6,118},{7,119},{8... | collective-permute-start | bytes 589832 | tf_op jit(solution)/shard_map/ppermute | solution.py:432
  3.9 15.3 %all-to-all-start = ((s32[16,1,128]{2,1,0:T(1,128)}), s32[16,1,128]{2,1,0:T(1,128)S(1)}, u32[]{:S(2)}, u32[]{:S(2)}) async-start(s32[16,1,128]{2,1,0:T(1,128)} %bitcast.19), calls=%async_computation | async-start | bytes 16384 | tf_op jit(solution)/shard_map/all_to_all | solution.py:434
  12.9 0.9 %copy-start.3 = (bf16[24,4096]{1,0:T(8,128)(2,1)S(1)}, bf16[24,4096]{1,0:T(8,128)(2,1)}, u32[]{:S(2)}) copy-start(bf16[24,4096]{1,0:T(8,128)(2,1)} %own_ref.1) | copy-start | bytes 589828
  19.2 5.8 %copy-start.8 = (s32[64,2]{0,1:T(2,128)S(1)}, s32[64,2]{0,1:T(2,128)}, u32[]{:S(2)}) copy-start(s32[64,2]{0,1:T(2,128)} %param.19) | copy-start | bytes 1540
  19.2 5.8 %copy-start.9 = (s32[16,2]{0,1:T(2,128)S(1)}, s32[16,2]{0,1:T(2,128)}, u32[]{:S(2)}) copy-start(s32[16,2]{0,1:T(2,128)} %param.22) | copy-start | bytes 388
  21.3 23.5 %all-to-all-start.1 = ((bf16[240,24,128]{2,1,0:T(8,128)(2,1)}), bf16[240,24,128]{2,1,0:T(8,128)(2,1)S(1)}, u32[]{:S(2)}, u32[]{:S(2)}) async-start(bf16[240,24,128]{2,1,0:T(8,128)(2,1)} %serve.1), calls=%async_computation.1 | async-start | bytes 2949120 | tf_op jit(solution)/shard_map/all_to_all | solution.py:436
  25.0 19.7 %copy-start.1 = (f32[8,8192]{1,0:T(8,128)S(1)}, f32[8,8192]{1,0:T(8,128)}, u32[]{:S(2)}) copy-start(f32[8,8192]{1,0:T(8,128)} %osv.1) | copy-start | bytes 786436
  25.0 19.7 %copy-start.2 = (f32[8,8192]{1,0:T(8,128)S(1)}, f32[8,8192]{1,0:T(8,128)}, u32[]{:S(2)}) copy-start(f32[8,8192]{1,0:T(8,128)} %isv.1) | copy-start | bytes 786436
  25.0 19.7 %copy-start.4 = (f32[8,2048]{1,0:T(8,128)S(1)}, f32[8,2048]{1,0:T(8,128)}, u32[]{:S(2)}) copy-start(f32[8,2048]{1,0:T(8,128)} %ls.1) | copy-start | bytes 196612
  25.0 19.7 %copy-start.5 = (s32[8192]{0:T(1024)S(1)}, s32[8192]{0:T(1024)}, u32[]{:S(2)}) copy-start(s32[8192]{0:T(1024)} %param.15) | copy-start | bytes 98308
  25.1 19.7 %copy-start.6 = (s32[2048]{0:T(1024)S(1)}, s32[2048]{0:T(1024)}, u32[]{:S(2)}) copy-start(s32[2048]{0:T(1024)} %param.17) | copy-start | bytes 24580
  25.1 19.7 %copy-start.7 = (s32[8,128]{1,0:T(8,128)S(1)}, s32[8,128]{1,0:T(8,128)}, u32[]{:S(2)}) copy-start(s32[8,128]{1,0:T(8,128)} %get-tuple-element.11.slot_hbm) | copy-start | bytes 12292
  49.5 14.1 %all-to-all-start.2 = ((bf16[240,8,128]{2,1,0:T(8,128)(2,1)}), bf16[240,8,128]{2,1,0:T(8,128)(2,1)S(1)}, u32[]{:S(2)}, u32[]{:S(2)}) async-start(bf16[240,8,128]{2,1,0:T(8,128)(2,1)} %get-tuple-element.12), calls=%async_computation.2 | async-start | bytes 983040 | tf_op jit(solution)/shard_map/all_to_all | solution.py:443
  64.6 7.6 %collective-permute-start.1 = (bf16[8,4096]{1,0:T(8,128)(2,1)S(1)}, bf16[8,4096]{1,0:T(8,128)(2,1)S(1)}, u32[]{:S(2)}, u32[]{:S(2)}) collective-permute-start(bf16[8,4096]{1,0:T(8,128)(2,1)S(1)} %collect_far.1), channel_id=1, source_target_pairs={{112,0},{113,1},{114,2},{115,3},{116,4},{117,5},{118,6},{119,7},{2... | collective-permute-start | bytes 196616 | tf_op jit(solution)/shard_map/ppermute | solution.py:446
  70.1 0.9 %copy-start = (f32[8,4096]{1,0:T(8,128)S(1)}, f32[8,4096]{1,0:T(8,128)}, u32[]{:S(2)}) copy-start(f32[8,4096]{1,0:T(8,128)} %near_back.1.refs_0_) | copy-start | bytes 393220
